TPU v7x, 32 devices: a whole 2x2x4 slice. The times are simulated.
32 devices in a mesh: groups: 2 (over x), ctx: 16 (over z, y, core).
Axes of the slice: x: 2, y: 2, z: 4, core: 2. Of those that a mesh axis runs over, the one named last changes fastest.
Arguments:
- hidden_in: bfloat16 [4096, 2048], P(('groups', 'ctx')), parts along dimension 0, may hold values from -6 to 6
- queries: bfloat16 [4096, 1024], P(('groups', 'ctx')), parts along dimension 0, as said below
- keys: bfloat16 [4096, 128], P(('groups', 'ctx')), parts along dimension 0, as said below
- values: bfloat16 [4096, 128], P(('groups', 'ctx')), parts along dimension 0, may hold values from -6 to 6
- out_weight: bfloat16 [1024, 2048], replicated, may hold values from -0.5 to 0.5
- norm_gain: float32 [2048], replicated, may hold values from 0.1 to 1.9
- gate_weight: bfloat16 [2048, 11008], P(None, 'ctx'), may hold values from -0.125 to 0.125
- up_weight: bfloat16 [2048, 11008], P(None, 'ctx'), may hold values from -0.125 to 0.125
- down_weight: bfloat16 [11008, 2048], P('ctx'), may hold values from -0.0546875 to 0.0546875
- pair_ids: int32 [4096], P('groups'), parts along dimension 0, may hold values from 0 to 3, as said below
- roles: int32 [4096], P('groups'), parts along dimension 0, may hold values from 0 to 2, as said below
- send_rows: int32 [32, 128], P(('groups', 'ctx')), parts along dimension 0, may hold values from 0 to 127, as said below
- send_counts: int32 [32, 16], P('groups'), parts along dimension 0, may hold values from 0 to 8, as said below
Outputs:
- layer_out: bfloat16 [4096, 2048], P(('groups', 'ctx')), parts along dimension 0
There are 2 independent parts, one for each index of `groups`. A program takes and returns all parts, laid end to end along the dimension named above; an argument that names none is the same for every part. Nothing has to cross between parts.
Inputs may be any that keep to these rules, and one draw needn't show every extreme that they name: `pair_ids`: never falls along the sequence; every pair is present, and one pair's chosen response spans 256 positions or more. `roles`: each pair is a prompt, then its chosen response, then its rejected response, each of one position or more; responses fill exactly 1536 positions. `send_rows`: slots j * 8 + k with k < send_counts[i, j] list distinct local rows of device i, together exactly its positions whose role is not 0; other slots hold 0. `send_counts`: replicated on every device; every column sums to 96; some entry equals 8. `queries`: values within -8 to 8. `keys`: values within -8 to 8.
All inputs are finite; a program needn't handle non-finite values.
Results may differ from a plain program's by a relative error of at most 0.015.
Values may be sent and summed in bfloat16 or wider, within the bound.
No kernel may reach another device: no remote copies, remote signals or barrier semaphores. Data moves between devices by JAX's collectives and lax.ppermute only.
A program may use at most 128 MiB of HBM per device.

v0:
```python
import functools
import math

import jax
import jax.numpy as jnp
import numpy as np
from jax import lax
from jax.experimental import pallas as pl
from jax.experimental.pallas import tpu as pltpu
from jax.sharding import PartitionSpec as P

NEG_FILL = -1e30
CORES = 2
PLANE = 4
MIB = 1 << 20
CHUNKS = 2


def in_hbm(x):
    return pltpu.with_memory_space_constraint(x, pltpu.HBM)


def in_vmem(x):
    return pltpu.with_memory_space_constraint(x, pltpu.VMEM)


def hold(first, then):
    return lax.optimization_barrier((first, then))


class Ring:
    def __init__(self, groups, devices):
        chips = devices // CORES
        columns = max(1, PLANE // groups)
        if chips % columns:
            columns = 1
        depth = chips // columns
        order = []
        for column in range(columns):
            line = [level * columns + column for level in range(depth)]
            order += line if column % 2 == 0 else line[::-1]
        self.chips = chips
        self.half = chips // 2
        self.order = order
        self.swap = [(i, i ^ 1) for i in range(devices)]

    def go(self, block, hops):
        pairs = []
        for place in range(self.chips):
            here, there = self.order[place], self.order[(place + hops) % self.chips]
            pairs += [(here * CORES + core, there * CORES + core) for core in range(CORES)]
        return lax.ppermute(block, "ctx", pairs)

    def go_mate(self, block):
        return lax.ppermute(block, "ctx", self.swap)

    def go_split(self, block, hops):
        pairs = []
        for place in range(self.chips):
            for core, way in ((0, hops), (1, -hops)):
                here, there = self.order[place], self.order[(place + way) % self.chips]
                pairs.append((here * CORES + core, there * CORES + core))
        return lax.ppermute(block, "ctx", pairs)

    def owners(self, spots, swapped=False):
        place_of = {chip: place for place, chip in enumerate(self.order)}
        table = []
        for device in range(self.chips * CORES):
            chip, core = divmod(device, CORES)
            row = []
            for spot in spots:
                first = self.order[(place_of[chip] + spot[core]) % self.chips] * CORES + core
                row += [first ^ 1, first] if swapped else [first, first ^ 1]
            table.append(row)
        return np.asarray(table, np.int32)


def attention_kernel(
    count,
    pieces,
    heads,
    head_dim,
    owner_ref,
    pair_smem,
    role_smem,
    query_ref,
    pair_ref,
    role_ref,
    hidden_ref,
    gain_ref,
    weight_ref,
    *refs,
):
    blocks, refs = refs[:pieces], refs[pieces:]
    chunk_refs, refs = refs[:CHUNKS], refs[CHUNKS:]
    (residual_ref, stacked, scores, top, total, summed) = refs
    rows = query_ref.shape[0]
    places = [(block, 2 * k) for block in blocks for k in range(block.shape[0] // (2 * rows))]
    me = owner_ref[0]
    for head in range(heads):
        stacked[pl.ds(head * rows, rows), :] = query_ref[:, head * head_dim : (head + 1) * head_dim]

    def column(ref):
        return jnp.broadcast_to(ref[pl.ds(me, 1), :], (rows, rows)).T

    query_pair, query_role = column(pair_ref), column(role_ref)
    query_pos = me * rows + lax.broadcasted_iota(jnp.int32, (rows, rows), 0)
    key_off = lax.broadcasted_iota(jnp.int32, (rows, rows), 1)

    def needed(owner):
        first_pair, last_pair = pair_smem[owner, 0], pair_smem[owner, rows - 1]
        first_role, last_role = role_smem[owner, 0], role_smem[owner, rows - 1]
        my_first, my_last = pair_smem[me, 0], pair_smem[me, rows - 1]
        my_role = role_smem[me, 0]
        apart = (
            (first_pair == last_pair)
            & (my_first == my_last)
            & (first_role == last_role)
            & (my_role == role_smem[me, rows - 1])
            & (first_role != 0)
            & (first_role != my_role)
        )
        return (owner <= me) & (last_pair >= my_first) & jnp.logical_not(apart)

    top[...] = jnp.full_like(top, NEG_FILL)
    total[...] = jnp.zeros_like(total)
    summed[...] = jnp.zeros_like(summed)
    for j in range(count):
        owner = owner_ref[j]

        @pl.when(needed(owner))
        def _():
            seen = (
                (query_pair == pair_ref[pl.ds(owner, 1), :])
                & (owner * rows + key_off <= query_pos)
                & (
                    (role_ref[pl.ds(owner, 1), :] == 0)
                    | (role_ref[pl.ds(owner, 1), :] == query_role)
                )
            )
            bias = jnp.where(seen, 0.0, NEG_FILL)
            raw = lax.dot_general(
                stacked[...],
                places[j][0][pl.ds(places[j][1] * rows, rows), :],
                (((1,), (1,)), ((), ())),
                preferred_element_type=jnp.float32,
            )
            masked = raw.reshape(heads, rows, rows) + bias[None]
            scores[j] = masked
            top[...] = jnp.maximum(top[...], masked)

    top[...] = jnp.broadcast_to(jnp.max(top[...], axis=-1, keepdims=True), top.shape)
    factor = math.log2(math.e) / math.sqrt(head_dim)
    for j in range(count):
        owner = owner_ref[j]

        @pl.when(needed(owner))
        def _():
            weights = jnp.exp2((scores[j] - top[...]) * factor)
            total[...] += weights
            summed[...] += jnp.dot(
                weights.astype(jnp.bfloat16).reshape(heads * rows, rows),
                places[j][0][pl.ds((places[j][1] + 1) * rows, rows), :],
                preferred_element_type=jnp.float32,
            ).reshape(heads, rows, head_dim)

    mixed = (summed[...] / jnp.sum(total[...], axis=-1, keepdims=True)).astype(jnp.bfloat16)
    mixed = jnp.concatenate([mixed[head] for head in range(heads)], axis=1)
    projected = jnp.dot(mixed, weight_ref[...], preferred_element_type=jnp.float32)
    residual = (hidden_ref[...].astype(jnp.float32) + projected).astype(jnp.bfloat16)
    residual_ref[...] = residual
    wide = residual.astype(jnp.float32)
    mean_sq = jnp.mean(wide * wide, axis=-1, keepdims=True)
    normed = (wide * lax.rsqrt(mean_sq + 1e-06) * gain_ref[...]).astype(jnp.bfloat16)
    part = rows // CHUNKS
    for chunk in range(CHUNKS):
        chunk_refs[chunk][...] = normed[chunk * part : (chunk + 1) * part]


def attend(owners, pairs, parts, inputs, blocks):
    queries, _, _, hidden, _, _ = inputs
    rows, width = queries.shape
    head_dim = blocks[0].shape[1]
    heads = width // head_dim
    count = owners.shape[0]
    tall = heads * rows * rows * jnp.dtype(jnp.float32).itemsize
    smem = pl.BlockSpec(memory_space=pltpu.SMEM)
    vmem = pl.BlockSpec(memory_space=pltpu.VMEM)
    square = pltpu.VMEM((heads, rows, rows), jnp.float32)
    chunk = jax.ShapeDtypeStruct((rows // CHUNKS, hidden.shape[1]), jnp.bfloat16)
    *chunks, residual = pl.pallas_call(
        functools.partial(attention_kernel, count, len(blocks), heads, head_dim),
        out_shape=(chunk,) * CHUNKS + (jax.ShapeDtypeStruct(hidden.shape, jnp.bfloat16),),
        in_specs=[smem] * 3 + [vmem] * (len(inputs) + len(blocks)),
        out_specs=(vmem,) * (CHUNKS + 1),
        scratch_shapes=[
            pltpu.VMEM((heads * rows, head_dim), jnp.bfloat16),
            pltpu.VMEM((count, heads, rows, rows), jnp.float32),
            square,
            square,
            pltpu.VMEM((heads, rows, head_dim), jnp.float32),
        ],
        compiler_params=pltpu.CompilerParams(vmem_limit_bytes=(count + 3) * tall + 10 * MIB),
        name="attention",
    )(owners, pairs, parts, *(in_vmem(x) for x in inputs), in_vmem(blocks[0]), *blocks[1:])
    return residual, chunks


def load_kernel(count, *refs):
    inputs, outputs, sems = refs[:count], refs[count : 2 * count], refs[2 * count]
    moves = [pltpu.make_async_copy(inputs[k], outputs[k], sems.at[k]) for k in range(count)]
    for move in moves:
        move.start()
    for move in moves:
        move.wait()


def load(*arrays):
    count = len(arrays)
    return pl.pallas_call(
        functools.partial(load_kernel, count),
        out_shape=tuple(pltpu.VMEM(x.shape, x.dtype) for x in arrays),
        in_specs=[pl.BlockSpec(memory_space=pl.ANY)] * count,
        out_specs=(pl.BlockSpec(memory_space=pltpu.VMEM),) * count,
        scratch_shapes=[pltpu.SemaphoreType.DMA((count,))],
        compiler_params=pltpu.CompilerParams(vmem_limit_bytes=2 * MIB),
        name="load",
    )(*arrays)


def join_kernel(count, *refs):
    inputs, both_ref, sems = refs[:count], refs[count], refs[count + 1]
    rows = inputs[0].shape[0]
    moves = [
        pltpu.make_async_copy(inputs[k], both_ref.at[pl.ds(k * rows, rows), :], sems.at[k])
        for k in range(count)
    ]
    for move in moves:
        move.start()
    for move in moves:
        move.wait()


def join(*parts):
    count = len(parts)
    rows, width = parts[0].shape
    return pl.pallas_call(
        functools.partial(join_kernel, count),
        out_shape=pltpu.VMEM((count * rows, width), parts[0].dtype),
        in_specs=[pl.BlockSpec(memory_space=pl.ANY)] * (count // CORES)
        + [pl.BlockSpec(memory_space=pltpu.VMEM)] * (count - count // CORES),
        out_specs=pl.BlockSpec(memory_space=pltpu.VMEM),
        scratch_shapes=[pltpu.SemaphoreType.DMA((count,))],
        name="join",
    )(*parts)


def ffn_kernel(blocks, *refs):
    inputs, refs = refs[:blocks], refs[blocks:]
    weights, refs = refs[:6], refs[6:]
    outputs, refs = refs[:blocks], refs[blocks:]
    turned, inner, total = refs
    part = inputs[0].shape[0]
    turned[...] = jnp.concatenate([ref[...] for ref in inputs], axis=0).T
    for side in range(2):
        gate, up, down = weights[3 * side : 3 * side + 3]
        gate_out = jnp.dot(gate[...], turned[...], preferred_element_type=jnp.float32)
        up_out = jnp.dot(up[...], turned[...], preferred_element_type=jnp.float32)
        inner[...] = (gate_out / (1.0 + jnp.exp(-gate_out)) * up_out).astype(jnp.bfloat16)
        term = jnp.dot(inner[...].T, down[...], preferred_element_type=jnp.float32)
        if side == 0:
            total[...] = term
        else:
            term = (term + total[...]).astype(jnp.bfloat16)
            for k in range(blocks):
                outputs[k][...] = term[k * part : (k + 1) * part]


def ffn(blocks, weights):
    count = len(blocks)
    rows, width = blocks[0].shape
    hidden = weights[0].shape[0]
    vmem = pl.BlockSpec(memory_space=pltpu.VMEM)
    return pl.pallas_call(
        functools.partial(ffn_kernel, count),
        out_shape=tuple(jax.ShapeDtypeStruct(b.shape, jnp.bfloat16) for b in blocks),
        in_specs=[vmem] * (count + 6),
        out_specs=(vmem,) * count,
        scratch_shapes=[
            pltpu.VMEM((width, count * rows), jnp.bfloat16),
            pltpu.VMEM((hidden, count * rows), jnp.bfloat16),
            pltpu.VMEM((count * rows, width), jnp.float32),
        ],
        compiler_params=pltpu.CompilerParams(vmem_limit_bytes=16 * MIB),
        cost_estimate=pl.CostEstimate(flops=1000, transcendentals=0, bytes_accessed=1000),
        name="feed_forward",
    )(*blocks, *(in_vmem(w) for w in weights))


def feed_forward(ring, chunks, own, mates):
    half = ring.half

    def send(pair, way):
        return ring.go(pair[0], way), ring.go(pair[1], -way)

    chunks, own, mates = lax.optimization_barrier((chunks, own, mates))
    held = [[(chunks[0], chunks[1])], [(chunks[1], chunks[0])]]
    terms = [{}, {}]
    for group in range(2):
        held[group].append(send(held[group][0], 1))
    weights = load(*(in_hbm(w) for w in own)) + load(*mates)
    weights, held[0][1] = hold(weights, held[0][1])
    for step in range(1, half):
        held[0].append(send(held[0][step], 1))
        older = held[1][step - 1] if step > 1 else held[0][0]
        done = ffn(held[0][step] + older, weights)
        if step + 1 < half:
            done, pair = hold(done, held[1][step])
            held[1].append(send(pair, 1))
        terms[0][step], terms[1][step - 1] = done[:2], done[2:]
    older = held[1][half - 1] if half > 1 else held[0][0]
    if half > 1:
        done, older = hold(done, older)
        terms[0][half - 1], terms[1][half - 2] = done[:2], done[2:]
    done = ffn(held[0][half] + older, weights)
    terms[0][half], terms[1][half - 1] = done[:2], done[2:]

    def add(a, b):
        return (a.astype(jnp.float32) + b.astype(jnp.float32)).astype(jnp.bfloat16)

    home = [None, None]
    for step in range(half, 0, -1):
        for group in range(2):
            place = step - group
            if place == 0:
                continue
            pair = terms[group][place]
            if home[group] is not None:
                pair = (add(home[group][0], pair[0]), add(home[group][1], pair[1]))
            home[group] = send(pair, -1)
    sums = [[x.astype(jnp.float32) for x in terms[1][0]]]
    if home[1] is not None:
        sums.append([x.astype(jnp.float32) for x in home[1][::-1]])
    sums.append([x.astype(jnp.float32) for x in home[0]])
    return [sum(x[k] for x in sums) for k in range(2)]


def gather_kv(ring, keys, values, weights, extras):
    half = ring.half
    gate, up, down = weights
    both = join(in_hbm(keys), in_hbm(values), *(in_vmem(ring.go_mate(x)) for x in (keys, values)))
    gate, up, both = lax.optimization_barrier((gate, up, both))
    gate_mate, up_mate = ring.go_mate(gate), ring.go_mate(up)
    held, mates = {0: both}, {}
    reach = 0
    while reach < half:
        fresh = range(reach + 1, min(reach + 2, half) + 1)
        for hops in fresh:
            jump = min(2, hops)
            held[hops] = ring.go_split(held[hops - jump], jump)
        for hops in range(max(1, reach - 1), reach + 1):
            mates[hops] = ring.go_mate(held[hops])
        held, mates, extras = lax.optimization_barrier((held, mates, extras))
        reach = fresh[-1]
    for hops in range(1, half):
        if hops not in mates:
            mates[hops] = ring.go_mate(held[hops])
    gate_mate, up_mate, down, held, mates = lax.optimization_barrier(
        (gate_mate, up_mate, down, held, mates)
    )
    down_mate = ring.go_mate(down)
    blocks = tuple(held[hops] for hops in range(half + 1))
    blocks += tuple(mates[hops] for hops in range(1, half))
    return blocks, (gate_mate, up_mate, down_mate), extras


def block_owners(ring):
    half = ring.half
    owners = [ring.owners([(-hops, hops)]) for hops in range(half + 1)]
    owners += [ring.owners([(hops, -hops)], True) for hops in range(1, half)]
    return np.concatenate(owners, axis=1)


def on_device(
    ring,
    hidden_in,
    queries,
    keys,
    values,
    out_weight,
    norm_gain,
    gate_weight,
    up_weight,
    down_weight,
    pair_ids,
    roles,
    send_rows,
    send_counts,
):
    my_index = lax.axis_index("ctx")
    tok_rows = hidden_in.shape[0]
    own = (gate_weight.T, up_weight.T, down_weight)
    owners = jnp.asarray(block_owners(ring))[my_index]
    pairs = pair_ids.reshape(-1, tok_rows)
    parts = roles.reshape(-1, tok_rows)
    my_roles = lax.dynamic_slice_in_dim(roles, my_index * tok_rows, tok_rows)
    live = (my_roles != 0).astype(jnp.float32)
    inputs = load(
        *(in_hbm(x) for x in (queries, pairs, parts, hidden_in, norm_gain.reshape(1, -1), out_weight))
    )
    blocks, mates, extras = gather_kv(ring, keys, values, own, (owners, live, inputs))
    owners, live, inputs = extras
    residual, chunks = attend(owners, pairs, parts, inputs, blocks)
    summed = feed_forward(ring, chunks, own, mates)
    ffn_back = jnp.concatenate(summed, axis=0).astype(jnp.bfloat16).astype(jnp.float32)
    return (residual.astype(jnp.float32) + ffn_back * live[:, None]).astype(jnp.bfloat16)


def solution(mesh):
    ring = Ring(mesh.shape["groups"], mesh.shape["ctx"])

    def run(*arrays):
        return on_device(ring, *arrays)

    return jax.shard_map(
        run,
        mesh=mesh,
        in_specs=(
            P(("groups", "ctx"), None),
            P(("groups", "ctx"), None),
            P(("groups", "ctx"), None),
            P(("groups", "ctx"), None),
            P(),
            P(),
            P(None, "ctx"),
            P(None, "ctx"),
            P("ctx", None),
            P("groups"),
            P("groups"),
            P(("groups", "ctx"), None),
            P("groups", None),
        ),
        out_specs=P(("groups", "ctx"), None),
        check_vma=False,
    )
```

profile of v0, /device:TPU:0, one launch (start us, length us, event | category | flops | bytes accessed | tf_op | source)
XLA Modules:
  0.0 122.0 jit_solution(9037258710337681049)
XLA Ops:
  3.3 2.7 %collective-permute-start.2 = (bf16[512,128]{1,0:T(8,128)(2,1)S(1)}, bf16[512,128]{1,0:T(8,128)(2,1)S(1)}, u32[]{:S(2)}, u32[]{:S(2)}) collective-permute-start(bf16[512,128]{1,0:T(8,128)(2,1)S(1)} %join.1.refs_0_), channel_id=1, source_target_pairs={{0,4},{1,3},{4,8},{5,1},{8,12},{9,5},{12,14},{13,9},{14,10},{15,13... | collective-permute-start | bytes 393224 | tf_op jit(solution)/shard_map/ppermute | solution.py:63
  6.0 2.6 %collective-permute-start.3 = (bf16[512,128]{1,0:T(8,128)(2,1)S(1)}, bf16[512,128]{1,0:T(8,128)(2,1)S(1)}, u32[]{:S(2)}, u32[]{:S(2)}) collective-permute-start(bf16[512,128]{1,0:T(8,128)(2,1)S(1)} %join.1.refs_0_), channel_id=1, source_target_pairs={{0,8},{1,7},{4,12},{5,3},{8,14},{9,1},{12,10},{13,5},{14,6},{15,9}... | collective-permute-start | bytes 393224 | tf_op jit(solution)/shard_map/ppermute | solution.py:63
  9.4 2.7 %load.3 = (bf16[128,1024]{1,0:T(8,128)(2,1)S(1)}, s32[16,128]{1,0:T(8,128)S(1)}, s32[16,128]{1,0:T(8,128)S(1)}, bf16[128,2048]{1,0:T(8,128)(2,1)S(1)}, f32[1,204...) custom-call(bf16[128,1024]{1,0:T(8,128)(2,1)} %refs_0_.3, s32[16,128]{1,0:T(8,128)} %bitcast.7, s32[16,128]{1,0:T(8,128)} %bitcast.9, ...), custom_call_target="tpu_custom_call" | custom-call | tf_op jit(solution)/shard_map/load/pallas_call | solution.py:220
  13.3 1.7 %collective-permute-start.4 = (bf16[512,128]{1,0:T(8,128)(2,1)S(1)}, bf16[512,128]{1,0:T(8,128)(2,1)S(1)}, u32[]{:S(2)}, u32[]{:S(2)}) collective-permute-start(bf16[512,128]{1,0:T(8,128)(2,1)S(1)} %collective-permute-done.2.refs_1_), channel_id=1, source_target_pairs={{0,8},{1,7},{4,12},{5,3},{8,14},{9,1},{12,10},{13,5},{14,6},{15,9}... | collective-permute-start | bytes 393224 | tf_op jit(solution)/shard_map/ppermute | solution.py:63
  16.3 4.0 %collective-permute-done.4.refs_3_ = bf16[512,128]{1,0:T(8,128)(2,1)S(1)} collective-permute-done((bf16[512,128]{1,0:T(8,128)(2,1)S(1)}, bf16[512,128]{1,0:T(8,128)(2,1)S(1)}, u32[]{:S(2)}, u32[]{:S(2)}) %collective-permute-start.4) | collective-permute-done | bytes 131104 | tf_op jit(solution)/shard_map/ppermute | solution.py:63
  20.2 2.6 %collective-permute-done.5.refs_4_ = bf16[512,128]{1,0:T(8,128)(2,1)S(1)} collective-permute-done((bf16[512,128]{1,0:T(8,128)(2,1)S(1)}, bf16[512,128]{1,0:T(8,128)(2,1)S(1)}, u32[]{:S(2)}, u32[]{:S(2)}) %collective-permute-start.5) | collective-permute-done | bytes 131104 | tf_op jit(solution)/shard_map/ppermute | solution.py:63
  24.4 3.1 %attention.1 = (bf16[64,2048]{1,0:T(8,128)(2,1)S(1)}, bf16[64,2048]{1,0:T(8,128)(2,1)S(1)}, bf16[128,2048]{1,0:T(8,128)(2,1)S(1)}) custom-call(s32[16]{0:T(128)S(1)} %dynamic-slice_bitcast_fusion.owner_ref, s32[16,128]{1,0:T(8,128)S(1)} %bitcast.8, s32[16,128]{1,0:T(8,128)S(1)} %bitcast.10, bf16[128,1024]{1,0:T(8,128)(2,1)S(1)} %get-tuple-element.129.query_ref, ...), custom_call_target="tpu_custom_call" | custom-call | tf_op jit(solution)/shard_map/attention/pallas_call | solution.py:191
  27.6 1.9 %collective-permute-done.11.refs_2_ = bf16[688,2048]{1,0:T(8,128)(2,1)S(1)} collective-permute-done((bf16[688,2048]{1,0:T(8,128)(2,1)S(1)}, bf16[688,2048]{1,0:T(8,128)(2,1)S(1)}, u32[]{:S(2)}, u32[]{:S(2)}) %collective-permute-start.11) | collective-permute-done | bytes 2818080 | tf_op jit(solution)/shard_map/ppermute | solution.py:55
  33.5 2.2 %load.5 = (bf16[688,2048]{1,0:T(8,128)(2,1)S(1)}, bf16[688,2048]{1,0:T(8,128)(2,1)S(1)}, bf16[688,2048]{1,0:T(8,128)(2,1)S(1)}) custom-call(bf16[688,2048]{1,0:T(8,128)(2,1)S(1)} %collective-permute-done.8.refs_0_, bf16[688,2048]{1,0:T(8,128)(2,1)} %collective-permute-done.9.refs_1_, bf16[688,2048]{1,0:T(8,128)(2,1)S(1)} %collective-permute-done.11.refs_2_), custom_call_target="tpu_custom_call" | custom-call | tf_op jit(solution)/shard_map/load/pallas_call | solution.py:220
  35.8 3.5 %load.4 = (bf16[688,2048]{1,0:T(8,128)(2,1)S(1)}, bf16[688,2048]{1,0:T(8,128)(2,1)S(1)}, bf16[688,2048]{1,0:T(8,128)(2,1)S(1)}) custom-call(bf16[688,2048]{1,0:T(8,128)(2,1)} %bitcast.12, bf16[688,2048]{1,0:T(8,128)(2,1)} %bitcast.14, bf16[688,2048]{1,0:T(8,128)(2,1)} %refs_2_), custom_call_target="tpu_custom_call" | custom-call | tf_op jit(solution)/shard_map/load/pallas_call | solution.py:220
  39.8 1.9 %collective-permute-start.16 = (bf16[64,2048]{1,0:T(8,128)(2,1)S(1)}, bf16[64,2048]{1,0:T(8,128)(2,1)S(1)}, u32[]{:S(2)}, u32[]{:S(2)}) collective-permute-start(bf16[64,2048]{1,0:T(8,128)(2,1)S(1)} %collective-permute-done.12.refs_0_), channel_id=1, source_target_pairs={{0,4},{1,5},{4,8},{5,9},{8,12},{9,13},{12,14},{13,15},{14,10},{15,... | collective-permute-start | bytes 786440 | tf_op jit(solution)/shard_map/ppermute | solution.py:52
  41.8 4.9 %feed_forward.4 = (bf16[64,2048]{1,0:T(8,128)(2,1)S(1)}, bf16[64,2048]{1,0:T(8,128)(2,1)S(1)}, bf16[64,2048]{1,0:T(8,128)(2,1)S(1)}, bf16[64,2048]{1,0:T(8,128)(2,1)S(1)}) custom-call(bf16[64,2048]{1,0:T(8,128)(2,1)S(1)} %collective-permute-done.12.refs_0_, bf16[64,2048]{1,0:T(8,128)(2,1)S(1)} %collective-permute-done.13.refs_1_, ...), custom_call_target="tpu_custom_call" | custom-call | flops 1000 | bytes 1000 | tf_op jit(solution)/shard_map/feed_forward/pallas_call | solution.py:284
  46.8 2.0 %collective-permute-start.22 = (bf16[64,2048]{1,0:T(8,128)(2,1)S(1)}, bf16[64,2048]{1,0:T(8,128)(2,1)S(1)}, u32[]{:S(2)}, u32[]{:S(2)}) collective-permute-start(bf16[64,2048]{1,0:T(8,128)(2,1)S(1)} %collective-permute-done.14.refs_2_), channel_id=1, source_target_pairs={{0,4},{1,5},{4,8},{5,9},{8,12},{9,13},{12,14},{13,15},{14,10},{15,... | collective-permute-start | bytes 786440 | tf_op jit(solution)/shard_map/ppermute | solution.py:52
  51.4 4.9 %feed_forward.6 = (bf16[64,2048]{1,0:T(8,128)(2,1)S(1)}, bf16[64,2048]{1,0:T(8,128)(2,1)S(1)}, bf16[64,2048]{1,0:T(8,128)(2,1)S(1)}, bf16[64,2048]{1,0:T(8,128)(2,1)S(1)}) custom-call(bf16[64,2048]{1,0:T(8,128)(2,1)S(1)} %collective-permute-done.16.refs_0_, bf16[64,2048]{1,0:T(8,128)(2,1)S(1)} %collective-permute-done.19.refs_1_, ...), custom_call_target="tpu_custom_call" | custom-call | flops 1000 | bytes 1000 | tf_op jit(solution)/shard_map/feed_forward/pallas_call | solution.py:284
  60.1 1.7 %collective-permute-done.17.refs_0_ = bf16[64,2048]{1,0:T(8,128)(2,1)S(1)} collective-permute-done((bf16[64,2048]{1,0:T(8,128)(2,1)S(1)}, bf16[64,2048]{1,0:T(8,128)(2,1)S(1)}, u32[]{:S(2)}, u32[]{:S(2)}) %collective-permute-start.17) | collective-permute-done | bytes 262176 | tf_op jit(solution)/shard_map/ppermute | solution.py:52
  61.7 1.7 %collective-permute-start.18 = (bf16[64,2048]{1,0:T(8,128)(2,1)S(1)}, bf16[64,2048]{1,0:T(8,128)(2,1)S(1)}, u32[]{:S(2)}, u32[]{:S(2)}) collective-permute-start(bf16[64,2048]{1,0:T(8,128)(2,1)S(1)} %collective-permute-done.17.refs_0_), channel_id=1, source_target_pairs={{0,4},{1,5},{4,8},{5,9},{8,12},{9,13},{12,14},{13,15},{14,10},{15,... | collective-permute-start | bytes 786440 | tf_op jit(solution)/shard_map/ppermute | solution.py:52
  63.7 4.9 %feed_forward.5 = (bf16[64,2048]{1,0:T(8,128)(2,1)S(1)}, bf16[64,2048]{1,0:T(8,128)(2,1)S(1)}, bf16[64,2048]{1,0:T(8,128)(2,1)S(1)}, bf16[64,2048]{1,0:T(8,128)(2,1)S(1)}) custom-call(bf16[64,2048]{1,0:T(8,128)(2,1)S(1)} %collective-permute-done.17.refs_0_, bf16[64,2048]{1,0:T(8,128)(2,1)S(1)} %collective-permute-done.20.refs_1_, ...), custom_call_target="tpu_custom_call" | custom-call | flops 1000 | bytes 1000 | tf_op jit(solution)/shard_map/feed_forward/pallas_call | solution.py:284
  69.3 2.3 %collective-permute-done.18.refs_0_ = bf16[64,2048]{1,0:T(8,128)(2,1)S(1)} collective-permute-done((bf16[64,2048]{1,0:T(8,128)(2,1)S(1)}, bf16[64,2048]{1,0:T(8,128)(2,1)S(1)}, u32[]{:S(2)}, u32[]{:S(2)}) %collective-permute-start.18) | collective-permute-done | bytes 262176 | tf_op jit(solution)/shard_map/ppermute | solution.py:52
  71.5 1.8 %collective-permute-done.21.refs_1_ = bf16[64,2048]{1,0:T(8,128)(2,1)S(1)} collective-permute-done((bf16[64,2048]{1,0:T(8,128)(2,1)S(1)}, bf16[64,2048]{1,0:T(8,128)(2,1)S(1)}, u32[]{:S(2)}, u32[]{:S(2)}) %collective-permute-start.21) | collective-permute-done | bytes 262176 | tf_op jit(solution)/shard_map/ppermute | solution.py:52
  73.3 4.9 %feed_forward.7 = (bf16[64,2048]{1,0:T(8,128)(2,1)S(1)}, bf16[64,2048]{1,0:T(8,128)(2,1)S(1)}, bf16[64,2048]{1,0:T(8,128)(2,1)S(1)}, bf16[64,2048]{1,0:T(8,128)(2,1)S(1)}) custom-call(bf16[64,2048]{1,0:T(8,128)(2,1)S(1)} %collective-permute-done.18.refs_0_, bf16[64,2048]{1,0:T(8,128)(2,1)S(1)} %collective-permute-done.21.refs_1_, ...), custom_call_target="tpu_custom_call" | custom-call | flops 1000 | bytes 1000 | tf_op jit(solution)/shard_map/feed_forward/pallas_call | solution.py:284
  78.3 1.8 %collective-permute-start.26 = (bf16[64,2048]{1,0:T(8,128)(2,1)S(1)}, bf16[64,2048]{1,0:T(8,128)(2,1)S(1)}, u32[]{:S(2)}, u32[]{:S(2)}) collective-permute-start(bf16[64,2048]{1,0:T(8,128)(2,1)S(1)} %get-tuple-element.199), channel_id=1, source_target_pairs={{0,4},{1,5},{4,8},{5,9},{8,12},{9,13},{12,14},{13,15},{14,10},{15,... | collective-permute-start | bytes 786440 | tf_op jit(solution)/shard_map/ppermute | solution.py:52
  80.4 2.0 %collective-permute-start.36 = (bf16[64,2048]{1,0:T(8,128)(2,1)S(1)}, bf16[64,2048]{1,0:T(8,128)(2,1)S(1)}, u32[]{:S(2)}, u32[]{:S(2)}) collective-permute-start(bf16[64,2048]{1,0:T(8,128)(2,1)S(1)} %get-tuple-element.210), channel_id=1, source_target_pairs={{0,4},{1,5},{4,8},{5,9},{8,12},{9,13},{12,14},{13,15},{14,10},{15,... | collective-permute-start | bytes 786440 | tf_op jit(solution)/shard_map/ppermute | solution.py:52
  82.4 5.2 %collective-permute-done.26 = bf16[64,2048]{1,0:T(8,128)(2,1)S(1)} collective-permute-done((bf16[64,2048]{1,0:T(8,128)(2,1)S(1)}, bf16[64,2048]{1,0:T(8,128)(2,1)S(1)}, u32[]{:S(2)}, u32[]{:S(2)}) %collective-permute-start.26) | collective-permute-done | bytes 262176 | tf_op jit(solution)/shard_map/ppermute | solution.py:52
  87.7 1.8 %collective-permute-start.27 = (bf16[64,2048]{1,0:T(8,128)(2,1)S(1)}, bf16[64,2048]{1,0:T(8,128)(2,1)S(1)}, u32[]{:S(2)}, u32[]{:S(2)}) collective-permute-start(bf16[64,2048]{1,0:T(8,128)(2,1)S(1)} %add_convert_fusion.12), channel_id=1, source_target_pairs={{0,4},{1,5},{4,8},{5,9},{8,12},{9,13},{12,14},{13,15},{14,10},{15,... | collective-permute-start | bytes 786440 | tf_op jit(solution)/shard_map/ppermute | solution.py:52
  89.9 5.1 %collective-permute-done.33 = bf16[64,2048]{1,0:T(8,128)(2,1)S(1)} collective-permute-done((bf16[64,2048]{1,0:T(8,128)(2,1)S(1)}, bf16[64,2048]{1,0:T(8,128)(2,1)S(1)}, u32[]{:S(2)}, u32[]{:S(2)}) %collective-permute-start.33) | collective-permute-done | bytes 262176 | tf_op jit(solution)/shard_map/ppermute | solution.py:52
  95.4 1.8 %collective-permute-start.37 = (bf16[64,2048]{1,0:T(8,128)(2,1)S(1)}, bf16[64,2048]{1,0:T(8,128)(2,1)S(1)}, u32[]{:S(2)}, u32[]{:S(2)}) collective-permute-start(bf16[64,2048]{1,0:T(8,128)(2,1)S(1)} %add_convert_fusion.4), channel_id=1, source_target_pairs={{0,4},{1,5},{4,8},{5,9},{8,12},{9,13},{12,14},{13,15},{14,10},{15,... | collective-permute-start | bytes 786440 | tf_op jit(solution)/shard_map/ppermute | solution.py:52
  98.9 1.8 %collective-permute-start.28 = (bf16[64,2048]{1,0:T(8,128)(2,1)S(1)}, bf16[64,2048]{1,0:T(8,128)(2,1)S(1)}, u32[]{:S(2)}, u32[]{:S(2)}) collective-permute-start(bf16[64,2048]{1,0:T(8,128)(2,1)S(1)} %add_convert_fusion.11), channel_id=1, source_target_pairs={{0,4},{1,5},{4,8},{5,9},{8,12},{9,13},{12,14},{13,15},{14,10},{15,... | collective-permute-start | bytes 786440 | tf_op jit(solution)/shard_map/ppermute | solution.py:52
  101.1 5.1 %collective-permute-done.34 = bf16[64,2048]{1,0:T(8,128)(2,1)S(1)} collective-permute-done((bf16[64,2048]{1,0:T(8,128)(2,1)S(1)}, bf16[64,2048]{1,0:T(8,128)(2,1)S(1)}, u32[]{:S(2)}, u32[]{:S(2)}) %collective-permute-start.34) | collective-permute-done | bytes 262176 | tf_op jit(solution)/shard_map/ppermute | solution.py:52
  106.7 1.8 %collective-permute-start.38 = (bf16[64,2048]{1,0:T(8,128)(2,1)S(1)}, bf16[64,2048]{1,0:T(8,128)(2,1)S(1)}, u32[]{:S(2)}, u32[]{:S(2)}) collective-permute-start(bf16[64,2048]{1,0:T(8,128)(2,1)S(1)} %add_convert_fusion.3), channel_id=1, source_target_pairs={{0,4},{1,5},{4,8},{5,9},{8,12},{9,13},{12,14},{13,15},{14,10},{15,... | collective-permute-start | bytes 786440 | tf_op jit(solution)/shard_map/ppermute | solution.py:52
  108.5 3.3 %collective-permute-done.31 = bf16[64,2048]{1,0:T(8,128)(2,1)S(1)} collective-permute-done((bf16[64,2048]{1,0:T(8,128)(2,1)S(1)}, bf16[64,2048]{1,0:T(8,128)(2,1)S(1)}, u32[]{:S(2)}, u32[]{:S(2)}) %collective-permute-start.31) | collective-permute-done | bytes 262176 | tf_op jit(solution)/shard_map/ppermute | solution.py:52
  113.3 2.3 %collective-permute-start.39 = (bf16[64,2048]{1,0:T(8,128)(2,1)S(1)}, bf16[64,2048]{1,0:T(8,128)(2,1)S(1)}, u32[]{:S(2)}, u32[]{:S(2)}) collective-permute-start(bf16[64,2048]{1,0:T(8,128)(2,1)S(1)} %add_convert_fusion.2), channel_id=1, source_target_pairs={{0,4},{1,5},{4,8},{5,9},{8,12},{9,13},{12,14},{13,15},{14,10},{15,... | collective-permute-start | bytes 786440 | tf_op jit(solution)/shard_map/ppermute | solution.py:52
  115.5 5.2 %collective-permute-done.32 = bf16[64,2048]{1,0:T(8,128)(2,1)S(1)} collective-permute-done((bf16[64,2048]{1,0:T(8,128)(2,1)S(1)}, bf16[64,2048]{1,0:T(8,128)(2,1)S(1)}, u32[]{:S(2)}, u32[]{:S(2)}) %collective-permute-start.32) | collective-permute-done | bytes 262176 | tf_op jit(solution)/shard_map/ppermute | solution.py:52
  (78 shorter events, 26.4 us)
Async XLA Ops:
  2.7 21.5 %collective-permute-start.8 = (bf16[688,2048]{1,0:T(8,128)(2,1)}, bf16[688,2048]{1,0:T(8,128)(2,1)S(1)}, u32[]{:S(2)}, u32[]{:S(2)}) collective-permute-start(bf16[688,2048]{1,0:T(8,128)(2,1)} %bitcast.11), channel_id=1, source_target_pairs={{0,1},{1,0},{2,3},{3,2},{4,5},{5,4},{6,7},{7,6},{8,9},{9,8},{10,11... | collective-permute-start | bytes 8454152 | tf_op jit(solution)/shard_map/ppermute | solution.py:55
  2.9 21.3 %collective-permute-start.9 = (bf16[688,2048]{1,0:T(8,128)(2,1)}, bf16[688,2048]{1,0:T(8,128)(2,1)}, u32[]{:S(2)}, u32[]{:S(2)}) collective-permute-start(bf16[688,2048]{1,0:T(8,128)(2,1)} %bitcast.13), channel_id=1, source_target_pairs={{0,1},{1,0},{2,3},{3,2},{4,5},{5,4},{6,7},{7,6},{8,9},{9,8},{10,11... | collective-permute-start | bytes 8454152 | tf_op jit(solution)/shard_map/ppermute | solution.py:55
  3.3 9.5 %collective-permute-start.2 = (bf16[512,128]{1,0:T(8,128)(2,1)S(1)}, bf16[512,128]{1,0:T(8,128)(2,1)S(1)}, u32[]{:S(2)}, u32[]{:S(2)}) collective-permute-start(bf16[512,128]{1,0:T(8,128)(2,1)S(1)} %join.1.refs_0_), channel_id=1, source_target_pairs={{0,4},{1,3},{4,8},{5,1},{8,12},{9,5},{12,14},{13,9},{14,10},{15,13... | collective-permute-start | bytes 393224 | tf_op jit(solution)/shard_map/ppermute | solution.py:63
  15.0 7.8 %collective-permute-start.6 = (bf16[512,128]{1,0:T(8,128)(2,1)S(1)}, bf16[512,128]{1,0:T(8,128)(2,1)S(1)}, u32[]{:S(2)}, u32[]{:S(2)}) collective-permute-start(bf16[512,128]{1,0:T(8,128)(2,1)S(1)} %collective-permute-done.2.refs_1_), channel_id=1, source_target_pairs={{0,1},{1,0},{2,3},{3,2},{4,5},{5,4},{6,7},{7,6},{8,9},{9,8},{10,11... | collective-permute-start | bytes 393224 | tf_op jit(solution)/shard_map/ppermute | solution.py:55
  15.0 7.8 %collective-permute-start.5 = (bf16[512,128]{1,0:T(8,128)(2,1)S(1)}, bf16[512,128]{1,0:T(8,128)(2,1)S(1)}, u32[]{:S(2)}, u32[]{:S(2)}) collective-permute-start(bf16[512,128]{1,0:T(8,128)(2,1)S(1)} %collective-permute-done.3.refs_2_), channel_id=1, source_target_pairs={{0,8},{1,7},{4,12},{5,3},{8,14},{9,1},{12,10},{13,5},{14,6},{15,9}... | collective-permute-start | bytes 393224 | tf_op jit(solution)/shard_map/ppermute | solution.py:63
  29.5 9.8 %collective-permute-start.12 = (bf16[64,2048]{1,0:T(8,128)(2,1)S(1)}, bf16[64,2048]{1,0:T(8,128)(2,1)S(1)}, u32[]{:S(2)}, u32[]{:S(2)}) collective-permute-start(bf16[64,2048]{1,0:T(8,128)(2,1)S(1)} %get-tuple-element.170.refs_2_), channel_id=1, source_target_pairs={{0,4},{1,5},{4,8},{5,9},{8,12},{9,13},{12,14},{13,15},{14,10},{15,... | collective-permute-start | bytes 786440 | tf_op jit(solution)/shard_map/ppermute | solution.py:52
  30.4 9.3 %collective-permute-start.13 = (bf16[64,2048]{1,0:T(8,128)(2,1)S(1)}, bf16[64,2048]{1,0:T(8,128)(2,1)S(1)}, u32[]{:S(2)}, u32[]{:S(2)}) collective-permute-start(bf16[64,2048]{1,0:T(8,128)(2,1)S(1)} %get-tuple-element.171.refs_3_), channel_id=1, source_target_pairs={{0,2},{1,3},{4,0},{5,1},{8,4},{9,5},{12,8},{13,9},{14,12},{15,13},... | collective-permute-start | bytes 786440 | tf_op jit(solution)/shard_map/ppermute | solution.py:52
  31.5 15.3 %collective-permute-start.14 = (bf16[64,2048]{1,0:T(8,128)(2,1)S(1)}, bf16[64,2048]{1,0:T(8,128)(2,1)S(1)}, u32[]{:S(2)}, u32[]{:S(2)}) collective-permute-start(bf16[64,2048]{1,0:T(8,128)(2,1)S(1)} %get-tuple-element.171.refs_3_), channel_id=1, source_target_pairs={{0,4},{1,5},{4,8},{5,9},{8,12},{9,13},{12,14},{13,15},{14,10},{15,... | collective-permute-start | bytes 786440 | tf_op jit(solution)/shard_map/ppermute | solution.py:52
  32.6 14.1 %collective-permute-start.15 = (bf16[64,2048]{1,0:T(8,128)(2,1)S(1)}, bf16[64,2048]{1,0:T(8,128)(2,1)S(1)}, u32[]{:S(2)}, u32[]{:S(2)}) collective-permute-start(bf16[64,2048]{1,0:T(8,128)(2,1)S(1)} %get-tuple-element.170.refs_2_), channel_id=1, source_target_pairs={{0,2},{1,3},{4,0},{5,1},{8,4},{9,5},{12,8},{13,9},{14,12},{15,13},... | collective-permute-start | bytes 786440 | tf_op jit(solution)/shard_map/ppermute | solution.py:52
  39.8 9.6 %collective-permute-start.16 = (bf16[64,2048]{1,0:T(8,128)(2,1)S(1)}, bf16[64,2048]{1,0:T(8,128)(2,1)S(1)}, u32[]{:S(2)}, u32[]{:S(2)}) collective-permute-start(bf16[64,2048]{1,0:T(8,128)(2,1)S(1)} %collective-permute-done.12.refs_0_), channel_id=1, source_target_pairs={{0,4},{1,5},{4,8},{5,9},{8,12},{9,13},{12,14},{13,15},{14,10},{15,... | collective-permute-start | bytes 786440 | tf_op jit(solution)/shard_map/ppermute | solution.py:52
  41.7 9.3 %collective-permute-start.19 = (bf16[64,2048]{1,0:T(8,128)(2,1)S(1)}, bf16[64,2048]{1,0:T(8,128)(2,1)S(1)}, u32[]{:S(2)}, u32[]{:S(2)}) collective-permute-start(bf16[64,2048]{1,0:T(8,128)(2,1)S(1)} %collective-permute-done.13.refs_1_), channel_id=1, source_target_pairs={{0,2},{1,3},{4,0},{5,1},{8,4},{9,5},{12,8},{13,9},{14,12},{15,13},... | collective-permute-start | bytes 786440 | tf_op jit(solution)/shard_map/ppermute | solution.py:52
  46.8 9.6 %collective-permute-start.22 = (bf16[64,2048]{1,0:T(8,128)(2,1)S(1)}, bf16[64,2048]{1,0:T(8,128)(2,1)S(1)}, u32[]{:S(2)}, u32[]{:S(2)}) collective-permute-start(bf16[64,2048]{1,0:T(8,128)(2,1)S(1)} %collective-permute-done.14.refs_2_), channel_id=1, source_target_pairs={{0,4},{1,5},{4,8},{5,9},{8,12},{9,13},{12,14},{13,15},{14,10},{15,... | collective-permute-start | bytes 786440 | tf_op jit(solution)/shard_map/ppermute | solution.py:52
  48.8 9.2 %collective-permute-start.23 = (bf16[64,2048]{1,0:T(8,128)(2,1)S(1)}, bf16[64,2048]{1,0:T(8,128)(2,1)S(1)}, u32[]{:S(2)}, u32[]{:S(2)}) collective-permute-start(bf16[64,2048]{1,0:T(8,128)(2,1)S(1)} %collective-permute-done.15.refs_3_), channel_id=1, source_target_pairs={{0,2},{1,3},{4,0},{5,1},{8,4},{9,5},{12,8},{13,9},{14,12},{15,13},... | collective-permute-start | bytes 786440 | tf_op jit(solution)/shard_map/ppermute | solution.py:52
  49.4 12.3 %collective-permute-start.17 = (bf16[64,2048]{1,0:T(8,128)(2,1)S(1)}, bf16[64,2048]{1,0:T(8,128)(2,1)S(1)}, u32[]{:S(2)}, u32[]{:S(2)}) collective-permute-start(bf16[64,2048]{1,0:T(8,128)(2,1)S(1)} %collective-permute-done.16.refs_0_), channel_id=1, source_target_pairs={{0,4},{1,5},{4,8},{5,9},{8,12},{9,13},{12,14},{13,15},{14,10},{15,... | collective-permute-start | bytes 786440 | tf_op jit(solution)/shard_map/ppermute | solution.py:52
  51.0 12.6 %collective-permute-start.20 = (bf16[64,2048]{1,0:T(8,128)(2,1)S(1)}, bf16[64,2048]{1,0:T(8,128)(2,1)S(1)}, u32[]{:S(2)}, u32[]{:S(2)}) collective-permute-start(bf16[64,2048]{1,0:T(8,128)(2,1)S(1)} %collective-permute-done.19.refs_1_), channel_id=1, source_target_pairs={{0,2},{1,3},{4,0},{5,1},{8,4},{9,5},{12,8},{13,9},{14,12},{15,13},... | collective-permute-start | bytes 786440 | tf_op jit(solution)/shard_map/ppermute | solution.py:52
  58.0 10.7 %collective-permute-start.24 = (bf16[64,2048]{1,0:T(8,128)(2,1)S(1)}, bf16[64,2048]{1,0:T(8,128)(2,1)S(1)}, u32[]{:S(2)}, u32[]{:S(2)}) collective-permute-start(bf16[64,2048]{1,0:T(8,128)(2,1)S(1)} %collective-permute-done.22.refs_2_), channel_id=1, source_target_pairs={{0,4},{1,5},{4,8},{5,9},{8,12},{9,13},{12,14},{13,15},{14,10},{15,... | collective-permute-start | bytes 786440 | tf_op jit(solution)/shard_map/ppermute | solution.py:52
  59.3 10.0 %collective-permute-start.25 = (bf16[64,2048]{1,0:T(8,128)(2,1)S(1)}, bf16[64,2048]{1,0:T(8,128)(2,1)S(1)}, u32[]{:S(2)}, u32[]{:S(2)}) collective-permute-start(bf16[64,2048]{1,0:T(8,128)(2,1)S(1)} %collective-permute-done.23.refs_3_), channel_id=1, source_target_pairs={{0,2},{1,3},{4,0},{5,1},{8,4},{9,5},{12,8},{13,9},{14,12},{15,13},... | collective-permute-start | bytes 786440 | tf_op jit(solution)/shard_map/ppermute | solution.py:52
  61.7 9.8 %collective-permute-start.18 = (bf16[64,2048]{1,0:T(8,128)(2,1)S(1)}, bf16[64,2048]{1,0:T(8,128)(2,1)S(1)}, u32[]{:S(2)}, u32[]{:S(2)}) collective-permute-start(bf16[64,2048]{1,0:T(8,128)(2,1)S(1)} %collective-permute-done.17.refs_0_), channel_id=1, source_target_pairs={{0,4},{1,5},{4,8},{5,9},{8,12},{9,13},{12,14},{13,15},{14,10},{15,... | collective-permute-start | bytes 786440 | tf_op jit(solution)/shard_map/ppermute | solution.py:52
  63.6 9.7 %collective-permute-start.21 = (bf16[64,2048]{1,0:T(8,128)(2,1)S(1)}, bf16[64,2048]{1,0:T(8,128)(2,1)S(1)}, u32[]{:S(2)}, u32[]{:S(2)}) collective-permute-start(bf16[64,2048]{1,0:T(8,128)(2,1)S(1)} %collective-permute-done.20.refs_1_), channel_id=1, source_target_pairs={{0,2},{1,3},{4,0},{5,1},{8,4},{9,5},{12,8},{13,9},{14,12},{15,13},... | collective-permute-start | bytes 786440 | tf_op jit(solution)/shard_map/ppermute | solution.py:52
  78.3 9.3 %collective-permute-start.26 = (bf16[64,2048]{1,0:T(8,128)(2,1)S(1)}, bf16[64,2048]{1,0:T(8,128)(2,1)S(1)}, u32[]{:S(2)}, u32[]{:S(2)}) collective-permute-start(bf16[64,2048]{1,0:T(8,128)(2,1)S(1)} %get-tuple-element.199), channel_id=1, source_target_pairs={{0,4},{1,5},{4,8},{5,9},{8,12},{9,13},{12,14},{13,15},{14,10},{15,... | collective-permute-start | bytes 786440 | tf_op jit(solution)/shard_map/ppermute | solution.py:52
  80.1 9.4 %collective-permute-start.29 = (bf16[64,2048]{1,0:T(8,128)(2,1)S(1)}, bf16[64,2048]{1,0:T(8,128)(2,1)S(1)}, u32[]{:S(2)}, u32[]{:S(2)}) collective-permute-start(bf16[64,2048]{1,0:T(8,128)(2,1)S(1)} %get-tuple-element.202), channel_id=1, source_target_pairs={{0,2},{1,3},{4,0},{5,1},{8,4},{9,5},{12,8},{13,9},{14,12},{15,13},... | collective-permute-start | bytes 786440 | tf_op jit(solution)/shard_map/ppermute | solution.py:52
  80.4 14.6 %collective-permute-start.33 = (bf16[64,2048]{1,0:T(8,128)(2,1)S(1)}, bf16[64,2048]{1,0:T(8,128)(2,1)S(1)}, u32[]{:S(2)}, u32[]{:S(2)}) collective-permute-start(bf16[64,2048]{1,0:T(8,128)(2,1)S(1)} %get-tuple-element.207), channel_id=1, source_target_pairs={{0,2},{1,3},{4,0},{5,1},{8,4},{9,5},{12,8},{13,9},{14,12},{15,13},... | collective-permute-start | bytes 786440 | tf_op jit(solution)/shard_map/ppermute | solution.py:52
  80.4 15.0 %collective-permute-start.36 = (bf16[64,2048]{1,0:T(8,128)(2,1)S(1)}, bf16[64,2048]{1,0:T(8,128)(2,1)S(1)}, u32[]{:S(2)}, u32[]{:S(2)}) collective-permute-start(bf16[64,2048]{1,0:T(8,128)(2,1)S(1)} %get-tuple-element.210), channel_id=1, source_target_pairs={{0,4},{1,5},{4,8},{5,9},{8,12},{9,13},{12,14},{13,15},{14,10},{15,... | collective-permute-start | bytes 786440 | tf_op jit(solution)/shard_map/ppermute | solution.py:52
  87.7 11.2 %collective-permute-start.27 = (bf16[64,2048]{1,0:T(8,128)(2,1)S(1)}, bf16[64,2048]{1,0:T(8,128)(2,1)S(1)}, u32[]{:S(2)}, u32[]{:S(2)}) collective-permute-start(bf16[64,2048]{1,0:T(8,128)(2,1)S(1)} %add_convert_fusion.12), channel_id=1, source_target_pairs={{0,4},{1,5},{4,8},{5,9},{8,12},{9,13},{12,14},{13,15},{14,10},{15,... | collective-permute-start | bytes 786440 | tf_op jit(solution)/shard_map/ppermute | solution.py:52
  89.5 11.2 %collective-permute-start.30 = (bf16[64,2048]{1,0:T(8,128)(2,1)S(1)}, bf16[64,2048]{1,0:T(8,128)(2,1)S(1)}, u32[]{:S(2)}, u32[]{:S(2)}) collective-permute-start(bf16[64,2048]{1,0:T(8,128)(2,1)S(1)} %add_convert_fusion.10), channel_id=1, source_target_pairs={{0,2},{1,3},{4,0},{5,1},{8,4},{9,5},{12,8},{13,9},{14,12},{15,13},... | collective-permute-start | bytes 786440 | tf_op jit(solution)/shard_map/ppermute | solution.py:52
  95.0 11.2 %collective-permute-start.34 = (bf16[64,2048]{1,0:T(8,128)(2,1)S(1)}, bf16[64,2048]{1,0:T(8,128)(2,1)S(1)}, u32[]{:S(2)}, u32[]{:S(2)}) collective-permute-start(bf16[64,2048]{1,0:T(8,128)(2,1)S(1)} %add_convert_fusion.6), channel_id=1, source_target_pairs={{0,2},{1,3},{4,0},{5,1},{8,4},{9,5},{12,8},{13,9},{14,12},{15,13},... | collective-permute-start | bytes 786440 | tf_op jit(solution)/shard_map/ppermute | solution.py:52
  95.4 11.2 %collective-permute-start.37 = (bf16[64,2048]{1,0:T(8,128)(2,1)S(1)}, bf16[64,2048]{1,0:T(8,128)(2,1)S(1)}, u32[]{:S(2)}, u32[]{:S(2)}) collective-permute-start(bf16[64,2048]{1,0:T(8,128)(2,1)S(1)} %add_convert_fusion.4), channel_id=1, source_target_pairs={{0,4},{1,5},{4,8},{5,9},{8,12},{9,13},{12,14},{13,15},{14,10},{15,... | collective-permute-start | bytes 786440 | tf_op jit(solution)/shard_map/ppermute | solution.py:52
  98.9 16.7 %collective-permute-start.28 = (bf16[64,2048]{1,0:T(8,128)(2,1)S(1)}, bf16[64,2048]{1,0:T(8,128)(2,1)S(1)}, u32[]{:S(2)}, u32[]{:S(2)}) collective-permute-start(bf16[64,2048]{1,0:T(8,128)(2,1)S(1)} %add_convert_fusion.11), channel_id=1, source_target_pairs={{0,4},{1,5},{4,8},{5,9},{8,12},{9,13},{12,14},{13,15},{14,10},{15,... | collective-permute-start | bytes 786440 | tf_op jit(solution)/shard_map/ppermute | solution.py:52
  100.8 11.0 %collective-permute-start.31 = (bf16[64,2048]{1,0:T(8,128)(2,1)S(1)}, bf16[64,2048]{1,0:T(8,128)(2,1)S(1)}, u32[]{:S(2)}, u32[]{:S(2)}) collective-permute-start(bf16[64,2048]{1,0:T(8,128)(2,1)S(1)} %add_convert_fusion.9), channel_id=1, source_target_pairs={{0,2},{1,3},{4,0},{5,1},{8,4},{9,5},{12,8},{13,9},{14,12},{15,13},... | collective-permute-start | bytes 786440 | tf_op jit(solution)/shard_map/ppermute | solution.py:52
  106.3 14.6 %collective-permute-start.35 = (bf16[64,2048]{1,0:T(8,128)(2,1)S(1)}, bf16[64,2048]{1,0:T(8,128)(2,1)S(1)}, u32[]{:S(2)}, u32[]{:S(2)}) collective-permute-start(bf16[64,2048]{1,0:T(8,128)(2,1)S(1)} %add_convert_fusion.5), channel_id=1, source_target_pairs={{0,2},{1,3},{4,0},{5,1},{8,4},{9,5},{12,8},{13,9},{14,12},{15,13},... | collective-permute-start | bytes 786440 | tf_op jit(solution)/shard_map/ppermute | solution.py:52
  111.9 8.9 %collective-permute-start.32 = (bf16[64,2048]{1,0:T(8,128)(2,1)S(1)}, bf16[64,2048]{1,0:T(8,128)(2,1)S(1)}, u32[]{:S(2)}, u32[]{:S(2)}) collective-permute-start(bf16[64,2048]{1,0:T(8,128)(2,1)S(1)} %add_convert_fusion.8), channel_id=1, source_target_pairs={{0,2},{1,3},{4,0},{5,1},{8,4},{9,5},{12,8},{13,9},{14,12},{15,13},... | collective-permute-start | bytes 786440 | tf_op jit(solution)/shard_map/ppermute | solution.py:52
  113.3 7.6 %collective-permute-start.39 = (bf16[64,2048]{1,0:T(8,128)(2,1)S(1)}, bf16[64,2048]{1,0:T(8,128)(2,1)S(1)}, u32[]{:S(2)}, u32[]{:S(2)}) collective-permute-start(bf16[64,2048]{1,0:T(8,128)(2,1)S(1)} %add_convert_fusion.2), channel_id=1, source_target_pairs={{0,4},{1,5},{4,8},{5,9},{8,12},{9,13},{12,14},{13,15},{14,10},{15,... | collective-permute-start | bytes 786440 | tf_op jit(solution)/shard_map/ppermute | solution.py:52
  (11 other events, 96.7 us)
where the time goes:
time: 122 us
  waiting for transfers between devices  47.5 us (39%)
  starting transfers between devices  38.8 us (32%)
  Pallas kernels  32.1 us (26%)
  other arithmetic  2.63 us (2%)
    ppermute x28, waiting for transfers between devices, go(): return lax.ppermute(block, 'ctx', pairs)  35.8 us
    ppermute x28, starting transfers between devices, go(): return lax.ppermute(block, 'ctx', pairs)  29.2 us
    pallas_call x4, Pallas kernels, ffn(): pl.pallas_call(functools.partial(ffn_kernel, count), out_shape=tuple((jax...  19.8 us
    pallas_call x3, Pallas kernels, load(): pl.pallas_call(functools.partial(load_kernel, count), out_shape=tuple((pl...  8.43 us
    ppermute x4, starting transfers between devices, go_split(): return lax.ppermute(block, 'ctx', pairs)  8.3 us
    ppermute x4, waiting for transfers between devices, go_split(): return lax.ppermute(block, 'ctx', pairs)  7.11 us
    ppermute x8, waiting for transfers between devices, go_mate(): return lax.ppermute(block, 'ctx', self.swap)  4.61 us
    pallas_call x1, Pallas kernels, attend(): pl.pallas_call(functools.partial(attention_kernel, count, len(blocks), he...  3.11 us
  transfers between devices with their start and end apart: 40, of which 22 were waited for; matrix products, arithmetic and copies ran while one was open for 2% of the time, Pallas kernels for 22%

commit v1 on v0

--- a/solution.py
+++ b/solution.py
@@ -76,7 +76,6 @@
 
 
 def attention_kernel(
-    count,
     pieces,
     heads,
     head_dim,
@@ -95,7 +94,6 @@
     chunk_refs, refs = refs[:CHUNKS], refs[CHUNKS:]
     (residual_ref, stacked, scores, top, total, summed) = refs
     rows = query_ref.shape[0]
-    places = [(block, 2 * k) for block in blocks for k in range(block.shape[0] // (2 * rows))]
     me = owner_ref[0]
     for head in range(heads):
         stacked[pl.ds(head * rows, rows), :] = query_ref[:, head * head_dim : (head + 1) * head_dim]
@@ -122,45 +120,48 @@
         )
         return (owner <= me) & (last_pair >= my_first) & jnp.logical_not(apart)
 
+    def bias_of(owner):
+        key_role = role_ref[pl.ds(owner, 1), :]
+        seen = (
+            (query_pair == pair_ref[pl.ds(owner, 1), :])
+            & (owner * rows + key_off <= query_pos)
+            & ((key_role == 0) | (key_role == query_role))
+        )
+        return jnp.where(seen, 0.0, NEG_FILL)
+
     top[...] = jnp.full_like(top, NEG_FILL)
     total[...] = jnp.zeros_like(total)
     summed[...] = jnp.zeros_like(summed)
-    for j in range(count):
-        owner = owner_ref[j]
-
-        @pl.when(needed(owner))
+    for j, block in enumerate(blocks):
+        owners = owner_ref[2 * j], owner_ref[2 * j + 1]
+
+        @pl.when(needed(owners[0]) | needed(owners[1]))
         def _():
-            seen = (
-                (query_pair == pair_ref[pl.ds(owner, 1), :])
-                & (owner * rows + key_off <= query_pos)
-                & (
-                    (role_ref[pl.ds(owner, 1), :] == 0)
-                    | (role_ref[pl.ds(owner, 1), :] == query_role)
-                )
-            )
-            bias = jnp.where(seen, 0.0, NEG_FILL)
+            bias = jnp.concatenate([bias_of(owner) for owner in owners], axis=1)
             raw = lax.dot_general(
                 stacked[...],
-                places[j][0][pl.ds(places[j][1] * rows, rows), :],
+                block[pl.ds(0, 2 * rows), :],
                 (((1,), (1,)), ((), ())),
                 preferred_element_type=jnp.float32,
             )
-            masked = raw.reshape(heads, rows, rows) + bias[None]
+            masked = raw.reshape(heads, rows, 2 * rows) + bias[None]
             scores[j] = masked
-            top[...] = jnp.maximum(top[...], masked)
+            top[...] = jnp.maximum(
+                top[...], jnp.maximum(masked[:, :, :rows], masked[:, :, rows:])
+            )
 
     top[...] = jnp.broadcast_to(jnp.max(top[...], axis=-1, keepdims=True), top.shape)
     factor = math.log2(math.e) / math.sqrt(head_dim)
-    for j in range(count):
-        owner = owner_ref[j]
-
-        @pl.when(needed(owner))
+    for j, block in enumerate(blocks):
+        owners = owner_ref[2 * j], owner_ref[2 * j + 1]
+
+        @pl.when(needed(owners[0]) | needed(owners[1]))
         def _():
-            weights = jnp.exp2((scores[j] - top[...]) * factor)
-            total[...] += weights
+            weights = jnp.exp2((scores[j] - jnp.concatenate([top[...]] * 2, axis=2)) * factor)
+            total[...] += weights[:, :, :rows] + weights[:, :, rows:]
             summed[...] += jnp.dot(
-                weights.astype(jnp.bfloat16).reshape(heads * rows, rows),
-                places[j][0][pl.ds((places[j][1] + 1) * rows, rows), :],
+                weights.astype(jnp.bfloat16).reshape(heads * rows, 2 * rows),
+                block[pl.ds(2 * rows, 2 * rows), :],
                 preferred_element_type=jnp.float32,
             ).reshape(heads, rows, head_dim)
 
@@ -189,13 +190,13 @@
     square = pltpu.VMEM((heads, rows, rows), jnp.float32)
     chunk = jax.ShapeDtypeStruct((rows // CHUNKS, hidden.shape[1]), jnp.bfloat16)
     *chunks, residual = pl.pallas_call(
-        functools.partial(attention_kernel, count, len(blocks), heads, head_dim),
+        functools.partial(attention_kernel, len(blocks), heads, head_dim),
         out_shape=(chunk,) * CHUNKS + (jax.ShapeDtypeStruct(hidden.shape, jnp.bfloat16),),
         in_specs=[smem] * 3 + [vmem] * (len(inputs) + len(blocks)),
         out_specs=(vmem,) * (CHUNKS + 1),
         scratch_shapes=[
             pltpu.VMEM((heads * rows, head_dim), jnp.bfloat16),
-            pltpu.VMEM((count, heads, rows, rows), jnp.float32),
+            pltpu.VMEM((len(blocks), heads, rows, 2 * rows), jnp.float32),
             square,
             square,
             pltpu.VMEM((heads, rows, head_dim), jnp.float32),
@@ -229,30 +230,31 @@
 
 
 def join_kernel(count, *refs):
-    inputs, both_ref, sems = refs[:count], refs[count], refs[count + 1]
+    inputs, both_ref, sems = refs[: 2 * count], refs[2 * count], refs[2 * count + 1]
     rows = inputs[0].shape[0]
-    moves = [
-        pltpu.make_async_copy(inputs[k], both_ref.at[pl.ds(k * rows, rows), :], sems.at[k])
-        for k in range(count)
-    ]
+    moves = []
+    for k in range(2 * count):
+        owner, kind = divmod(k, count)
+        place = pl.ds((kind * 2 + owner) * rows, rows)
+        moves.append(pltpu.make_async_copy(inputs[k], both_ref.at[place, :], sems.at[k]))
     for move in moves:
         move.start()
     for move in moves:
         move.wait()
 
 
-def join(*parts):
-    count = len(parts)
-    rows, width = parts[0].shape
+def join(own, mate):
+    count = len(own)
+    rows, width = own[0].shape
     return pl.pallas_call(
         functools.partial(join_kernel, count),
-        out_shape=pltpu.VMEM((count * rows, width), parts[0].dtype),
-        in_specs=[pl.BlockSpec(memory_space=pl.ANY)] * (count // CORES)
-        + [pl.BlockSpec(memory_space=pltpu.VMEM)] * (count - count // CORES),
+        out_shape=pltpu.VMEM((2 * count * rows, width), own[0].dtype),
+        in_specs=[pl.BlockSpec(memory_space=pl.ANY)] * count
+        + [pl.BlockSpec(memory_space=pltpu.VMEM)] * count,
         out_specs=pl.BlockSpec(memory_space=pltpu.VMEM),
-        scratch_shapes=[pltpu.SemaphoreType.DMA((count,))],
+        scratch_shapes=[pltpu.SemaphoreType.DMA((2 * count,))],
         name="join",
-    )(*parts)
+    )(*own, *mate)
 
 
 def ffn_kernel(blocks, *refs):
@@ -348,7 +350,9 @@
 def gather_kv(ring, keys, values, weights, extras):
     half = ring.half
     gate, up, down = weights
-    both = join(in_hbm(keys), in_hbm(values), *(in_vmem(ring.go_mate(x)) for x in (keys, values)))
+    both = join(
+        (in_hbm(keys), in_hbm(values)), (in_vmem(ring.go_mate(keys)), in_vmem(ring.go_mate(values)))
+    )
     gate, up, both = lax.optimization_barrier((gate, up, both))
     gate_mate, up_mate = ring.go_mate(gate), ring.go_mate(up)
     held, mates = {0: both}, {}

time: 122 us -> 121 us (level)
  transfers between devices with their start and end apart: 40 -> 40, of which waited for: 22 -> 21; matrix products, arithmetic and copies ran while one was open for 2% -> 2% of each run, Pallas kernels for 22% -> 22%
where the time goes in v1:
time: 121 us
  waiting for transfers between devices  47.1 us (39%)
  starting transfers between devices  37.8 us (31%)
  Pallas kernels  32.1 us (27%)
  other arithmetic  2.63 us (2%)
    ppermute x28, waiting for transfers between devices, go(): return lax.ppermute(block, 'ctx', pairs)  35.4 us
    ppermute x28, starting transfers between devices, go(): return lax.ppermute(block, 'ctx', pairs)  28.2 us
    pallas_call x4, Pallas kernels, ffn(): pl.pallas_call(functools.partial(ffn_kernel, count), out_shape=tuple((jax...  19.7 us
    pallas_call x3, Pallas kernels, load(): pl.pallas_call(functools.partial(load_kernel, count), out_shape=tuple((pl...  8.43 us
    ppermute x4, starting transfers between devices, go_split(): return lax.ppermute(block, 'ctx', pairs)  8.3 us
    ppermute x4, waiting for transfers between devices, go_split(): return lax.ppermute(block, 'ctx', pairs)  7.11 us
    ppermute x8, waiting for transfers between devices, go_mate(): return lax.ppermute(block, 'ctx', self.swap)  4.61 us
    pallas_call x1, Pallas kernels, attend(): pl.pallas_call(functools.partial(attention_kernel, len(blocks), heads, he...  3.12 us
  transfers between devices with their start and end apart: 40, of which 21 were waited for; matrix products, arithmetic and copies ran while one was open for 2% of the time, Pallas kernels for 22%

profile of v1, /device:TPU:0, one launch (start us, length us, event | category | flops | bytes accessed | tf_op | source)
XLA Modules:
  0.0 120.6 jit_solution(13359658404966513125)
XLA Ops:
  3.3 2.7 %collective-permute-start.2 = (bf16[512,128]{1,0:T(8,128)(2,1)S(1)}, bf16[512,128]{1,0:T(8,128)(2,1)S(1)}, u32[]{:S(2)}, u32[]{:S(2)}) collective-permute-start(bf16[512,128]{1,0:T(8,128)(2,1)S(1)} %join.1.refs_0_), channel_id=1, source_target_pairs={{0,4},{1,3},{4,8},{5,1},{8,12},{9,5},{12,14},{13,9},{14,10},{15,13... | collective-permute-start | bytes 393224 | tf_op jit(solution)/shard_map/ppermute | solution.py:63
  6.0 2.6 %collective-permute-start.3 = (bf16[512,128]{1,0:T(8,128)(2,1)S(1)}, bf16[512,128]{1,0:T(8,128)(2,1)S(1)}, u32[]{:S(2)}, u32[]{:S(2)}) collective-permute-start(bf16[512,128]{1,0:T(8,128)(2,1)S(1)} %join.1.refs_0_), channel_id=1, source_target_pairs={{0,8},{1,7},{4,12},{5,3},{8,14},{9,1},{12,10},{13,5},{14,6},{15,9}... | collective-permute-start | bytes 393224 | tf_op jit(solution)/shard_map/ppermute | solution.py:63
  9.4 2.7 %load.3 = (bf16[128,1024]{1,0:T(8,128)(2,1)S(1)}, s32[16,128]{1,0:T(8,128)S(1)}, s32[16,128]{1,0:T(8,128)S(1)}, bf16[128,2048]{1,0:T(8,128)(2,1)S(1)}, f32[1,204...) custom-call(bf16[128,1024]{1,0:T(8,128)(2,1)} %refs_0_.3, s32[16,128]{1,0:T(8,128)} %bitcast.7, s32[16,128]{1,0:T(8,128)} %bitcast.9, ...), custom_call_target="tpu_custom_call" | custom-call | tf_op jit(solution)/shard_map/load/pallas_call | solution.py:221
  13.3 1.7 %collective-permute-start.4 = (bf16[512,128]{1,0:T(8,128)(2,1)S(1)}, bf16[512,128]{1,0:T(8,128)(2,1)S(1)}, u32[]{:S(2)}, u32[]{:S(2)}) collective-permute-start(bf16[512,128]{1,0:T(8,128)(2,1)S(1)} %collective-permute-done.2.refs_1_), channel_id=1, source_target_pairs={{0,8},{1,7},{4,12},{5,3},{8,14},{9,1},{12,10},{13,5},{14,6},{15,9}... | collective-permute-start | bytes 393224 | tf_op jit(solution)/shard_map/ppermute | solution.py:63
  16.3 4.0 %collective-permute-done.4.refs_3_ = bf16[512,128]{1,0:T(8,128)(2,1)S(1)} collective-permute-done((bf16[512,128]{1,0:T(8,128)(2,1)S(1)}, bf16[512,128]{1,0:T(8,128)(2,1)S(1)}, u32[]{:S(2)}, u32[]{:S(2)}) %collective-permute-start.4) | collective-permute-done | bytes 131104 | tf_op jit(solution)/shard_map/ppermute | solution.py:63
  20.2 2.6 %collective-permute-done.5.refs_4_ = bf16[512,128]{1,0:T(8,128)(2,1)S(1)} collective-permute-done((bf16[512,128]{1,0:T(8,128)(2,1)S(1)}, bf16[512,128]{1,0:T(8,128)(2,1)S(1)}, u32[]{:S(2)}, u32[]{:S(2)}) %collective-permute-start.5) | collective-permute-done | bytes 131104 | tf_op jit(solution)/shard_map/ppermute | solution.py:63
  22.9 1.3 %collective-permute-done.10.refs_7_ = bf16[512,128]{1,0:T(8,128)(2,1)S(1)} collective-permute-done((bf16[512,128]{1,0:T(8,128)(2,1)S(1)}, bf16[512,128]{1,0:T(8,128)(2,1)S(1)}, u32[]{:S(2)}, u32[]{:S(2)}) %collective-permute-start.10) | collective-permute-done | bytes 131104 | tf_op jit(solution)/shard_map/ppermute | solution.py:55
  24.4 3.1 %attention.1 = (bf16[64,2048]{1,0:T(8,128)(2,1)S(1)}, bf16[64,2048]{1,0:T(8,128)(2,1)S(1)}, bf16[128,2048]{1,0:T(8,128)(2,1)S(1)}) custom-call(s32[16]{0:T(128)S(1)} %dynamic-slice_bitcast_fusion.owner_ref, s32[16,128]{1,0:T(8,128)S(1)} %bitcast.8, s32[16,128]{1,0:T(8,128)S(1)} %bitcast.10, bf16[128,1024]{1,0:T(8,128)(2,1)S(1)} %get-tuple-element.129.query_ref, ...), custom_call_target="tpu_custom_call" | custom-call | tf_op jit(solution)/shard_map/attention/pallas_call | solution.py:192
  27.6 1.9 %collective-permute-done.11.refs_2_ = bf16[688,2048]{1,0:T(8,128)(2,1)S(1)} collective-permute-done((bf16[688,2048]{1,0:T(8,128)(2,1)S(1)}, bf16[688,2048]{1,0:T(8,128)(2,1)S(1)}, u32[]{:S(2)}, u32[]{:S(2)}) %collective-permute-start.11) | collective-permute-done | bytes 2818080 | tf_op jit(solution)/shard_map/ppermute | solution.py:55
  33.5 2.2 %load.5 = (bf16[688,2048]{1,0:T(8,128)(2,1)S(1)}, bf16[688,2048]{1,0:T(8,128)(2,1)S(1)}, bf16[688,2048]{1,0:T(8,128)(2,1)S(1)}) custom-call(bf16[688,2048]{1,0:T(8,128)(2,1)S(1)} %collective-permute-done.8.refs_0_, bf16[688,2048]{1,0:T(8,128)(2,1)} %collective-permute-done.9.refs_1_, bf16[688,2048]{1,0:T(8,128)(2,1)S(1)} %collective-permute-done.11.refs_2_), custom_call_target="tpu_custom_call" | custom-call | tf_op jit(solution)/shard_map/load/pallas_call | solution.py:221
  35.8 3.5 %load.4 = (bf16[688,2048]{1,0:T(8,128)(2,1)S(1)}, bf16[688,2048]{1,0:T(8,128)(2,1)S(1)}, bf16[688,2048]{1,0:T(8,128)(2,1)S(1)}) custom-call(bf16[688,2048]{1,0:T(8,128)(2,1)} %bitcast.12, bf16[688,2048]{1,0:T(8,128)(2,1)} %bitcast.14, bf16[688,2048]{1,0:T(8,128)(2,1)} %refs_2_), custom_call_target="tpu_custom_call" | custom-call | tf_op jit(solution)/shard_map/load/pallas_call | solution.py:221
  39.6 1.3 %collective-permute-start.16 = (bf16[64,2048]{1,0:T(8,128)(2,1)S(1)}, bf16[64,2048]{1,0:T(8,128)(2,1)S(1)}, u32[]{:S(2)}, u32[]{:S(2)}) collective-permute-start(bf16[64,2048]{1,0:T(8,128)(2,1)S(1)} %collective-permute-done.12.refs_0_), channel_id=1, source_target_pairs={{0,4},{1,5},{4,8},{5,9},{8,12},{9,13},{12,14},{13,15},{14,10},{15,... | collective-permute-start | bytes 786440 | tf_op jit(solution)/shard_map/ppermute | solution.py:52
  41.7 4.9 %feed_forward.4 = (bf16[64,2048]{1,0:T(8,128)(2,1)S(1)}, bf16[64,2048]{1,0:T(8,128)(2,1)S(1)}, bf16[64,2048]{1,0:T(8,128)(2,1)S(1)}, bf16[64,2048]{1,0:T(8,128)(2,1)S(1)}) custom-call(bf16[64,2048]{1,0:T(8,128)(2,1)S(1)} %collective-permute-done.12.refs_0_, bf16[64,2048]{1,0:T(8,128)(2,1)S(1)} %collective-permute-done.13.refs_1_, ...), custom_call_target="tpu_custom_call" | custom-call | flops 1000 | bytes 1000 | tf_op jit(solution)/shard_map/feed_forward/pallas_call | solution.py:286
  46.6 1.4 %collective-permute-start.22 = (bf16[64,2048]{1,0:T(8,128)(2,1)S(1)}, bf16[64,2048]{1,0:T(8,128)(2,1)S(1)}, u32[]{:S(2)}, u32[]{:S(2)}) collective-permute-start(bf16[64,2048]{1,0:T(8,128)(2,1)S(1)} %collective-permute-done.14.refs_2_), channel_id=1, source_target_pairs={{0,4},{1,5},{4,8},{5,9},{8,12},{9,13},{12,14},{13,15},{14,10},{15,... | collective-permute-start | bytes 786440 | tf_op jit(solution)/shard_map/ppermute | solution.py:52
  51.9 4.9 %feed_forward.6 = (bf16[64,2048]{1,0:T(8,128)(2,1)S(1)}, bf16[64,2048]{1,0:T(8,128)(2,1)S(1)}, bf16[64,2048]{1,0:T(8,128)(2,1)S(1)}, bf16[64,2048]{1,0:T(8,128)(2,1)S(1)}) custom-call(bf16[64,2048]{1,0:T(8,128)(2,1)S(1)} %collective-permute-done.16.refs_0_, bf16[64,2048]{1,0:T(8,128)(2,1)S(1)} %collective-permute-done.19.refs_1_, ...), custom_call_target="tpu_custom_call" | custom-call | flops 1000 | bytes 1000 | tf_op jit(solution)/shard_map/feed_forward/pallas_call | solution.py:286
  57.3 2.0 %collective-permute-start.24 = (bf16[64,2048]{1,0:T(8,128)(2,1)S(1)}, bf16[64,2048]{1,0:T(8,128)(2,1)S(1)}, u32[]{:S(2)}, u32[]{:S(2)}) collective-permute-start(bf16[64,2048]{1,0:T(8,128)(2,1)S(1)} %collective-permute-done.22.refs_2_), channel_id=1, source_target_pairs={{0,4},{1,5},{4,8},{5,9},{8,12},{9,13},{12,14},{13,15},{14,10},{15,... | collective-permute-start | bytes 786440 | tf_op jit(solution)/shard_map/ppermute | solution.py:52
  59.3 2.2 %collective-permute-done.17.refs_0_ = bf16[64,2048]{1,0:T(8,128)(2,1)S(1)} collective-permute-done((bf16[64,2048]{1,0:T(8,128)(2,1)S(1)}, bf16[64,2048]{1,0:T(8,128)(2,1)S(1)}, u32[]{:S(2)}, u32[]{:S(2)}) %collective-permute-start.17) | collective-permute-done | bytes 262176 | tf_op jit(solution)/shard_map/ppermute | solution.py:52
  61.6 1.4 %collective-permute-start.18 = (bf16[64,2048]{1,0:T(8,128)(2,1)S(1)}, bf16[64,2048]{1,0:T(8,128)(2,1)S(1)}, u32[]{:S(2)}, u32[]{:S(2)}) collective-permute-start(bf16[64,2048]{1,0:T(8,128)(2,1)S(1)} %collective-permute-done.17.refs_0_), channel_id=1, source_target_pairs={{0,4},{1,5},{4,8},{5,9},{8,12},{9,13},{12,14},{13,15},{14,10},{15,... | collective-permute-start | bytes 786440 | tf_op jit(solution)/shard_map/ppermute | solution.py:52
  63.6 4.9 %feed_forward.5 = (bf16[64,2048]{1,0:T(8,128)(2,1)S(1)}, bf16[64,2048]{1,0:T(8,128)(2,1)S(1)}, bf16[64,2048]{1,0:T(8,128)(2,1)S(1)}, bf16[64,2048]{1,0:T(8,128)(2,1)S(1)}) custom-call(bf16[64,2048]{1,0:T(8,128)(2,1)S(1)} %collective-permute-done.17.refs_0_, bf16[64,2048]{1,0:T(8,128)(2,1)S(1)} %collective-permute-done.20.refs_1_, ...), custom_call_target="tpu_custom_call" | custom-call | flops 1000 | bytes 1000 | tf_op jit(solution)/shard_map/feed_forward/pallas_call | solution.py:286
  68.5 3.0 %collective-permute-done.18.refs_0_ = bf16[64,2048]{1,0:T(8,128)(2,1)S(1)} collective-permute-done((bf16[64,2048]{1,0:T(8,128)(2,1)S(1)}, bf16[64,2048]{1,0:T(8,128)(2,1)S(1)}, u32[]{:S(2)}, u32[]{:S(2)}) %collective-permute-start.18) | collective-permute-done | bytes 262176 | tf_op jit(solution)/shard_map/ppermute | solution.py:52
  72.2 4.9 %feed_forward.7 = (bf16[64,2048]{1,0:T(8,128)(2,1)S(1)}, bf16[64,2048]{1,0:T(8,128)(2,1)S(1)}, bf16[64,2048]{1,0:T(8,128)(2,1)S(1)}, bf16[64,2048]{1,0:T(8,128)(2,1)S(1)}) custom-call(bf16[64,2048]{1,0:T(8,128)(2,1)S(1)} %collective-permute-done.18.refs_0_, bf16[64,2048]{1,0:T(8,128)(2,1)S(1)} %collective-permute-done.21.refs_1_, ...), custom_call_target="tpu_custom_call" | custom-call | flops 1000 | bytes 1000 | tf_op jit(solution)/shard_map/feed_forward/pallas_call | solution.py:286
  77.2 1.7 %collective-permute-start.26 = (bf16[64,2048]{1,0:T(8,128)(2,1)S(1)}, bf16[64,2048]{1,0:T(8,128)(2,1)S(1)}, u32[]{:S(2)}, u32[]{:S(2)}) collective-permute-start(bf16[64,2048]{1,0:T(8,128)(2,1)S(1)} %get-tuple-element.199), channel_id=1, source_target_pairs={{0,4},{1,5},{4,8},{5,9},{8,12},{9,13},{12,14},{13,15},{14,10},{15,... | collective-permute-start | bytes 786440 | tf_op jit(solution)/shard_map/ppermute | solution.py:52
  81.3 5.2 %collective-permute-done.26 = bf16[64,2048]{1,0:T(8,128)(2,1)S(1)} collective-permute-done((bf16[64,2048]{1,0:T(8,128)(2,1)S(1)}, bf16[64,2048]{1,0:T(8,128)(2,1)S(1)}, u32[]{:S(2)}, u32[]{:S(2)}) %collective-permute-start.26) | collective-permute-done | bytes 262176 | tf_op jit(solution)/shard_map/ppermute | solution.py:52
  86.5 1.7 %collective-permute-start.27 = (bf16[64,2048]{1,0:T(8,128)(2,1)S(1)}, bf16[64,2048]{1,0:T(8,128)(2,1)S(1)}, u32[]{:S(2)}, u32[]{:S(2)}) collective-permute-start(bf16[64,2048]{1,0:T(8,128)(2,1)S(1)} %add_convert_fusion.12), channel_id=1, source_target_pairs={{0,4},{1,5},{4,8},{5,9},{8,12},{9,13},{12,14},{13,15},{14,10},{15,... | collective-permute-start | bytes 786440 | tf_op jit(solution)/shard_map/ppermute | solution.py:52
  88.8 5.0 %collective-permute-done.33 = bf16[64,2048]{1,0:T(8,128)(2,1)S(1)} collective-permute-done((bf16[64,2048]{1,0:T(8,128)(2,1)S(1)}, bf16[64,2048]{1,0:T(8,128)(2,1)S(1)}, u32[]{:S(2)}, u32[]{:S(2)}) %collective-permute-start.33) | collective-permute-done | bytes 262176 | tf_op jit(solution)/shard_map/ppermute | solution.py:52
  94.3 1.7 %collective-permute-start.37 = (bf16[64,2048]{1,0:T(8,128)(2,1)S(1)}, bf16[64,2048]{1,0:T(8,128)(2,1)S(1)}, u32[]{:S(2)}, u32[]{:S(2)}) collective-permute-start(bf16[64,2048]{1,0:T(8,128)(2,1)S(1)} %add_convert_fusion.4), channel_id=1, source_target_pairs={{0,4},{1,5},{4,8},{5,9},{8,12},{9,13},{12,14},{13,15},{14,10},{15,... | collective-permute-start | bytes 786440 | tf_op jit(solution)/shard_map/ppermute | solution.py:52
  96.0 1.7 %collective-permute-done.27 = bf16[64,2048]{1,0:T(8,128)(2,1)S(1)} collective-permute-done((bf16[64,2048]{1,0:T(8,128)(2,1)S(1)}, bf16[64,2048]{1,0:T(8,128)(2,1)S(1)}, u32[]{:S(2)}, u32[]{:S(2)}) %collective-permute-start.27) | collective-permute-done | bytes 262176 | tf_op jit(solution)/shard_map/ppermute | solution.py:52
  100.0 5.0 %collective-permute-done.34 = bf16[64,2048]{1,0:T(8,128)(2,1)S(1)} collective-permute-done((bf16[64,2048]{1,0:T(8,128)(2,1)S(1)}, bf16[64,2048]{1,0:T(8,128)(2,1)S(1)}, u32[]{:S(2)}, u32[]{:S(2)}) %collective-permute-start.34) | collective-permute-done | bytes 262176 | tf_op jit(solution)/shard_map/ppermute | solution.py:52
  105.5 1.7 %collective-permute-start.38 = (bf16[64,2048]{1,0:T(8,128)(2,1)S(1)}, bf16[64,2048]{1,0:T(8,128)(2,1)S(1)}, u32[]{:S(2)}, u32[]{:S(2)}) collective-permute-start(bf16[64,2048]{1,0:T(8,128)(2,1)S(1)} %add_convert_fusion.3), channel_id=1, source_target_pairs={{0,4},{1,5},{4,8},{5,9},{8,12},{9,13},{12,14},{13,15},{14,10},{15,... | collective-permute-start | bytes 786440 | tf_op jit(solution)/shard_map/ppermute | solution.py:52
  107.3 3.3 %collective-permute-done.31 = bf16[64,2048]{1,0:T(8,128)(2,1)S(1)} collective-permute-done((bf16[64,2048]{1,0:T(8,128)(2,1)S(1)}, bf16[64,2048]{1,0:T(8,128)(2,1)S(1)}, u32[]{:S(2)}, u32[]{:S(2)}) %collective-permute-start.31) | collective-permute-done | bytes 262176 | tf_op jit(solution)/shard_map/ppermute | solution.py:52
  112.3 1.4 %collective-permute-start.39 = (bf16[64,2048]{1,0:T(8,128)(2,1)S(1)}, bf16[64,2048]{1,0:T(8,128)(2,1)S(1)}, u32[]{:S(2)}, u32[]{:S(2)}) collective-permute-start(bf16[64,2048]{1,0:T(8,128)(2,1)S(1)} %add_convert_fusion.2), channel_id=1, source_target_pairs={{0,4},{1,5},{4,8},{5,9},{8,12},{9,13},{12,14},{13,15},{14,10},{15,... | collective-permute-start | bytes 786440 | tf_op jit(solution)/shard_map/ppermute | solution.py:52
  113.7 5.6 %collective-permute-done.32 = bf16[64,2048]{1,0:T(8,128)(2,1)S(1)} collective-permute-done((bf16[64,2048]{1,0:T(8,128)(2,1)S(1)}, bf16[64,2048]{1,0:T(8,128)(2,1)S(1)}, u32[]{:S(2)}, u32[]{:S(2)}) %collective-permute-start.32) | collective-permute-done | bytes 262176 | tf_op jit(solution)/shard_map/ppermute | solution.py:52
  (78 shorter events, 26.8 us)
Async XLA Ops:
  2.7 21.5 %collective-permute-start.8 = (bf16[688,2048]{1,0:T(8,128)(2,1)}, bf16[688,2048]{1,0:T(8,128)(2,1)S(1)}, u32[]{:S(2)}, u32[]{:S(2)}) collective-permute-start(bf16[688,2048]{1,0:T(8,128)(2,1)} %bitcast.11), channel_id=1, source_target_pairs={{0,1},{1,0},{2,3},{3,2},{4,5},{5,4},{6,7},{7,6},{8,9},{9,8},{10,11... | collective-permute-start | bytes 8454152 | tf_op jit(solution)/shard_map/ppermute | solution.py:55
  2.9 21.3 %collective-permute-start.9 = (bf16[688,2048]{1,0:T(8,128)(2,1)}, bf16[688,2048]{1,0:T(8,128)(2,1)}, u32[]{:S(2)}, u32[]{:S(2)}) collective-permute-start(bf16[688,2048]{1,0:T(8,128)(2,1)} %bitcast.13), channel_id=1, source_target_pairs={{0,1},{1,0},{2,3},{3,2},{4,5},{5,4},{6,7},{7,6},{8,9},{9,8},{10,11... | collective-permute-start | bytes 8454152 | tf_op jit(solution)/shard_map/ppermute | solution.py:55
  3.3 9.5 %collective-permute-start.2 = (bf16[512,128]{1,0:T(8,128)(2,1)S(1)}, bf16[512,128]{1,0:T(8,128)(2,1)S(1)}, u32[]{:S(2)}, u32[]{:S(2)}) collective-permute-start(bf16[512,128]{1,0:T(8,128)(2,1)S(1)} %join.1.refs_0_), channel_id=1, source_target_pairs={{0,4},{1,3},{4,8},{5,1},{8,12},{9,5},{12,14},{13,9},{14,10},{15,13... | collective-permute-start | bytes 393224 | tf_op jit(solution)/shard_map/ppermute | solution.py:63
  6.0 7.3 %collective-permute-start.3 = (bf16[512,128]{1,0:T(8,128)(2,1)S(1)}, bf16[512,128]{1,0:T(8,128)(2,1)S(1)}, u32[]{:S(2)}, u32[]{:S(2)}) collective-permute-start(bf16[512,128]{1,0:T(8,128)(2,1)S(1)} %join.1.refs_0_), channel_id=1, source_target_pairs={{0,8},{1,7},{4,12},{5,3},{8,14},{9,1},{12,10},{13,5},{14,6},{15,9}... | collective-permute-start | bytes 393224 | tf_op jit(solution)/shard_map/ppermute | solution.py:63
  15.0 7.8 %collective-permute-start.6 = (bf16[512,128]{1,0:T(8,128)(2,1)S(1)}, bf16[512,128]{1,0:T(8,128)(2,1)S(1)}, u32[]{:S(2)}, u32[]{:S(2)}) collective-permute-start(bf16[512,128]{1,0:T(8,128)(2,1)S(1)} %collective-permute-done.2.refs_1_), channel_id=1, source_target_pairs={{0,1},{1,0},{2,3},{3,2},{4,5},{5,4},{6,7},{7,6},{8,9},{9,8},{10,11... | collective-permute-start | bytes 393224 | tf_op jit(solution)/shard_map/ppermute | solution.py:55
  15.0 7.8 %collective-permute-start.5 = (bf16[512,128]{1,0:T(8,128)(2,1)S(1)}, bf16[512,128]{1,0:T(8,128)(2,1)S(1)}, u32[]{:S(2)}, u32[]{:S(2)}) collective-permute-start(bf16[512,128]{1,0:T(8,128)(2,1)S(1)} %collective-permute-done.3.refs_2_), channel_id=1, source_target_pairs={{0,8},{1,7},{4,12},{5,3},{8,14},{9,1},{12,10},{13,5},{14,6},{15,9}... | collective-permute-start | bytes 393224 | tf_op jit(solution)/shard_map/ppermute | solution.py:63
  29.5 9.8 %collective-permute-start.12 = (bf16[64,2048]{1,0:T(8,128)(2,1)S(1)}, bf16[64,2048]{1,0:T(8,128)(2,1)S(1)}, u32[]{:S(2)}, u32[]{:S(2)}) collective-permute-start(bf16[64,2048]{1,0:T(8,128)(2,1)S(1)} %get-tuple-element.170.refs_2_), channel_id=1, source_target_pairs={{0,4},{1,5},{4,8},{5,9},{8,12},{9,13},{12,14},{13,15},{14,10},{15,... | collective-permute-start | bytes 786440 | tf_op jit(solution)/shard_map/ppermute | solution.py:52
  30.4 9.2 %collective-permute-start.13 = (bf16[64,2048]{1,0:T(8,128)(2,1)S(1)}, bf16[64,2048]{1,0:T(8,128)(2,1)S(1)}, u32[]{:S(2)}, u32[]{:S(2)}) collective-permute-start(bf16[64,2048]{1,0:T(8,128)(2,1)S(1)} %get-tuple-element.171.refs_3_), channel_id=1, source_target_pairs={{0,2},{1,3},{4,0},{5,1},{8,4},{9,5},{12,8},{13,9},{14,12},{15,13},... | collective-permute-start | bytes 786440 | tf_op jit(solution)/shard_map/ppermute | solution.py:52
  31.5 15.1 %collective-permute-start.14 = (bf16[64,2048]{1,0:T(8,128)(2,1)S(1)}, bf16[64,2048]{1,0:T(8,128)(2,1)S(1)}, u32[]{:S(2)}, u32[]{:S(2)}) collective-permute-start(bf16[64,2048]{1,0:T(8,128)(2,1)S(1)} %get-tuple-element.171.refs_3_), channel_id=1, source_target_pairs={{0,4},{1,5},{4,8},{5,9},{8,12},{9,13},{12,14},{13,15},{14,10},{15,... | collective-permute-start | bytes 786440 | tf_op jit(solution)/shard_map/ppermute | solution.py:52
  32.5 14.2 %collective-permute-start.15 = (bf16[64,2048]{1,0:T(8,128)(2,1)S(1)}, bf16[64,2048]{1,0:T(8,128)(2,1)S(1)}, u32[]{:S(2)}, u32[]{:S(2)}) collective-permute-start(bf16[64,2048]{1,0:T(8,128)(2,1)S(1)} %get-tuple-element.170.refs_2_), channel_id=1, source_target_pairs={{0,2},{1,3},{4,0},{5,1},{8,4},{9,5},{12,8},{13,9},{14,12},{15,13},... | collective-permute-start | bytes 786440 | tf_op jit(solution)/shard_map/ppermute | solution.py:52
  39.6 10.2 %collective-permute-start.16 = (bf16[64,2048]{1,0:T(8,128)(2,1)S(1)}, bf16[64,2048]{1,0:T(8,128)(2,1)S(1)}, u32[]{:S(2)}, u32[]{:S(2)}) collective-permute-start(bf16[64,2048]{1,0:T(8,128)(2,1)S(1)} %collective-permute-done.12.refs_0_), channel_id=1, source_target_pairs={{0,4},{1,5},{4,8},{5,9},{8,12},{9,13},{12,14},{13,15},{14,10},{15,... | collective-permute-start | bytes 786440 | tf_op jit(solution)/shard_map/ppermute | solution.py:52
  41.0 9.9 %collective-permute-start.19 = (bf16[64,2048]{1,0:T(8,128)(2,1)S(1)}, bf16[64,2048]{1,0:T(8,128)(2,1)S(1)}, u32[]{:S(2)}, u32[]{:S(2)}) collective-permute-start(bf16[64,2048]{1,0:T(8,128)(2,1)S(1)} %collective-permute-done.13.refs_1_), channel_id=1, source_target_pairs={{0,2},{1,3},{4,0},{5,1},{8,4},{9,5},{12,8},{13,9},{14,12},{15,13},... | collective-permute-start | bytes 786440 | tf_op jit(solution)/shard_map/ppermute | solution.py:52
  46.6 10.2 %collective-permute-start.22 = (bf16[64,2048]{1,0:T(8,128)(2,1)S(1)}, bf16[64,2048]{1,0:T(8,128)(2,1)S(1)}, u32[]{:S(2)}, u32[]{:S(2)}) collective-permute-start(bf16[64,2048]{1,0:T(8,128)(2,1)S(1)} %collective-permute-done.14.refs_2_), channel_id=1, source_target_pairs={{0,4},{1,5},{4,8},{5,9},{8,12},{9,13},{12,14},{13,15},{14,10},{15,... | collective-permute-start | bytes 786440 | tf_op jit(solution)/shard_map/ppermute | solution.py:52
  48.0 9.2 %collective-permute-start.23 = (bf16[64,2048]{1,0:T(8,128)(2,1)S(1)}, bf16[64,2048]{1,0:T(8,128)(2,1)S(1)}, u32[]{:S(2)}, u32[]{:S(2)}) collective-permute-start(bf16[64,2048]{1,0:T(8,128)(2,1)S(1)} %collective-permute-done.15.refs_3_), channel_id=1, source_target_pairs={{0,2},{1,3},{4,0},{5,1},{8,4},{9,5},{12,8},{13,9},{14,12},{15,13},... | collective-permute-start | bytes 786440 | tf_op jit(solution)/shard_map/ppermute | solution.py:52
  49.9 11.7 %collective-permute-start.17 = (bf16[64,2048]{1,0:T(8,128)(2,1)S(1)}, bf16[64,2048]{1,0:T(8,128)(2,1)S(1)}, u32[]{:S(2)}, u32[]{:S(2)}) collective-permute-start(bf16[64,2048]{1,0:T(8,128)(2,1)S(1)} %collective-permute-done.16.refs_0_), channel_id=1, source_target_pairs={{0,4},{1,5},{4,8},{5,9},{8,12},{9,13},{12,14},{13,15},{14,10},{15,... | collective-permute-start | bytes 786440 | tf_op jit(solution)/shard_map/ppermute | solution.py:52
  50.9 12.0 %collective-permute-start.20 = (bf16[64,2048]{1,0:T(8,128)(2,1)S(1)}, bf16[64,2048]{1,0:T(8,128)(2,1)S(1)}, u32[]{:S(2)}, u32[]{:S(2)}) collective-permute-start(bf16[64,2048]{1,0:T(8,128)(2,1)S(1)} %collective-permute-done.19.refs_1_), channel_id=1, source_target_pairs={{0,2},{1,3},{4,0},{5,1},{8,4},{9,5},{12,8},{13,9},{14,12},{15,13},... | collective-permute-start | bytes 786440 | tf_op jit(solution)/shard_map/ppermute | solution.py:52
  57.3 11.2 %collective-permute-start.24 = (bf16[64,2048]{1,0:T(8,128)(2,1)S(1)}, bf16[64,2048]{1,0:T(8,128)(2,1)S(1)}, u32[]{:S(2)}, u32[]{:S(2)}) collective-permute-start(bf16[64,2048]{1,0:T(8,128)(2,1)S(1)} %collective-permute-done.22.refs_2_), channel_id=1, source_target_pairs={{0,4},{1,5},{4,8},{5,9},{8,12},{9,13},{12,14},{13,15},{14,10},{15,... | collective-permute-start | bytes 786440 | tf_op jit(solution)/shard_map/ppermute | solution.py:52
  59.3 9.2 %collective-permute-start.25 = (bf16[64,2048]{1,0:T(8,128)(2,1)S(1)}, bf16[64,2048]{1,0:T(8,128)(2,1)S(1)}, u32[]{:S(2)}, u32[]{:S(2)}) collective-permute-start(bf16[64,2048]{1,0:T(8,128)(2,1)S(1)} %collective-permute-done.23.refs_3_), channel_id=1, source_target_pairs={{0,2},{1,3},{4,0},{5,1},{8,4},{9,5},{12,8},{13,9},{14,12},{15,13},... | collective-permute-start | bytes 786440 | tf_op jit(solution)/shard_map/ppermute | solution.py:52
  61.6 10.0 %collective-permute-start.18 = (bf16[64,2048]{1,0:T(8,128)(2,1)S(1)}, bf16[64,2048]{1,0:T(8,128)(2,1)S(1)}, u32[]{:S(2)}, u32[]{:S(2)}) collective-permute-start(bf16[64,2048]{1,0:T(8,128)(2,1)S(1)} %collective-permute-done.17.refs_0_), channel_id=1, source_target_pairs={{0,4},{1,5},{4,8},{5,9},{8,12},{9,13},{12,14},{13,15},{14,10},{15,... | collective-permute-start | bytes 786440 | tf_op jit(solution)/shard_map/ppermute | solution.py:52
  62.9 9.3 %collective-permute-start.21 = (bf16[64,2048]{1,0:T(8,128)(2,1)S(1)}, bf16[64,2048]{1,0:T(8,128)(2,1)S(1)}, u32[]{:S(2)}, u32[]{:S(2)}) collective-permute-start(bf16[64,2048]{1,0:T(8,128)(2,1)S(1)} %collective-permute-done.20.refs_1_), channel_id=1, source_target_pairs={{0,2},{1,3},{4,0},{5,1},{8,4},{9,5},{12,8},{13,9},{14,12},{15,13},... | collective-permute-start | bytes 786440 | tf_op jit(solution)/shard_map/ppermute | solution.py:52
  77.2 9.3 %collective-permute-start.26 = (bf16[64,2048]{1,0:T(8,128)(2,1)S(1)}, bf16[64,2048]{1,0:T(8,128)(2,1)S(1)}, u32[]{:S(2)}, u32[]{:S(2)}) collective-permute-start(bf16[64,2048]{1,0:T(8,128)(2,1)S(1)} %get-tuple-element.199), channel_id=1, source_target_pairs={{0,4},{1,5},{4,8},{5,9},{8,12},{9,13},{12,14},{13,15},{14,10},{15,... | collective-permute-start | bytes 786440 | tf_op jit(solution)/shard_map/ppermute | solution.py:52
  78.9 9.4 %collective-permute-start.29 = (bf16[64,2048]{1,0:T(8,128)(2,1)S(1)}, bf16[64,2048]{1,0:T(8,128)(2,1)S(1)}, u32[]{:S(2)}, u32[]{:S(2)}) collective-permute-start(bf16[64,2048]{1,0:T(8,128)(2,1)S(1)} %get-tuple-element.202), channel_id=1, source_target_pairs={{0,2},{1,3},{4,0},{5,1},{8,4},{9,5},{12,8},{13,9},{14,12},{15,13},... | collective-permute-start | bytes 786440 | tf_op jit(solution)/shard_map/ppermute | solution.py:52
  79.3 14.5 %collective-permute-start.33 = (bf16[64,2048]{1,0:T(8,128)(2,1)S(1)}, bf16[64,2048]{1,0:T(8,128)(2,1)S(1)}, u32[]{:S(2)}, u32[]{:S(2)}) collective-permute-start(bf16[64,2048]{1,0:T(8,128)(2,1)S(1)} %get-tuple-element.207), channel_id=1, source_target_pairs={{0,2},{1,3},{4,0},{5,1},{8,4},{9,5},{12,8},{13,9},{14,12},{15,13},... | collective-permute-start | bytes 786440 | tf_op jit(solution)/shard_map/ppermute | solution.py:52
  80.3 13.9 %collective-permute-start.36 = (bf16[64,2048]{1,0:T(8,128)(2,1)S(1)}, bf16[64,2048]{1,0:T(8,128)(2,1)S(1)}, u32[]{:S(2)}, u32[]{:S(2)}) collective-permute-start(bf16[64,2048]{1,0:T(8,128)(2,1)S(1)} %get-tuple-element.210), channel_id=1, source_target_pairs={{0,4},{1,5},{4,8},{5,9},{8,12},{9,13},{12,14},{13,15},{14,10},{15,... | collective-permute-start | bytes 786440 | tf_op jit(solution)/shard_map/ppermute | solution.py:52
  86.5 11.2 %collective-permute-start.27 = (bf16[64,2048]{1,0:T(8,128)(2,1)S(1)}, bf16[64,2048]{1,0:T(8,128)(2,1)S(1)}, u32[]{:S(2)}, u32[]{:S(2)}) collective-permute-start(bf16[64,2048]{1,0:T(8,128)(2,1)S(1)} %add_convert_fusion.12), channel_id=1, source_target_pairs={{0,4},{1,5},{4,8},{5,9},{8,12},{9,13},{12,14},{13,15},{14,10},{15,... | collective-permute-start | bytes 786440 | tf_op jit(solution)/shard_map/ppermute | solution.py:52
  88.3 11.0 %collective-permute-start.30 = (bf16[64,2048]{1,0:T(8,128)(2,1)S(1)}, bf16[64,2048]{1,0:T(8,128)(2,1)S(1)}, u32[]{:S(2)}, u32[]{:S(2)}) collective-permute-start(bf16[64,2048]{1,0:T(8,128)(2,1)S(1)} %add_convert_fusion.10), channel_id=1, source_target_pairs={{0,2},{1,3},{4,0},{5,1},{8,4},{9,5},{12,8},{13,9},{14,12},{15,13},... | collective-permute-start | bytes 786440 | tf_op jit(solution)/shard_map/ppermute | solution.py:52
  93.8 11.2 %collective-permute-start.34 = (bf16[64,2048]{1,0:T(8,128)(2,1)S(1)}, bf16[64,2048]{1,0:T(8,128)(2,1)S(1)}, u32[]{:S(2)}, u32[]{:S(2)}) collective-permute-start(bf16[64,2048]{1,0:T(8,128)(2,1)S(1)} %add_convert_fusion.6), channel_id=1, source_target_pairs={{0,2},{1,3},{4,0},{5,1},{8,4},{9,5},{12,8},{13,9},{14,12},{15,13},... | collective-permute-start | bytes 786440 | tf_op jit(solution)/shard_map/ppermute | solution.py:52
  94.3 11.2 %collective-permute-start.37 = (bf16[64,2048]{1,0:T(8,128)(2,1)S(1)}, bf16[64,2048]{1,0:T(8,128)(2,1)S(1)}, u32[]{:S(2)}, u32[]{:S(2)}) collective-permute-start(bf16[64,2048]{1,0:T(8,128)(2,1)S(1)} %add_convert_fusion.4), channel_id=1, source_target_pairs={{0,4},{1,5},{4,8},{5,9},{8,12},{9,13},{12,14},{13,15},{14,10},{15,... | collective-permute-start | bytes 786440 | tf_op jit(solution)/shard_map/ppermute | solution.py:52
  97.8 16.0 %collective-permute-start.28 = (bf16[64,2048]{1,0:T(8,128)(2,1)S(1)}, bf16[64,2048]{1,0:T(8,128)(2,1)S(1)}, u32[]{:S(2)}, u32[]{:S(2)}) collective-permute-start(bf16[64,2048]{1,0:T(8,128)(2,1)S(1)} %add_convert_fusion.11), channel_id=1, source_target_pairs={{0,4},{1,5},{4,8},{5,9},{8,12},{9,13},{12,14},{13,15},{14,10},{15,... | collective-permute-start | bytes 786440 | tf_op jit(solution)/shard_map/ppermute | solution.py:52
  99.4 11.2 %collective-permute-start.31 = (bf16[64,2048]{1,0:T(8,128)(2,1)S(1)}, bf16[64,2048]{1,0:T(8,128)(2,1)S(1)}, u32[]{:S(2)}, u32[]{:S(2)}) collective-permute-start(bf16[64,2048]{1,0:T(8,128)(2,1)S(1)} %add_convert_fusion.9), channel_id=1, source_target_pairs={{0,2},{1,3},{4,0},{5,1},{8,4},{9,5},{12,8},{13,9},{14,12},{15,13},... | collective-permute-start | bytes 786440 | tf_op jit(solution)/shard_map/ppermute | solution.py:52
  105.0 14.4 %collective-permute-start.35 = (bf16[64,2048]{1,0:T(8,128)(2,1)S(1)}, bf16[64,2048]{1,0:T(8,128)(2,1)S(1)}, u32[]{:S(2)}, u32[]{:S(2)}) collective-permute-start(bf16[64,2048]{1,0:T(8,128)(2,1)S(1)} %add_convert_fusion.5), channel_id=1, source_target_pairs={{0,2},{1,3},{4,0},{5,1},{8,4},{9,5},{12,8},{13,9},{14,12},{15,13},... | collective-permute-start | bytes 786440 | tf_op jit(solution)/shard_map/ppermute | solution.py:52
  110.7 8.7 %collective-permute-start.32 = (bf16[64,2048]{1,0:T(8,128)(2,1)S(1)}, bf16[64,2048]{1,0:T(8,128)(2,1)S(1)}, u32[]{:S(2)}, u32[]{:S(2)}) collective-permute-start(bf16[64,2048]{1,0:T(8,128)(2,1)S(1)} %add_convert_fusion.8), channel_id=1, source_target_pairs={{0,2},{1,3},{4,0},{5,1},{8,4},{9,5},{12,8},{13,9},{14,12},{15,13},... | collective-permute-start | bytes 786440 | tf_op jit(solution)/shard_map/ppermute | solution.py:52
  (11 other events, 96.7 us)

commit v2 on v1

--- a/solution.py
+++ b/solution.py
@@ -347,6 +347,15 @@
     return [sum(x[k] for x in sums) for k in range(2)]
 
 
+def kv_phases(half):
+    if half < 4:
+        return [[(hops, 0) for hops in range(1, half + 1)]]
+    phases = [[(1, 0), (3, 0)], [(2, 1), (4, 3)]]
+    for hops in range(5, half + 1, 2):
+        phases.append([(k, k - 2) for k in (hops, hops + 1) if k <= half])
+    return phases
+
+
 def gather_kv(ring, keys, values, weights, extras):
     half = ring.half
     gate, up, down = weights
@@ -356,16 +365,12 @@
     gate, up, both = lax.optimization_barrier((gate, up, both))
     gate_mate, up_mate = ring.go_mate(gate), ring.go_mate(up)
     held, mates = {0: both}, {}
-    reach = 0
-    while reach < half:
-        fresh = range(reach + 1, min(reach + 2, half) + 1)
-        for hops in fresh:
-            jump = min(2, hops)
-            held[hops] = ring.go_split(held[hops - jump], jump)
-        for hops in range(max(1, reach - 1), reach + 1):
-            mates[hops] = ring.go_mate(held[hops])
+    for phase in kv_phases(half):
+        for block in [b for b in held if 0 < b and b not in mates]:
+            mates[block] = ring.go_mate(held[block])
+        for hops, source in phase:
+            held[hops] = ring.go_split(held[source], hops - source)
         held, mates, extras = lax.optimization_barrier((held, mates, extras))
-        reach = fresh[-1]
     for hops in range(1, half):
         if hops not in mates:
             mates[hops] = ring.go_mate(held[hops])

time: 121 us -> 119 us (0.983)
  waiting for transfers between devices: 47.1 us -> 45.5 us
    ppermute x28, waiting for transfers between devices: 35.4 us -> 33.7 us  [go(): return lax.ppermute(block, 'ctx', pairs)]
  transfers between devices with their start and end apart: 40 -> 40, of which waited for: 21 -> 19; matrix products, arithmetic and copies ran while one was open for 2% -> 2% of each run, Pallas kernels for 22% -> 22%
where the time goes in v2:
time: 119 us
  waiting for transfers between devices  45.5 us (38%)
  starting transfers between devices  37.5 us (32%)
  Pallas kernels  32.1 us (27%)
  other arithmetic  2.63 us (2%)
    ppermute x28, waiting for transfers between devices, go(): return lax.ppermute(block, 'ctx', pairs)  33.7 us
    ppermute x28, starting transfers between devices, go(): return lax.ppermute(block, 'ctx', pairs)  28.8 us
    pallas_call x4, Pallas kernels, ffn(): pl.pallas_call(functools.partial(ffn_kernel, count), out_shape=tuple((jax...  19.8 us
    pallas_call x3, Pallas kernels, load(): pl.pallas_call(functools.partial(load_kernel, count), out_shape=tuple((pl...  8.43 us
    ppermute x4, waiting for transfers between devices, go_split(): return lax.ppermute(block, 'ctx', pairs)  7.25 us
    ppermute x4, starting transfers between devices, go_split(): return lax.ppermute(block, 'ctx', pairs)  7.12 us
    ppermute x8, waiting for transfers between devices, go_mate(): return lax.ppermute(block, 'ctx', self.swap)  4.53 us
    pallas_call x1, Pallas kernels, attend(): pl.pallas_call(functools.partial(attention_kernel, len(blocks), heads, he...  3.12 us
  transfers between devices with their start and end apart: 40, of which 19 were waited for; matrix products, arithmetic and copies ran while one was open for 2% of the time, Pallas kernels for 22%

profile of v2, /device:TPU:0, one launch (start us, length us, event | category | flops | bytes accessed | tf_op | source)
XLA Modules:
  0.0 118.7 jit_solution(15078006724479558550)
XLA Ops:
  3.3 2.7 %collective-permute-start.2 = (bf16[512,128]{1,0:T(8,128)(2,1)S(1)}, bf16[512,128]{1,0:T(8,128)(2,1)S(1)}, u32[]{:S(2)}, u32[]{:S(2)}) collective-permute-start(bf16[512,128]{1,0:T(8,128)(2,1)S(1)} %join.1.refs_0_), channel_id=1, source_target_pairs={{0,4},{1,3},{4,8},{5,1},{8,12},{9,5},{12,14},{13,9},{14,10},{15,13... | collective-permute-start | bytes 393224 | tf_op jit(solution)/shard_map/ppermute | solution.py:63
  6.0 3.5 %collective-permute-start.3 = (bf16[512,128]{1,0:T(8,128)(2,1)S(1)}, bf16[512,128]{1,0:T(8,128)(2,1)S(1)}, u32[]{:S(2)}, u32[]{:S(2)}) collective-permute-start(bf16[512,128]{1,0:T(8,128)(2,1)S(1)} %join.1.refs_0_), channel_id=1, source_target_pairs={{0,12},{1,11},{4,14},{5,7},{8,10},{9,3},{12,6},{13,1},{14,2},{15,5... | collective-permute-start | bytes 393224 | tf_op jit(solution)/shard_map/ppermute | solution.py:63
  10.3 2.7 %load.3 = (bf16[128,1024]{1,0:T(8,128)(2,1)S(1)}, s32[16,128]{1,0:T(8,128)S(1)}, s32[16,128]{1,0:T(8,128)S(1)}, bf16[128,2048]{1,0:T(8,128)(2,1)S(1)}, f32[1,204...) custom-call(bf16[128,1024]{1,0:T(8,128)(2,1)} %refs_0_.3, s32[16,128]{1,0:T(8,128)} %bitcast.7, s32[16,128]{1,0:T(8,128)} %bitcast.9, ...), custom_call_target="tpu_custom_call" | custom-call | tf_op jit(solution)/shard_map/load/pallas_call | solution.py:221
  13.7 1.9 %collective-permute-done.3.refs_3_ = bf16[512,128]{1,0:T(8,128)(2,1)S(1)} collective-permute-done((bf16[512,128]{1,0:T(8,128)(2,1)S(1)}, bf16[512,128]{1,0:T(8,128)(2,1)S(1)}, u32[]{:S(2)}, u32[]{:S(2)}) %collective-permute-start.3) | collective-permute-done | bytes 131104 | tf_op jit(solution)/shard_map/ppermute | solution.py:63
  16.6 4.0 %collective-permute-done.4.refs_2_ = bf16[512,128]{1,0:T(8,128)(2,1)S(1)} collective-permute-done((bf16[512,128]{1,0:T(8,128)(2,1)S(1)}, bf16[512,128]{1,0:T(8,128)(2,1)S(1)}, u32[]{:S(2)}, u32[]{:S(2)}) %collective-permute-start.4) | collective-permute-done | bytes 131104 | tf_op jit(solution)/shard_map/ppermute | solution.py:63
  23.5 3.1 %attention.1 = (bf16[64,2048]{1,0:T(8,128)(2,1)S(1)}, bf16[64,2048]{1,0:T(8,128)(2,1)S(1)}, bf16[128,2048]{1,0:T(8,128)(2,1)S(1)}) custom-call(s32[16]{0:T(128)S(1)} %dynamic-slice_bitcast_fusion.owner_ref, s32[16,128]{1,0:T(8,128)S(1)} %bitcast.8, s32[16,128]{1,0:T(8,128)S(1)} %bitcast.10, bf16[128,1024]{1,0:T(8,128)(2,1)S(1)} %get-tuple-element.129.query_ref, ...), custom_call_target="tpu_custom_call" | custom-call | tf_op jit(solution)/shard_map/attention/pallas_call | solution.py:192
  26.7 1.9 %collective-permute-done.11.refs_2_ = bf16[688,2048]{1,0:T(8,128)(2,1)S(1)} collective-permute-done((bf16[688,2048]{1,0:T(8,128)(2,1)S(1)}, bf16[688,2048]{1,0:T(8,128)(2,1)S(1)}, u32[]{:S(2)}, u32[]{:S(2)}) %collective-permute-start.11) | collective-permute-done | bytes 2818080 | tf_op jit(solution)/shard_map/ppermute | solution.py:55
  28.6 2.0 %collective-permute-start.13 = (bf16[64,2048]{1,0:T(8,128)(2,1)S(1)}, bf16[64,2048]{1,0:T(8,128)(2,1)S(1)}, u32[]{:S(2)}, u32[]{:S(2)}) collective-permute-start(bf16[64,2048]{1,0:T(8,128)(2,1)S(1)} %get-tuple-element.171.refs_3_), channel_id=1, source_target_pairs={{0,2},{1,3},{4,0},{5,1},{8,4},{9,5},{12,8},{13,9},{14,12},{15,13},... | collective-permute-start | bytes 786440 | tf_op jit(solution)/shard_map/ppermute | solution.py:52
  30.6 2.0 %collective-permute-start.15 = (bf16[64,2048]{1,0:T(8,128)(2,1)S(1)}, bf16[64,2048]{1,0:T(8,128)(2,1)S(1)}, u32[]{:S(2)}, u32[]{:S(2)}) collective-permute-start(bf16[64,2048]{1,0:T(8,128)(2,1)S(1)} %get-tuple-element.170.refs_2_), channel_id=1, source_target_pairs={{0,2},{1,3},{4,0},{5,1},{8,4},{9,5},{12,8},{13,9},{14,12},{15,13},... | collective-permute-start | bytes 786440 | tf_op jit(solution)/shard_map/ppermute | solution.py:52
  32.6 2.2 %load.5 = (bf16[688,2048]{1,0:T(8,128)(2,1)S(1)}, bf16[688,2048]{1,0:T(8,128)(2,1)S(1)}, bf16[688,2048]{1,0:T(8,128)(2,1)S(1)}) custom-call(bf16[688,2048]{1,0:T(8,128)(2,1)S(1)} %collective-permute-done.8.refs_0_, bf16[688,2048]{1,0:T(8,128)(2,1)} %collective-permute-done.9.refs_1_, bf16[688,2048]{1,0:T(8,128)(2,1)S(1)} %collective-permute-done.11.refs_2_), custom_call_target="tpu_custom_call" | custom-call | tf_op jit(solution)/shard_map/load/pallas_call | solution.py:221
  34.9 3.5 %load.4 = (bf16[688,2048]{1,0:T(8,128)(2,1)S(1)}, bf16[688,2048]{1,0:T(8,128)(2,1)S(1)}, bf16[688,2048]{1,0:T(8,128)(2,1)S(1)}) custom-call(bf16[688,2048]{1,0:T(8,128)(2,1)} %bitcast.12, bf16[688,2048]{1,0:T(8,128)(2,1)} %bitcast.14, bf16[688,2048]{1,0:T(8,128)(2,1)} %refs_2_), custom_call_target="tpu_custom_call" | custom-call | tf_op jit(solution)/shard_map/load/pallas_call | solution.py:221
  40.5 4.9 %feed_forward.4 = (bf16[64,2048]{1,0:T(8,128)(2,1)S(1)}, bf16[64,2048]{1,0:T(8,128)(2,1)S(1)}, bf16[64,2048]{1,0:T(8,128)(2,1)S(1)}, bf16[64,2048]{1,0:T(8,128)(2,1)S(1)}) custom-call(bf16[64,2048]{1,0:T(8,128)(2,1)S(1)} %collective-permute-done.12.refs_0_, bf16[64,2048]{1,0:T(8,128)(2,1)S(1)} %collective-permute-done.13.refs_1_, ...), custom_call_target="tpu_custom_call" | custom-call | flops 1000 | bytes 1000 | tf_op jit(solution)/shard_map/feed_forward/pallas_call | solution.py:286
  49.0 2.1 %collective-permute-start.20 = (bf16[64,2048]{1,0:T(8,128)(2,1)S(1)}, bf16[64,2048]{1,0:T(8,128)(2,1)S(1)}, u32[]{:S(2)}, u32[]{:S(2)}) collective-permute-start(bf16[64,2048]{1,0:T(8,128)(2,1)S(1)} %collective-permute-done.19.refs_1_), channel_id=1, source_target_pairs={{0,2},{1,3},{4,0},{5,1},{8,4},{9,5},{12,8},{13,9},{14,12},{15,13},... | collective-permute-start | bytes 786440 | tf_op jit(solution)/shard_map/ppermute | solution.py:52
  51.0 4.9 %feed_forward.6 = (bf16[64,2048]{1,0:T(8,128)(2,1)S(1)}, bf16[64,2048]{1,0:T(8,128)(2,1)S(1)}, bf16[64,2048]{1,0:T(8,128)(2,1)S(1)}, bf16[64,2048]{1,0:T(8,128)(2,1)S(1)}) custom-call(bf16[64,2048]{1,0:T(8,128)(2,1)S(1)} %collective-permute-done.16.refs_0_, bf16[64,2048]{1,0:T(8,128)(2,1)S(1)} %collective-permute-done.19.refs_1_, ...), custom_call_target="tpu_custom_call" | custom-call | flops 1000 | bytes 1000 | tf_op jit(solution)/shard_map/feed_forward/pallas_call | solution.py:286
  56.0 1.8 %collective-permute-start.24 = (bf16[64,2048]{1,0:T(8,128)(2,1)S(1)}, bf16[64,2048]{1,0:T(8,128)(2,1)S(1)}, u32[]{:S(2)}, u32[]{:S(2)}) collective-permute-start(bf16[64,2048]{1,0:T(8,128)(2,1)S(1)} %collective-permute-done.22.refs_2_), channel_id=1, source_target_pairs={{0,4},{1,5},{4,8},{5,9},{8,12},{9,13},{12,14},{13,15},{14,10},{15,... | collective-permute-start | bytes 786440 | tf_op jit(solution)/shard_map/ppermute | solution.py:52
  58.1 2.3 %collective-permute-done.17.refs_0_ = bf16[64,2048]{1,0:T(8,128)(2,1)S(1)} collective-permute-done((bf16[64,2048]{1,0:T(8,128)(2,1)S(1)}, bf16[64,2048]{1,0:T(8,128)(2,1)S(1)}, u32[]{:S(2)}, u32[]{:S(2)}) %collective-permute-start.17) | collective-permute-done | bytes 262176 | tf_op jit(solution)/shard_map/ppermute | solution.py:52
  62.4 4.9 %feed_forward.5 = (bf16[64,2048]{1,0:T(8,128)(2,1)S(1)}, bf16[64,2048]{1,0:T(8,128)(2,1)S(1)}, bf16[64,2048]{1,0:T(8,128)(2,1)S(1)}, bf16[64,2048]{1,0:T(8,128)(2,1)S(1)}) custom-call(bf16[64,2048]{1,0:T(8,128)(2,1)S(1)} %collective-permute-done.17.refs_0_, bf16[64,2048]{1,0:T(8,128)(2,1)S(1)} %collective-permute-done.20.refs_1_, ...), custom_call_target="tpu_custom_call" | custom-call | flops 1000 | bytes 1000 | tf_op jit(solution)/shard_map/feed_forward/pallas_call | solution.py:286
  67.4 3.3 %collective-permute-done.18.refs_0_ = bf16[64,2048]{1,0:T(8,128)(2,1)S(1)} collective-permute-done((bf16[64,2048]{1,0:T(8,128)(2,1)S(1)}, bf16[64,2048]{1,0:T(8,128)(2,1)S(1)}, u32[]{:S(2)}, u32[]{:S(2)}) %collective-permute-start.18) | collective-permute-done | bytes 262176 | tf_op jit(solution)/shard_map/ppermute | solution.py:52
  70.7 4.9 %feed_forward.7 = (bf16[64,2048]{1,0:T(8,128)(2,1)S(1)}, bf16[64,2048]{1,0:T(8,128)(2,1)S(1)}, bf16[64,2048]{1,0:T(8,128)(2,1)S(1)}, bf16[64,2048]{1,0:T(8,128)(2,1)S(1)}) custom-call(bf16[64,2048]{1,0:T(8,128)(2,1)S(1)} %collective-permute-done.18.refs_0_, bf16[64,2048]{1,0:T(8,128)(2,1)S(1)} %collective-permute-done.21.refs_1_, ...), custom_call_target="tpu_custom_call" | custom-call | flops 1000 | bytes 1000 | tf_op jit(solution)/shard_map/feed_forward/pallas_call | solution.py:286
  75.7 1.8 %collective-permute-start.26 = (bf16[64,2048]{1,0:T(8,128)(2,1)S(1)}, bf16[64,2048]{1,0:T(8,128)(2,1)S(1)}, u32[]{:S(2)}, u32[]{:S(2)}) collective-permute-start(bf16[64,2048]{1,0:T(8,128)(2,1)S(1)} %get-tuple-element.199), channel_id=1, source_target_pairs={{0,4},{1,5},{4,8},{5,9},{8,12},{9,13},{12,14},{13,15},{14,10},{15,... | collective-permute-start | bytes 786440 | tf_op jit(solution)/shard_map/ppermute | solution.py:52
  77.8 1.6 %collective-permute-start.33 = (bf16[64,2048]{1,0:T(8,128)(2,1)S(1)}, bf16[64,2048]{1,0:T(8,128)(2,1)S(1)}, u32[]{:S(2)}, u32[]{:S(2)}) collective-permute-start(bf16[64,2048]{1,0:T(8,128)(2,1)S(1)} %get-tuple-element.207), channel_id=1, source_target_pairs={{0,2},{1,3},{4,0},{5,1},{8,4},{9,5},{12,8},{13,9},{14,12},{15,13},... | collective-permute-start | bytes 786440 | tf_op jit(solution)/shard_map/ppermute | solution.py:52
  79.8 5.2 %collective-permute-done.26 = bf16[64,2048]{1,0:T(8,128)(2,1)S(1)} collective-permute-done((bf16[64,2048]{1,0:T(8,128)(2,1)S(1)}, bf16[64,2048]{1,0:T(8,128)(2,1)S(1)}, u32[]{:S(2)}, u32[]{:S(2)}) %collective-permute-start.26) | collective-permute-done | bytes 262176 | tf_op jit(solution)/shard_map/ppermute | solution.py:52
  85.1 1.8 %collective-permute-start.27 = (bf16[64,2048]{1,0:T(8,128)(2,1)S(1)}, bf16[64,2048]{1,0:T(8,128)(2,1)S(1)}, u32[]{:S(2)}, u32[]{:S(2)}) collective-permute-start(bf16[64,2048]{1,0:T(8,128)(2,1)S(1)} %add_convert_fusion.12), channel_id=1, source_target_pairs={{0,4},{1,5},{4,8},{5,9},{8,12},{9,13},{12,14},{13,15},{14,10},{15,... | collective-permute-start | bytes 786440 | tf_op jit(solution)/shard_map/ppermute | solution.py:52
  87.3 5.1 %collective-permute-done.33 = bf16[64,2048]{1,0:T(8,128)(2,1)S(1)} collective-permute-done((bf16[64,2048]{1,0:T(8,128)(2,1)S(1)}, bf16[64,2048]{1,0:T(8,128)(2,1)S(1)}, u32[]{:S(2)}, u32[]{:S(2)}) %collective-permute-start.33) | collective-permute-done | bytes 262176 | tf_op jit(solution)/shard_map/ppermute | solution.py:52
  92.8 1.8 %collective-permute-start.37 = (bf16[64,2048]{1,0:T(8,128)(2,1)S(1)}, bf16[64,2048]{1,0:T(8,128)(2,1)S(1)}, u32[]{:S(2)}, u32[]{:S(2)}) collective-permute-start(bf16[64,2048]{1,0:T(8,128)(2,1)S(1)} %add_convert_fusion.4), channel_id=1, source_target_pairs={{0,4},{1,5},{4,8},{5,9},{8,12},{9,13},{12,14},{13,15},{14,10},{15,... | collective-permute-start | bytes 786440 | tf_op jit(solution)/shard_map/ppermute | solution.py:52
  94.6 1.6 %collective-permute-done.27 = bf16[64,2048]{1,0:T(8,128)(2,1)S(1)} collective-permute-done((bf16[64,2048]{1,0:T(8,128)(2,1)S(1)}, bf16[64,2048]{1,0:T(8,128)(2,1)S(1)}, u32[]{:S(2)}, u32[]{:S(2)}) %collective-permute-start.27) | collective-permute-done | bytes 262176 | tf_op jit(solution)/shard_map/ppermute | solution.py:52
  96.3 1.8 %collective-permute-start.28 = (bf16[64,2048]{1,0:T(8,128)(2,1)S(1)}, bf16[64,2048]{1,0:T(8,128)(2,1)S(1)}, u32[]{:S(2)}, u32[]{:S(2)}) collective-permute-start(bf16[64,2048]{1,0:T(8,128)(2,1)S(1)} %add_convert_fusion.11), channel_id=1, source_target_pairs={{0,4},{1,5},{4,8},{5,9},{8,12},{9,13},{12,14},{13,15},{14,10},{15,... | collective-permute-start | bytes 786440 | tf_op jit(solution)/shard_map/ppermute | solution.py:52
  98.5 5.1 %collective-permute-done.34 = bf16[64,2048]{1,0:T(8,128)(2,1)S(1)} collective-permute-done((bf16[64,2048]{1,0:T(8,128)(2,1)S(1)}, bf16[64,2048]{1,0:T(8,128)(2,1)S(1)}, u32[]{:S(2)}, u32[]{:S(2)}) %collective-permute-start.34) | collective-permute-done | bytes 262176 | tf_op jit(solution)/shard_map/ppermute | solution.py:52
  104.1 1.8 %collective-permute-start.38 = (bf16[64,2048]{1,0:T(8,128)(2,1)S(1)}, bf16[64,2048]{1,0:T(8,128)(2,1)S(1)}, u32[]{:S(2)}, u32[]{:S(2)}) collective-permute-start(bf16[64,2048]{1,0:T(8,128)(2,1)S(1)} %add_convert_fusion.3), channel_id=1, source_target_pairs={{0,4},{1,5},{4,8},{5,9},{8,12},{9,13},{12,14},{13,15},{14,10},{15,... | collective-permute-start | bytes 786440 | tf_op jit(solution)/shard_map/ppermute | solution.py:52
  105.9 3.3 %collective-permute-done.31 = bf16[64,2048]{1,0:T(8,128)(2,1)S(1)} collective-permute-done((bf16[64,2048]{1,0:T(8,128)(2,1)S(1)}, bf16[64,2048]{1,0:T(8,128)(2,1)S(1)}, u32[]{:S(2)}, u32[]{:S(2)}) %collective-permute-start.31) | collective-permute-done | bytes 262176 | tf_op jit(solution)/shard_map/ppermute | solution.py:52
  111.1 1.5 %collective-permute-start.39 = (bf16[64,2048]{1,0:T(8,128)(2,1)S(1)}, bf16[64,2048]{1,0:T(8,128)(2,1)S(1)}, u32[]{:S(2)}, u32[]{:S(2)}) collective-permute-start(bf16[64,2048]{1,0:T(8,128)(2,1)S(1)} %add_convert_fusion.2), channel_id=1, source_target_pairs={{0,4},{1,5},{4,8},{5,9},{8,12},{9,13},{12,14},{13,15},{14,10},{15,... | collective-permute-start | bytes 786440 | tf_op jit(solution)/shard_map/ppermute | solution.py:52
  112.6 4.5 %collective-permute-done.32 = bf16[64,2048]{1,0:T(8,128)(2,1)S(1)} collective-permute-done((bf16[64,2048]{1,0:T(8,128)(2,1)S(1)}, bf16[64,2048]{1,0:T(8,128)(2,1)S(1)}, u32[]{:S(2)}, u32[]{:S(2)}) %collective-permute-start.32) | collective-permute-done | bytes 262176 | tf_op jit(solution)/shard_map/ppermute | solution.py:52
  (78 shorter events, 22.7 us)
Async XLA Ops:
  2.7 20.6 %collective-permute-start.8 = (bf16[688,2048]{1,0:T(8,128)(2,1)}, bf16[688,2048]{1,0:T(8,128)(2,1)S(1)}, u32[]{:S(2)}, u32[]{:S(2)}) collective-permute-start(bf16[688,2048]{1,0:T(8,128)(2,1)} %bitcast.11), channel_id=1, source_target_pairs={{0,1},{1,0},{2,3},{3,2},{4,5},{5,4},{6,7},{7,6},{8,9},{9,8},{10,11... | collective-permute-start | bytes 8454152 | tf_op jit(solution)/shard_map/ppermute | solution.py:55
  2.9 20.4 %collective-permute-start.9 = (bf16[688,2048]{1,0:T(8,128)(2,1)}, bf16[688,2048]{1,0:T(8,128)(2,1)}, u32[]{:S(2)}, u32[]{:S(2)}) collective-permute-start(bf16[688,2048]{1,0:T(8,128)(2,1)} %bitcast.13), channel_id=1, source_target_pairs={{0,1},{1,0},{2,3},{3,2},{4,5},{5,4},{6,7},{7,6},{8,9},{9,8},{10,11... | collective-permute-start | bytes 8454152 | tf_op jit(solution)/shard_map/ppermute | solution.py:55
  3.3 10.4 %collective-permute-start.2 = (bf16[512,128]{1,0:T(8,128)(2,1)S(1)}, bf16[512,128]{1,0:T(8,128)(2,1)S(1)}, u32[]{:S(2)}, u32[]{:S(2)}) collective-permute-start(bf16[512,128]{1,0:T(8,128)(2,1)S(1)} %join.1.refs_0_), channel_id=1, source_target_pairs={{0,4},{1,3},{4,8},{5,1},{8,12},{9,5},{12,14},{13,9},{14,10},{15,13... | collective-permute-start | bytes 393224 | tf_op jit(solution)/shard_map/ppermute | solution.py:63
  6.0 9.6 %collective-permute-start.3 = (bf16[512,128]{1,0:T(8,128)(2,1)S(1)}, bf16[512,128]{1,0:T(8,128)(2,1)S(1)}, u32[]{:S(2)}, u32[]{:S(2)}) collective-permute-start(bf16[512,128]{1,0:T(8,128)(2,1)S(1)} %join.1.refs_0_), channel_id=1, source_target_pairs={{0,12},{1,11},{4,14},{5,7},{8,10},{9,3},{12,6},{13,1},{14,2},{15,5... | collective-permute-start | bytes 393224 | tf_op jit(solution)/shard_map/ppermute | solution.py:63
  28.6 9.8 %collective-permute-start.12 = (bf16[64,2048]{1,0:T(8,128)(2,1)S(1)}, bf16[64,2048]{1,0:T(8,128)(2,1)S(1)}, u32[]{:S(2)}, u32[]{:S(2)}) collective-permute-start(bf16[64,2048]{1,0:T(8,128)(2,1)S(1)} %get-tuple-element.170.refs_2_), channel_id=1, source_target_pairs={{0,4},{1,5},{4,8},{5,9},{8,12},{9,13},{12,14},{13,15},{14,10},{15,... | collective-permute-start | bytes 786440 | tf_op jit(solution)/shard_map/ppermute | solution.py:52
  28.6 9.8 %collective-permute-start.13 = (bf16[64,2048]{1,0:T(8,128)(2,1)S(1)}, bf16[64,2048]{1,0:T(8,128)(2,1)S(1)}, u32[]{:S(2)}, u32[]{:S(2)}) collective-permute-start(bf16[64,2048]{1,0:T(8,128)(2,1)S(1)} %get-tuple-element.171.refs_3_), channel_id=1, source_target_pairs={{0,2},{1,3},{4,0},{5,1},{8,4},{9,5},{12,8},{13,9},{14,12},{15,13},... | collective-permute-start | bytes 786440 | tf_op jit(solution)/shard_map/ppermute | solution.py:52
  30.6 14.8 %collective-permute-start.14 = (bf16[64,2048]{1,0:T(8,128)(2,1)S(1)}, bf16[64,2048]{1,0:T(8,128)(2,1)S(1)}, u32[]{:S(2)}, u32[]{:S(2)}) collective-permute-start(bf16[64,2048]{1,0:T(8,128)(2,1)S(1)} %get-tuple-element.171.refs_3_), channel_id=1, source_target_pairs={{0,4},{1,5},{4,8},{5,9},{8,12},{9,13},{12,14},{13,15},{14,10},{15,... | collective-permute-start | bytes 786440 | tf_op jit(solution)/shard_map/ppermute | solution.py:52
  30.6 14.9 %collective-permute-start.15 = (bf16[64,2048]{1,0:T(8,128)(2,1)S(1)}, bf16[64,2048]{1,0:T(8,128)(2,1)S(1)}, u32[]{:S(2)}, u32[]{:S(2)}) collective-permute-start(bf16[64,2048]{1,0:T(8,128)(2,1)S(1)} %get-tuple-element.170.refs_2_), channel_id=1, source_target_pairs={{0,2},{1,3},{4,0},{5,1},{8,4},{9,5},{12,8},{13,9},{14,12},{15,13},... | collective-permute-start | bytes 786440 | tf_op jit(solution)/shard_map/ppermute | solution.py:52
  38.4 10.5 %collective-permute-start.16 = (bf16[64,2048]{1,0:T(8,128)(2,1)S(1)}, bf16[64,2048]{1,0:T(8,128)(2,1)S(1)}, u32[]{:S(2)}, u32[]{:S(2)}) collective-permute-start(bf16[64,2048]{1,0:T(8,128)(2,1)S(1)} %collective-permute-done.12.refs_0_), channel_id=1, source_target_pairs={{0,4},{1,5},{4,8},{5,9},{8,12},{9,13},{12,14},{13,15},{14,10},{15,... | collective-permute-start | bytes 786440 | tf_op jit(solution)/shard_map/ppermute | solution.py:52
  39.6 9.4 %collective-permute-start.19 = (bf16[64,2048]{1,0:T(8,128)(2,1)S(1)}, bf16[64,2048]{1,0:T(8,128)(2,1)S(1)}, u32[]{:S(2)}, u32[]{:S(2)}) collective-permute-start(bf16[64,2048]{1,0:T(8,128)(2,1)S(1)} %collective-permute-done.13.refs_1_), channel_id=1, source_target_pairs={{0,2},{1,3},{4,0},{5,1},{8,4},{9,5},{12,8},{13,9},{14,12},{15,13},... | collective-permute-start | bytes 786440 | tf_op jit(solution)/shard_map/ppermute | solution.py:52
  45.5 10.5 %collective-permute-start.22 = (bf16[64,2048]{1,0:T(8,128)(2,1)S(1)}, bf16[64,2048]{1,0:T(8,128)(2,1)S(1)}, u32[]{:S(2)}, u32[]{:S(2)}) collective-permute-start(bf16[64,2048]{1,0:T(8,128)(2,1)S(1)} %collective-permute-done.14.refs_2_), channel_id=1, source_target_pairs={{0,4},{1,5},{4,8},{5,9},{8,12},{9,13},{12,14},{13,15},{14,10},{15,... | collective-permute-start | bytes 786440 | tf_op jit(solution)/shard_map/ppermute | solution.py:52
  46.6 9.4 %collective-permute-start.23 = (bf16[64,2048]{1,0:T(8,128)(2,1)S(1)}, bf16[64,2048]{1,0:T(8,128)(2,1)S(1)}, u32[]{:S(2)}, u32[]{:S(2)}) collective-permute-start(bf16[64,2048]{1,0:T(8,128)(2,1)S(1)} %collective-permute-done.15.refs_3_), channel_id=1, source_target_pairs={{0,2},{1,3},{4,0},{5,1},{8,4},{9,5},{12,8},{13,9},{14,12},{15,13},... | collective-permute-start | bytes 786440 | tf_op jit(solution)/shard_map/ppermute | solution.py:52
  49.0 11.4 %collective-permute-start.17 = (bf16[64,2048]{1,0:T(8,128)(2,1)S(1)}, bf16[64,2048]{1,0:T(8,128)(2,1)S(1)}, u32[]{:S(2)}, u32[]{:S(2)}) collective-permute-start(bf16[64,2048]{1,0:T(8,128)(2,1)S(1)} %collective-permute-done.16.refs_0_), channel_id=1, source_target_pairs={{0,4},{1,5},{4,8},{5,9},{8,12},{9,13},{12,14},{13,15},{14,10},{15,... | collective-permute-start | bytes 786440 | tf_op jit(solution)/shard_map/ppermute | solution.py:52
  49.0 12.5 %collective-permute-start.20 = (bf16[64,2048]{1,0:T(8,128)(2,1)S(1)}, bf16[64,2048]{1,0:T(8,128)(2,1)S(1)}, u32[]{:S(2)}, u32[]{:S(2)}) collective-permute-start(bf16[64,2048]{1,0:T(8,128)(2,1)S(1)} %collective-permute-done.19.refs_1_), channel_id=1, source_target_pairs={{0,2},{1,3},{4,0},{5,1},{8,4},{9,5},{12,8},{13,9},{14,12},{15,13},... | collective-permute-start | bytes 786440 | tf_op jit(solution)/shard_map/ppermute | solution.py:52
  56.0 11.4 %collective-permute-start.24 = (bf16[64,2048]{1,0:T(8,128)(2,1)S(1)}, bf16[64,2048]{1,0:T(8,128)(2,1)S(1)}, u32[]{:S(2)}, u32[]{:S(2)}) collective-permute-start(bf16[64,2048]{1,0:T(8,128)(2,1)S(1)} %collective-permute-done.22.refs_2_), channel_id=1, source_target_pairs={{0,4},{1,5},{4,8},{5,9},{8,12},{9,13},{12,14},{13,15},{14,10},{15,... | collective-permute-start | bytes 786440 | tf_op jit(solution)/shard_map/ppermute | solution.py:52
  57.8 9.6 %collective-permute-start.25 = (bf16[64,2048]{1,0:T(8,128)(2,1)S(1)}, bf16[64,2048]{1,0:T(8,128)(2,1)S(1)}, u32[]{:S(2)}, u32[]{:S(2)}) collective-permute-start(bf16[64,2048]{1,0:T(8,128)(2,1)S(1)} %collective-permute-done.23.refs_3_), channel_id=1, source_target_pairs={{0,2},{1,3},{4,0},{5,1},{8,4},{9,5},{12,8},{13,9},{14,12},{15,13},... | collective-permute-start | bytes 786440 | tf_op jit(solution)/shard_map/ppermute | solution.py:52
  60.4 10.3 %collective-permute-start.18 = (bf16[64,2048]{1,0:T(8,128)(2,1)S(1)}, bf16[64,2048]{1,0:T(8,128)(2,1)S(1)}, u32[]{:S(2)}, u32[]{:S(2)}) collective-permute-start(bf16[64,2048]{1,0:T(8,128)(2,1)S(1)} %collective-permute-done.17.refs_0_), channel_id=1, source_target_pairs={{0,4},{1,5},{4,8},{5,9},{8,12},{9,13},{12,14},{13,15},{14,10},{15,... | collective-permute-start | bytes 786440 | tf_op jit(solution)/shard_map/ppermute | solution.py:52
  61.5 9.3 %collective-permute-start.21 = (bf16[64,2048]{1,0:T(8,128)(2,1)S(1)}, bf16[64,2048]{1,0:T(8,128)(2,1)S(1)}, u32[]{:S(2)}, u32[]{:S(2)}) collective-permute-start(bf16[64,2048]{1,0:T(8,128)(2,1)S(1)} %collective-permute-done.20.refs_1_), channel_id=1, source_target_pairs={{0,2},{1,3},{4,0},{5,1},{8,4},{9,5},{12,8},{13,9},{14,12},{15,13},... | collective-permute-start | bytes 786440 | tf_op jit(solution)/shard_map/ppermute | solution.py:52
  75.7 9.3 %collective-permute-start.26 = (bf16[64,2048]{1,0:T(8,128)(2,1)S(1)}, bf16[64,2048]{1,0:T(8,128)(2,1)S(1)}, u32[]{:S(2)}, u32[]{:S(2)}) collective-permute-start(bf16[64,2048]{1,0:T(8,128)(2,1)S(1)} %get-tuple-element.199), channel_id=1, source_target_pairs={{0,4},{1,5},{4,8},{5,9},{8,12},{9,13},{12,14},{13,15},{14,10},{15,... | collective-permute-start | bytes 786440 | tf_op jit(solution)/shard_map/ppermute | solution.py:52
  77.5 9.4 %collective-permute-start.29 = (bf16[64,2048]{1,0:T(8,128)(2,1)S(1)}, bf16[64,2048]{1,0:T(8,128)(2,1)S(1)}, u32[]{:S(2)}, u32[]{:S(2)}) collective-permute-start(bf16[64,2048]{1,0:T(8,128)(2,1)S(1)} %get-tuple-element.202), channel_id=1, source_target_pairs={{0,2},{1,3},{4,0},{5,1},{8,4},{9,5},{12,8},{13,9},{14,12},{15,13},... | collective-permute-start | bytes 786440 | tf_op jit(solution)/shard_map/ppermute | solution.py:52
  77.8 14.6 %collective-permute-start.33 = (bf16[64,2048]{1,0:T(8,128)(2,1)S(1)}, bf16[64,2048]{1,0:T(8,128)(2,1)S(1)}, u32[]{:S(2)}, u32[]{:S(2)}) collective-permute-start(bf16[64,2048]{1,0:T(8,128)(2,1)S(1)} %get-tuple-element.207), channel_id=1, source_target_pairs={{0,2},{1,3},{4,0},{5,1},{8,4},{9,5},{12,8},{13,9},{14,12},{15,13},... | collective-permute-start | bytes 786440 | tf_op jit(solution)/shard_map/ppermute | solution.py:52
  79.4 13.3 %collective-permute-start.36 = (bf16[64,2048]{1,0:T(8,128)(2,1)S(1)}, bf16[64,2048]{1,0:T(8,128)(2,1)S(1)}, u32[]{:S(2)}, u32[]{:S(2)}) collective-permute-start(bf16[64,2048]{1,0:T(8,128)(2,1)S(1)} %get-tuple-element.210), channel_id=1, source_target_pairs={{0,4},{1,5},{4,8},{5,9},{8,12},{9,13},{12,14},{13,15},{14,10},{15,... | collective-permute-start | bytes 786440 | tf_op jit(solution)/shard_map/ppermute | solution.py:52
  85.1 11.2 %collective-permute-start.27 = (bf16[64,2048]{1,0:T(8,128)(2,1)S(1)}, bf16[64,2048]{1,0:T(8,128)(2,1)S(1)}, u32[]{:S(2)}, u32[]{:S(2)}) collective-permute-start(bf16[64,2048]{1,0:T(8,128)(2,1)S(1)} %add_convert_fusion.12), channel_id=1, source_target_pairs={{0,4},{1,5},{4,8},{5,9},{8,12},{9,13},{12,14},{13,15},{14,10},{15,... | collective-permute-start | bytes 786440 | tf_op jit(solution)/shard_map/ppermute | solution.py:52
  86.9 11.2 %collective-permute-start.30 = (bf16[64,2048]{1,0:T(8,128)(2,1)S(1)}, bf16[64,2048]{1,0:T(8,128)(2,1)S(1)}, u32[]{:S(2)}, u32[]{:S(2)}) collective-permute-start(bf16[64,2048]{1,0:T(8,128)(2,1)S(1)} %add_convert_fusion.10), channel_id=1, source_target_pairs={{0,2},{1,3},{4,0},{5,1},{8,4},{9,5},{12,8},{13,9},{14,12},{15,13},... | collective-permute-start | bytes 786440 | tf_op jit(solution)/shard_map/ppermute | solution.py:52
  92.4 11.2 %collective-permute-start.34 = (bf16[64,2048]{1,0:T(8,128)(2,1)S(1)}, bf16[64,2048]{1,0:T(8,128)(2,1)S(1)}, u32[]{:S(2)}, u32[]{:S(2)}) collective-permute-start(bf16[64,2048]{1,0:T(8,128)(2,1)S(1)} %add_convert_fusion.6), channel_id=1, source_target_pairs={{0,2},{1,3},{4,0},{5,1},{8,4},{9,5},{12,8},{13,9},{14,12},{15,13},... | collective-permute-start | bytes 786440 | tf_op jit(solution)/shard_map/ppermute | solution.py:52
  92.8 11.2 %collective-permute-start.37 = (bf16[64,2048]{1,0:T(8,128)(2,1)S(1)}, bf16[64,2048]{1,0:T(8,128)(2,1)S(1)}, u32[]{:S(2)}, u32[]{:S(2)}) collective-permute-start(bf16[64,2048]{1,0:T(8,128)(2,1)S(1)} %add_convert_fusion.4), channel_id=1, source_target_pairs={{0,4},{1,5},{4,8},{5,9},{8,12},{9,13},{12,14},{13,15},{14,10},{15,... | collective-permute-start | bytes 786440 | tf_op jit(solution)/shard_map/ppermute | solution.py:52
  96.3 16.3 %collective-permute-start.28 = (bf16[64,2048]{1,0:T(8,128)(2,1)S(1)}, bf16[64,2048]{1,0:T(8,128)(2,1)S(1)}, u32[]{:S(2)}, u32[]{:S(2)}) collective-permute-start(bf16[64,2048]{1,0:T(8,128)(2,1)S(1)} %add_convert_fusion.11), channel_id=1, source_target_pairs={{0,4},{1,5},{4,8},{5,9},{8,12},{9,13},{12,14},{13,15},{14,10},{15,... | collective-permute-start | bytes 786440 | tf_op jit(solution)/shard_map/ppermute | solution.py:52
  98.2 11.0 %collective-permute-start.31 = (bf16[64,2048]{1,0:T(8,128)(2,1)S(1)}, bf16[64,2048]{1,0:T(8,128)(2,1)S(1)}, u32[]{:S(2)}, u32[]{:S(2)}) collective-permute-start(bf16[64,2048]{1,0:T(8,128)(2,1)S(1)} %add_convert_fusion.9), channel_id=1, source_target_pairs={{0,2},{1,3},{4,0},{5,1},{8,4},{9,5},{12,8},{13,9},{14,12},{15,13},... | collective-permute-start | bytes 786440 | tf_op jit(solution)/shard_map/ppermute | solution.py:52
  103.7 13.6 %collective-permute-start.35 = (bf16[64,2048]{1,0:T(8,128)(2,1)S(1)}, bf16[64,2048]{1,0:T(8,128)(2,1)S(1)}, u32[]{:S(2)}, u32[]{:S(2)}) collective-permute-start(bf16[64,2048]{1,0:T(8,128)(2,1)S(1)} %add_convert_fusion.5), channel_id=1, source_target_pairs={{0,2},{1,3},{4,0},{5,1},{8,4},{9,5},{12,8},{13,9},{14,12},{15,13},... | collective-permute-start | bytes 786440 | tf_op jit(solution)/shard_map/ppermute | solution.py:52
  104.1 7.0 %collective-permute-start.38 = (bf16[64,2048]{1,0:T(8,128)(2,1)S(1)}, bf16[64,2048]{1,0:T(8,128)(2,1)S(1)}, u32[]{:S(2)}, u32[]{:S(2)}) collective-permute-start(bf16[64,2048]{1,0:T(8,128)(2,1)S(1)} %add_convert_fusion.3), channel_id=1, source_target_pairs={{0,4},{1,5},{4,8},{5,9},{8,12},{9,13},{12,14},{13,15},{14,10},{15,... | collective-permute-start | bytes 786440 | tf_op jit(solution)/shard_map/ppermute | solution.py:52
  109.3 7.9 %collective-permute-start.32 = (bf16[64,2048]{1,0:T(8,128)(2,1)S(1)}, bf16[64,2048]{1,0:T(8,128)(2,1)S(1)}, u32[]{:S(2)}, u32[]{:S(2)}) collective-permute-start(bf16[64,2048]{1,0:T(8,128)(2,1)S(1)} %add_convert_fusion.8), channel_id=1, source_target_pairs={{0,2},{1,3},{4,0},{5,1},{8,4},{9,5},{12,8},{13,9},{14,12},{15,13},... | collective-permute-start | bytes 786440 | tf_op jit(solution)/shard_map/ppermute | solution.py:52
  111.1 6.4 %collective-permute-start.39 = (bf16[64,2048]{1,0:T(8,128)(2,1)S(1)}, bf16[64,2048]{1,0:T(8,128)(2,1)S(1)}, u32[]{:S(2)}, u32[]{:S(2)}) collective-permute-start(bf16[64,2048]{1,0:T(8,128)(2,1)S(1)} %add_convert_fusion.2), channel_id=1, source_target_pairs={{0,4},{1,5},{4,8},{5,9},{8,12},{9,13},{12,14},{13,15},{14,10},{15,... | collective-permute-start | bytes 786440 | tf_op jit(solution)/shard_map/ppermute | solution.py:52
  (11 other events, 88.6 us)

commit v3 on v2

--- a/solution.py
+++ b/solution.py
@@ -261,21 +261,20 @@
     inputs, refs = refs[:blocks], refs[blocks:]
     weights, refs = refs[:6], refs[6:]
     outputs, refs = refs[:blocks], refs[blocks:]
-    turned, inner, total = refs
+    turned, inner = refs
     part = inputs[0].shape[0]
     turned[...] = jnp.concatenate([ref[...] for ref in inputs], axis=0).T
     for side in range(2):
-        gate, up, down = weights[3 * side : 3 * side + 3]
+        gate, up = weights[3 * side : 3 * side + 2]
         gate_out = jnp.dot(gate[...], turned[...], preferred_element_type=jnp.float32)
         up_out = jnp.dot(up[...], turned[...], preferred_element_type=jnp.float32)
-        inner[...] = (gate_out / (1.0 + jnp.exp(-gate_out)) * up_out).astype(jnp.bfloat16)
-        term = jnp.dot(inner[...].T, down[...], preferred_element_type=jnp.float32)
-        if side == 0:
-            total[...] = term
-        else:
-            term = (term + total[...]).astype(jnp.bfloat16)
-            for k in range(blocks):
-                outputs[k][...] = term[k * part : (k + 1) * part]
+        inner[side] = (gate_out / (1.0 + jnp.exp(-gate_out)) * up_out).astype(jnp.bfloat16)
+    term = sum(
+        jnp.dot(inner[side].T, weights[3 * side + 2][...], preferred_element_type=jnp.float32)
+        for side in range(2)
+    ).astype(jnp.bfloat16)
+    for k in range(blocks):
+        outputs[k][...] = term[k * part : (k + 1) * part]
 
 
 def ffn(blocks, weights):
@@ -290,8 +289,7 @@
         out_specs=(vmem,) * count,
         scratch_shapes=[
             pltpu.VMEM((width, count * rows), jnp.bfloat16),
-            pltpu.VMEM((hidden, count * rows), jnp.bfloat16),
-            pltpu.VMEM((count * rows, width), jnp.float32),
+            pltpu.VMEM((2, hidden, count * rows), jnp.bfloat16),
         ],
         compiler_params=pltpu.CompilerParams(vmem_limit_bytes=16 * MIB),
         cost_estimate=pl.CostEstimate(flops=1000, transcendentals=0, bytes_accessed=1000),

time: 119 us -> 119 us (level)
  transfers between devices with their start and end apart: 40 -> 40, of which waited for: 19 -> 18; matrix products, arithmetic and copies ran while one was open for 2% -> 2% of each run, Pallas kernels for 22% -> 22%
where the time goes in v3:
time: 119 us
  waiting for transfers between devices  46.3 us (39%)
  starting transfers between devices  37 us (31%)
  Pallas kernels  31.8 us (27%)
  other arithmetic  2.63 us (2%)
    ppermute x28, waiting for transfers between devices, go(): return lax.ppermute(block, 'ctx', pairs)  34.5 us
    ppermute x28, starting transfers between devices, go(): return lax.ppermute(block, 'ctx', pairs)  28.4 us
    pallas_call x4, Pallas kernels, ffn(): pl.pallas_call(functools.partial(ffn_kernel, count), out_shape=tuple((jax...  19.4 us
    pallas_call x3, Pallas kernels, load(): pl.pallas_call(functools.partial(load_kernel, count), out_shape=tuple((pl...  8.43 us
    ppermute x4, waiting for transfers between devices, go_split(): return lax.ppermute(block, 'ctx', pairs)  7.25 us
    ppermute x4, starting transfers between devices, go_split(): return lax.ppermute(block, 'ctx', pairs)  7.12 us
    ppermute x8, waiting for transfers between devices, go_mate(): return lax.ppermute(block, 'ctx', self.swap)  4.53 us
    pallas_call x1, Pallas kernels, attend(): pl.pallas_call(functools.partial(attention_kernel, len(blocks), heads, he...  3.12 us
  transfers between devices with their start and end apart: 40, of which 18 were waited for; matrix products, arithmetic and copies ran while one was open for 2% of the time, Pallas kernels for 22%

profile of v3, /device:TPU:0, one launch (start us, length us, event | category | flops | bytes accessed | tf_op | source)
XLA Modules:
  0.0 118.7 jit_solution(18347049536436686001)
XLA Ops:
  3.3 2.7 %collective-permute-start.2 = (bf16[512,128]{1,0:T(8,128)(2,1)S(1)}, bf16[512,128]{1,0:T(8,128)(2,1)S(1)}, u32[]{:S(2)}, u32[]{:S(2)}) collective-permute-start(bf16[512,128]{1,0:T(8,128)(2,1)S(1)} %join.1.refs_0_), channel_id=1, source_target_pairs={{0,4},{1,3},{4,8},{5,1},{8,12},{9,5},{12,14},{13,9},{14,10},{15,13... | collective-permute-start | bytes 393224 | tf_op jit(solution)/shard_map/ppermute | solution.py:63
  6.0 3.5 %collective-permute-start.3 = (bf16[512,128]{1,0:T(8,128)(2,1)S(1)}, bf16[512,128]{1,0:T(8,128)(2,1)S(1)}, u32[]{:S(2)}, u32[]{:S(2)}) collective-permute-start(bf16[512,128]{1,0:T(8,128)(2,1)S(1)} %join.1.refs_0_), channel_id=1, source_target_pairs={{0,12},{1,11},{4,14},{5,7},{8,10},{9,3},{12,6},{13,1},{14,2},{15,5... | collective-permute-start | bytes 393224 | tf_op jit(solution)/shard_map/ppermute | solution.py:63
  10.3 2.7 %load.3 = (bf16[128,1024]{1,0:T(8,128)(2,1)S(1)}, s32[16,128]{1,0:T(8,128)S(1)}, s32[16,128]{1,0:T(8,128)S(1)}, bf16[128,2048]{1,0:T(8,128)(2,1)S(1)}, f32[1,204...) custom-call(bf16[128,1024]{1,0:T(8,128)(2,1)} %refs_0_.3, s32[16,128]{1,0:T(8,128)} %bitcast.7, s32[16,128]{1,0:T(8,128)} %bitcast.9, ...), custom_call_target="tpu_custom_call" | custom-call | tf_op jit(solution)/shard_map/load/pallas_call | solution.py:221
  13.7 1.9 %collective-permute-done.3.refs_3_ = bf16[512,128]{1,0:T(8,128)(2,1)S(1)} collective-permute-done((bf16[512,128]{1,0:T(8,128)(2,1)S(1)}, bf16[512,128]{1,0:T(8,128)(2,1)S(1)}, u32[]{:S(2)}, u32[]{:S(2)}) %collective-permute-start.3) | collective-permute-done | bytes 131104 | tf_op jit(solution)/shard_map/ppermute | solution.py:63
  16.6 4.0 %collective-permute-done.4.refs_2_ = bf16[512,128]{1,0:T(8,128)(2,1)S(1)} collective-permute-done((bf16[512,128]{1,0:T(8,128)(2,1)S(1)}, bf16[512,128]{1,0:T(8,128)(2,1)S(1)}, u32[]{:S(2)}, u32[]{:S(2)}) %collective-permute-start.4) | collective-permute-done | bytes 131104 | tf_op jit(solution)/shard_map/ppermute | solution.py:63
  23.5 3.1 %attention.1 = (bf16[64,2048]{1,0:T(8,128)(2,1)S(1)}, bf16[64,2048]{1,0:T(8,128)(2,1)S(1)}, bf16[128,2048]{1,0:T(8,128)(2,1)S(1)}) custom-call(s32[16]{0:T(128)S(1)} %dynamic-slice_bitcast_fusion.owner_ref, s32[16,128]{1,0:T(8,128)S(1)} %bitcast.8, s32[16,128]{1,0:T(8,128)S(1)} %bitcast.10, bf16[128,1024]{1,0:T(8,128)(2,1)S(1)} %get-tuple-element.129.query_ref, ...), custom_call_target="tpu_custom_call" | custom-call | tf_op jit(solution)/shard_map/attention/pallas_call | solution.py:192
  26.7 1.9 %collective-permute-done.11.refs_2_ = bf16[688,2048]{1,0:T(8,128)(2,1)S(1)} collective-permute-done((bf16[688,2048]{1,0:T(8,128)(2,1)S(1)}, bf16[688,2048]{1,0:T(8,128)(2,1)S(1)}, u32[]{:S(2)}, u32[]{:S(2)}) %collective-permute-start.11) | collective-permute-done | bytes 2818080 | tf_op jit(solution)/shard_map/ppermute | solution.py:55
  28.6 2.0 %collective-permute-start.13 = (bf16[64,2048]{1,0:T(8,128)(2,1)S(1)}, bf16[64,2048]{1,0:T(8,128)(2,1)S(1)}, u32[]{:S(2)}, u32[]{:S(2)}) collective-permute-start(bf16[64,2048]{1,0:T(8,128)(2,1)S(1)} %get-tuple-element.171.refs_3_), channel_id=1, source_target_pairs={{0,2},{1,3},{4,0},{5,1},{8,4},{9,5},{12,8},{13,9},{14,12},{15,13},... | collective-permute-start | bytes 786440 | tf_op jit(solution)/shard_map/ppermute | solution.py:52
  30.6 2.0 %collective-permute-start.15 = (bf16[64,2048]{1,0:T(8,128)(2,1)S(1)}, bf16[64,2048]{1,0:T(8,128)(2,1)S(1)}, u32[]{:S(2)}, u32[]{:S(2)}) collective-permute-start(bf16[64,2048]{1,0:T(8,128)(2,1)S(1)} %get-tuple-element.170.refs_2_), channel_id=1, source_target_pairs={{0,2},{1,3},{4,0},{5,1},{8,4},{9,5},{12,8},{13,9},{14,12},{15,13},... | collective-permute-start | bytes 786440 | tf_op jit(solution)/shard_map/ppermute | solution.py:52
  32.6 2.2 %load.5 = (bf16[688,2048]{1,0:T(8,128)(2,1)S(1)}, bf16[688,2048]{1,0:T(8,128)(2,1)S(1)}, bf16[688,2048]{1,0:T(8,128)(2,1)S(1)}) custom-call(bf16[688,2048]{1,0:T(8,128)(2,1)S(1)} %collective-permute-done.8.refs_0_, bf16[688,2048]{1,0:T(8,128)(2,1)} %collective-permute-done.9.refs_1_, bf16[688,2048]{1,0:T(8,128)(2,1)S(1)} %collective-permute-done.11.refs_2_), custom_call_target="tpu_custom_call" | custom-call | tf_op jit(solution)/shard_map/load/pallas_call | solution.py:221
  34.9 3.5 %load.4 = (bf16[688,2048]{1,0:T(8,128)(2,1)S(1)}, bf16[688,2048]{1,0:T(8,128)(2,1)S(1)}, bf16[688,2048]{1,0:T(8,128)(2,1)S(1)}) custom-call(bf16[688,2048]{1,0:T(8,128)(2,1)} %bitcast.12, bf16[688,2048]{1,0:T(8,128)(2,1)} %bitcast.14, bf16[688,2048]{1,0:T(8,128)(2,1)} %refs_2_), custom_call_target="tpu_custom_call" | custom-call | tf_op jit(solution)/shard_map/load/pallas_call | solution.py:221
  40.5 4.8 %feed_forward.4 = (bf16[64,2048]{1,0:T(8,128)(2,1)S(1)}, bf16[64,2048]{1,0:T(8,128)(2,1)S(1)}, bf16[64,2048]{1,0:T(8,128)(2,1)S(1)}, bf16[64,2048]{1,0:T(8,128)(2,1)S(1)}) custom-call(bf16[64,2048]{1,0:T(8,128)(2,1)S(1)} %collective-permute-done.12.refs_0_, bf16[64,2048]{1,0:T(8,128)(2,1)S(1)} %collective-permute-done.13.refs_1_, ...), custom_call_target="tpu_custom_call" | custom-call | flops 1000 | bytes 1000 | tf_op jit(solution)/shard_map/feed_forward/pallas_call | solution.py:285
  49.0 2.1 %collective-permute-start.20 = (bf16[64,2048]{1,0:T(8,128)(2,1)S(1)}, bf16[64,2048]{1,0:T(8,128)(2,1)S(1)}, u32[]{:S(2)}, u32[]{:S(2)}) collective-permute-start(bf16[64,2048]{1,0:T(8,128)(2,1)S(1)} %collective-permute-done.19.refs_1_), channel_id=1, source_target_pairs={{0,2},{1,3},{4,0},{5,1},{8,4},{9,5},{12,8},{13,9},{14,12},{15,13},... | collective-permute-start | bytes 786440 | tf_op jit(solution)/shard_map/ppermute | solution.py:52
  51.0 4.9 %feed_forward.6 = (bf16[64,2048]{1,0:T(8,128)(2,1)S(1)}, bf16[64,2048]{1,0:T(8,128)(2,1)S(1)}, bf16[64,2048]{1,0:T(8,128)(2,1)S(1)}, bf16[64,2048]{1,0:T(8,128)(2,1)S(1)}) custom-call(bf16[64,2048]{1,0:T(8,128)(2,1)S(1)} %collective-permute-done.16.refs_0_, bf16[64,2048]{1,0:T(8,128)(2,1)S(1)} %collective-permute-done.19.refs_1_, ...), custom_call_target="tpu_custom_call" | custom-call | flops 1000 | bytes 1000 | tf_op jit(solution)/shard_map/feed_forward/pallas_call | solution.py:285
  55.9 1.8 %collective-permute-start.24 = (bf16[64,2048]{1,0:T(8,128)(2,1)S(1)}, bf16[64,2048]{1,0:T(8,128)(2,1)S(1)}, u32[]{:S(2)}, u32[]{:S(2)}) collective-permute-start(bf16[64,2048]{1,0:T(8,128)(2,1)S(1)} %collective-permute-done.22.refs_2_), channel_id=1, source_target_pairs={{0,4},{1,5},{4,8},{5,9},{8,12},{9,13},{12,14},{13,15},{14,10},{15,... | collective-permute-start | bytes 786440 | tf_op jit(solution)/shard_map/ppermute | solution.py:52
  58.0 2.3 %collective-permute-done.17.refs_0_ = bf16[64,2048]{1,0:T(8,128)(2,1)S(1)} collective-permute-done((bf16[64,2048]{1,0:T(8,128)(2,1)S(1)}, bf16[64,2048]{1,0:T(8,128)(2,1)S(1)}, u32[]{:S(2)}, u32[]{:S(2)}) %collective-permute-start.17) | collective-permute-done | bytes 262176 | tf_op jit(solution)/shard_map/ppermute | solution.py:52
  62.3 4.8 %feed_forward.5 = (bf16[64,2048]{1,0:T(8,128)(2,1)S(1)}, bf16[64,2048]{1,0:T(8,128)(2,1)S(1)}, bf16[64,2048]{1,0:T(8,128)(2,1)S(1)}, bf16[64,2048]{1,0:T(8,128)(2,1)S(1)}) custom-call(bf16[64,2048]{1,0:T(8,128)(2,1)S(1)} %collective-permute-done.17.refs_0_, bf16[64,2048]{1,0:T(8,128)(2,1)S(1)} %collective-permute-done.20.refs_1_, ...), custom_call_target="tpu_custom_call" | custom-call | flops 1000 | bytes 1000 | tf_op jit(solution)/shard_map/feed_forward/pallas_call | solution.py:285
  67.2 3.4 %collective-permute-done.18.refs_0_ = bf16[64,2048]{1,0:T(8,128)(2,1)S(1)} collective-permute-done((bf16[64,2048]{1,0:T(8,128)(2,1)S(1)}, bf16[64,2048]{1,0:T(8,128)(2,1)S(1)}, u32[]{:S(2)}, u32[]{:S(2)}) %collective-permute-start.18) | collective-permute-done | bytes 262176 | tf_op jit(solution)/shard_map/ppermute | solution.py:52
  70.6 4.8 %feed_forward.7 = (bf16[64,2048]{1,0:T(8,128)(2,1)S(1)}, bf16[64,2048]{1,0:T(8,128)(2,1)S(1)}, bf16[64,2048]{1,0:T(8,128)(2,1)S(1)}, bf16[64,2048]{1,0:T(8,128)(2,1)S(1)}) custom-call(bf16[64,2048]{1,0:T(8,128)(2,1)S(1)} %collective-permute-done.18.refs_0_, bf16[64,2048]{1,0:T(8,128)(2,1)S(1)} %collective-permute-done.21.refs_1_, ...), custom_call_target="tpu_custom_call" | custom-call | flops 1000 | bytes 1000 | tf_op jit(solution)/shard_map/feed_forward/pallas_call | solution.py:285
  75.5 1.8 %collective-permute-start.26 = (bf16[64,2048]{1,0:T(8,128)(2,1)S(1)}, bf16[64,2048]{1,0:T(8,128)(2,1)S(1)}, u32[]{:S(2)}, u32[]{:S(2)}) collective-permute-start(bf16[64,2048]{1,0:T(8,128)(2,1)S(1)} %get-tuple-element.199), channel_id=1, source_target_pairs={{0,4},{1,5},{4,8},{5,9},{8,12},{9,13},{12,14},{13,15},{14,10},{15,... | collective-permute-start | bytes 786440 | tf_op jit(solution)/shard_map/ppermute | solution.py:52
  77.6 1.7 %collective-permute-start.33 = (bf16[64,2048]{1,0:T(8,128)(2,1)S(1)}, bf16[64,2048]{1,0:T(8,128)(2,1)S(1)}, u32[]{:S(2)}, u32[]{:S(2)}) collective-permute-start(bf16[64,2048]{1,0:T(8,128)(2,1)S(1)} %get-tuple-element.207), channel_id=1, source_target_pairs={{0,2},{1,3},{4,0},{5,1},{8,4},{9,5},{12,8},{13,9},{14,12},{15,13},... | collective-permute-start | bytes 786440 | tf_op jit(solution)/shard_map/ppermute | solution.py:52
  79.6 5.2 %collective-permute-done.26 = bf16[64,2048]{1,0:T(8,128)(2,1)S(1)} collective-permute-done((bf16[64,2048]{1,0:T(8,128)(2,1)S(1)}, bf16[64,2048]{1,0:T(8,128)(2,1)S(1)}, u32[]{:S(2)}, u32[]{:S(2)}) %collective-permute-start.26) | collective-permute-done | bytes 262176 | tf_op jit(solution)/shard_map/ppermute | solution.py:52
  84.9 1.7 %collective-permute-start.27 = (bf16[64,2048]{1,0:T(8,128)(2,1)S(1)}, bf16[64,2048]{1,0:T(8,128)(2,1)S(1)}, u32[]{:S(2)}, u32[]{:S(2)}) collective-permute-start(bf16[64,2048]{1,0:T(8,128)(2,1)S(1)} %add_convert_fusion.12), channel_id=1, source_target_pairs={{0,4},{1,5},{4,8},{5,9},{8,12},{9,13},{12,14},{13,15},{14,10},{15,... | collective-permute-start | bytes 786440 | tf_op jit(solution)/shard_map/ppermute | solution.py:52
  87.1 5.0 %collective-permute-done.33 = bf16[64,2048]{1,0:T(8,128)(2,1)S(1)} collective-permute-done((bf16[64,2048]{1,0:T(8,128)(2,1)S(1)}, bf16[64,2048]{1,0:T(8,128)(2,1)S(1)}, u32[]{:S(2)}, u32[]{:S(2)}) %collective-permute-start.33) | collective-permute-done | bytes 262176 | tf_op jit(solution)/shard_map/ppermute | solution.py:52
  92.6 1.8 %collective-permute-start.37 = (bf16[64,2048]{1,0:T(8,128)(2,1)S(1)}, bf16[64,2048]{1,0:T(8,128)(2,1)S(1)}, u32[]{:S(2)}, u32[]{:S(2)}) collective-permute-start(bf16[64,2048]{1,0:T(8,128)(2,1)S(1)} %add_convert_fusion.4), channel_id=1, source_target_pairs={{0,4},{1,5},{4,8},{5,9},{8,12},{9,13},{12,14},{13,15},{14,10},{15,... | collective-permute-start | bytes 786440 | tf_op jit(solution)/shard_map/ppermute | solution.py:52
  94.4 1.6 %collective-permute-done.27 = bf16[64,2048]{1,0:T(8,128)(2,1)S(1)} collective-permute-done((bf16[64,2048]{1,0:T(8,128)(2,1)S(1)}, bf16[64,2048]{1,0:T(8,128)(2,1)S(1)}, u32[]{:S(2)}, u32[]{:S(2)}) %collective-permute-start.27) | collective-permute-done | bytes 262176 | tf_op jit(solution)/shard_map/ppermute | solution.py:52
  96.1 1.7 %collective-permute-start.28 = (bf16[64,2048]{1,0:T(8,128)(2,1)S(1)}, bf16[64,2048]{1,0:T(8,128)(2,1)S(1)}, u32[]{:S(2)}, u32[]{:S(2)}) collective-permute-start(bf16[64,2048]{1,0:T(8,128)(2,1)S(1)} %add_convert_fusion.11), channel_id=1, source_target_pairs={{0,4},{1,5},{4,8},{5,9},{8,12},{9,13},{12,14},{13,15},{14,10},{15,... | collective-permute-start | bytes 786440 | tf_op jit(solution)/shard_map/ppermute | solution.py:52
  98.3 5.0 %collective-permute-done.34 = bf16[64,2048]{1,0:T(8,128)(2,1)S(1)} collective-permute-done((bf16[64,2048]{1,0:T(8,128)(2,1)S(1)}, bf16[64,2048]{1,0:T(8,128)(2,1)S(1)}, u32[]{:S(2)}, u32[]{:S(2)}) %collective-permute-start.34) | collective-permute-done | bytes 262176 | tf_op jit(solution)/shard_map/ppermute | solution.py:52
  103.9 1.8 %collective-permute-start.38 = (bf16[64,2048]{1,0:T(8,128)(2,1)S(1)}, bf16[64,2048]{1,0:T(8,128)(2,1)S(1)}, u32[]{:S(2)}, u32[]{:S(2)}) collective-permute-start(bf16[64,2048]{1,0:T(8,128)(2,1)S(1)} %add_convert_fusion.3), channel_id=1, source_target_pairs={{0,4},{1,5},{4,8},{5,9},{8,12},{9,13},{12,14},{13,15},{14,10},{15,... | collective-permute-start | bytes 786440 | tf_op jit(solution)/shard_map/ppermute | solution.py:52
  105.6 3.3 %collective-permute-done.31 = bf16[64,2048]{1,0:T(8,128)(2,1)S(1)} collective-permute-done((bf16[64,2048]{1,0:T(8,128)(2,1)S(1)}, bf16[64,2048]{1,0:T(8,128)(2,1)S(1)}, u32[]{:S(2)}, u32[]{:S(2)}) %collective-permute-start.31) | collective-permute-done | bytes 262176 | tf_op jit(solution)/shard_map/ppermute | solution.py:52
  109.4 1.6 %collective-permute-done.38 = bf16[64,2048]{1,0:T(8,128)(2,1)S(1)} collective-permute-done((bf16[64,2048]{1,0:T(8,128)(2,1)S(1)}, bf16[64,2048]{1,0:T(8,128)(2,1)S(1)}, u32[]{:S(2)}, u32[]{:S(2)}) %collective-permute-start.38) | collective-permute-done | bytes 262176 | tf_op jit(solution)/shard_map/ppermute | solution.py:52
  112.1 5.0 %collective-permute-done.32 = bf16[64,2048]{1,0:T(8,128)(2,1)S(1)} collective-permute-done((bf16[64,2048]{1,0:T(8,128)(2,1)S(1)}, bf16[64,2048]{1,0:T(8,128)(2,1)S(1)}, u32[]{:S(2)}, u32[]{:S(2)}) %collective-permute-start.32) | collective-permute-done | bytes 262176 | tf_op jit(solution)/shard_map/ppermute | solution.py:52
  (78 shorter events, 22.5 us)
Async XLA Ops:
  2.7 20.6 %collective-permute-start.8 = (bf16[688,2048]{1,0:T(8,128)(2,1)}, bf16[688,2048]{1,0:T(8,128)(2,1)S(1)}, u32[]{:S(2)}, u32[]{:S(2)}) collective-permute-start(bf16[688,2048]{1,0:T(8,128)(2,1)} %bitcast.11), channel_id=1, source_target_pairs={{0,1},{1,0},{2,3},{3,2},{4,5},{5,4},{6,7},{7,6},{8,9},{9,8},{10,11... | collective-permute-start | bytes 8454152 | tf_op jit(solution)/shard_map/ppermute | solution.py:55
  2.9 20.4 %collective-permute-start.9 = (bf16[688,2048]{1,0:T(8,128)(2,1)}, bf16[688,2048]{1,0:T(8,128)(2,1)}, u32[]{:S(2)}, u32[]{:S(2)}) collective-permute-start(bf16[688,2048]{1,0:T(8,128)(2,1)} %bitcast.13), channel_id=1, source_target_pairs={{0,1},{1,0},{2,3},{3,2},{4,5},{5,4},{6,7},{7,6},{8,9},{9,8},{10,11... | collective-permute-start | bytes 8454152 | tf_op jit(solution)/shard_map/ppermute | solution.py:55
  3.3 10.4 %collective-permute-start.2 = (bf16[512,128]{1,0:T(8,128)(2,1)S(1)}, bf16[512,128]{1,0:T(8,128)(2,1)S(1)}, u32[]{:S(2)}, u32[]{:S(2)}) collective-permute-start(bf16[512,128]{1,0:T(8,128)(2,1)S(1)} %join.1.refs_0_), channel_id=1, source_target_pairs={{0,4},{1,3},{4,8},{5,1},{8,12},{9,5},{12,14},{13,9},{14,10},{15,13... | collective-permute-start | bytes 393224 | tf_op jit(solution)/shard_map/ppermute | solution.py:63
  6.0 9.6 %collective-permute-start.3 = (bf16[512,128]{1,0:T(8,128)(2,1)S(1)}, bf16[512,128]{1,0:T(8,128)(2,1)S(1)}, u32[]{:S(2)}, u32[]{:S(2)}) collective-permute-start(bf16[512,128]{1,0:T(8,128)(2,1)S(1)} %join.1.refs_0_), channel_id=1, source_target_pairs={{0,12},{1,11},{4,14},{5,7},{8,10},{9,3},{12,6},{13,1},{14,2},{15,5... | collective-permute-start | bytes 393224 | tf_op jit(solution)/shard_map/ppermute | solution.py:63
  28.6 9.8 %collective-permute-start.12 = (bf16[64,2048]{1,0:T(8,128)(2,1)S(1)}, bf16[64,2048]{1,0:T(8,128)(2,1)S(1)}, u32[]{:S(2)}, u32[]{:S(2)}) collective-permute-start(bf16[64,2048]{1,0:T(8,128)(2,1)S(1)} %get-tuple-element.170.refs_2_), channel_id=1, source_target_pairs={{0,4},{1,5},{4,8},{5,9},{8,12},{9,13},{12,14},{13,15},{14,10},{15,... | collective-permute-start | bytes 786440 | tf_op jit(solution)/shard_map/ppermute | solution.py:52
  28.6 9.8 %collective-permute-start.13 = (bf16[64,2048]{1,0:T(8,128)(2,1)S(1)}, bf16[64,2048]{1,0:T(8,128)(2,1)S(1)}, u32[]{:S(2)}, u32[]{:S(2)}) collective-permute-start(bf16[64,2048]{1,0:T(8,128)(2,1)S(1)} %get-tuple-element.171.refs_3_), channel_id=1, source_target_pairs={{0,2},{1,3},{4,0},{5,1},{8,4},{9,5},{12,8},{13,9},{14,12},{15,13},... | collective-permute-start | bytes 786440 | tf_op jit(solution)/shard_map/ppermute | solution.py:52
  30.6 14.8 %collective-permute-start.14 = (bf16[64,2048]{1,0:T(8,128)(2,1)S(1)}, bf16[64,2048]{1,0:T(8,128)(2,1)S(1)}, u32[]{:S(2)}, u32[]{:S(2)}) collective-permute-start(bf16[64,2048]{1,0:T(8,128)(2,1)S(1)} %get-tuple-element.171.refs_3_), channel_id=1, source_target_pairs={{0,4},{1,5},{4,8},{5,9},{8,12},{9,13},{12,14},{13,15},{14,10},{15,... | collective-permute-start | bytes 786440 | tf_op jit(solution)/shard_map/ppermute | solution.py:52
  30.6 14.8 %collective-permute-start.15 = (bf16[64,2048]{1,0:T(8,128)(2,1)S(1)}, bf16[64,2048]{1,0:T(8,128)(2,1)S(1)}, u32[]{:S(2)}, u32[]{:S(2)}) collective-permute-start(bf16[64,2048]{1,0:T(8,128)(2,1)S(1)} %get-tuple-element.170.refs_2_), channel_id=1, source_target_pairs={{0,2},{1,3},{4,0},{5,1},{8,4},{9,5},{12,8},{13,9},{14,12},{15,13},... | collective-permute-start | bytes 786440 | tf_op jit(solution)/shard_map/ppermute | solution.py:52
  38.4 10.5 %collective-permute-start.16 = (bf16[64,2048]{1,0:T(8,128)(2,1)S(1)}, bf16[64,2048]{1,0:T(8,128)(2,1)S(1)}, u32[]{:S(2)}, u32[]{:S(2)}) collective-permute-start(bf16[64,2048]{1,0:T(8,128)(2,1)S(1)} %collective-permute-done.12.refs_0_), channel_id=1, source_target_pairs={{0,4},{1,5},{4,8},{5,9},{8,12},{9,13},{12,14},{13,15},{14,10},{15,... | collective-permute-start | bytes 786440 | tf_op jit(solution)/shard_map/ppermute | solution.py:52
  39.6 9.4 %collective-permute-start.19 = (bf16[64,2048]{1,0:T(8,128)(2,1)S(1)}, bf16[64,2048]{1,0:T(8,128)(2,1)S(1)}, u32[]{:S(2)}, u32[]{:S(2)}) collective-permute-start(bf16[64,2048]{1,0:T(8,128)(2,1)S(1)} %collective-permute-done.13.refs_1_), channel_id=1, source_target_pairs={{0,2},{1,3},{4,0},{5,1},{8,4},{9,5},{12,8},{13,9},{14,12},{15,13},... | collective-permute-start | bytes 786440 | tf_op jit(solution)/shard_map/ppermute | solution.py:52
  45.4 10.5 %collective-permute-start.22 = (bf16[64,2048]{1,0:T(8,128)(2,1)S(1)}, bf16[64,2048]{1,0:T(8,128)(2,1)S(1)}, u32[]{:S(2)}, u32[]{:S(2)}) collective-permute-start(bf16[64,2048]{1,0:T(8,128)(2,1)S(1)} %collective-permute-done.14.refs_2_), channel_id=1, source_target_pairs={{0,4},{1,5},{4,8},{5,9},{8,12},{9,13},{12,14},{13,15},{14,10},{15,... | collective-permute-start | bytes 786440 | tf_op jit(solution)/shard_map/ppermute | solution.py:52
  46.6 9.4 %collective-permute-start.23 = (bf16[64,2048]{1,0:T(8,128)(2,1)S(1)}, bf16[64,2048]{1,0:T(8,128)(2,1)S(1)}, u32[]{:S(2)}, u32[]{:S(2)}) collective-permute-start(bf16[64,2048]{1,0:T(8,128)(2,1)S(1)} %collective-permute-done.15.refs_3_), channel_id=1, source_target_pairs={{0,2},{1,3},{4,0},{5,1},{8,4},{9,5},{12,8},{13,9},{14,12},{15,13},... | collective-permute-start | bytes 786440 | tf_op jit(solution)/shard_map/ppermute | solution.py:52
  49.0 11.3 %collective-permute-start.17 = (bf16[64,2048]{1,0:T(8,128)(2,1)S(1)}, bf16[64,2048]{1,0:T(8,128)(2,1)S(1)}, u32[]{:S(2)}, u32[]{:S(2)}) collective-permute-start(bf16[64,2048]{1,0:T(8,128)(2,1)S(1)} %collective-permute-done.16.refs_0_), channel_id=1, source_target_pairs={{0,4},{1,5},{4,8},{5,9},{8,12},{9,13},{12,14},{13,15},{14,10},{15,... | collective-permute-start | bytes 786440 | tf_op jit(solution)/shard_map/ppermute | solution.py:52
  49.0 12.4 %collective-permute-start.20 = (bf16[64,2048]{1,0:T(8,128)(2,1)S(1)}, bf16[64,2048]{1,0:T(8,128)(2,1)S(1)}, u32[]{:S(2)}, u32[]{:S(2)}) collective-permute-start(bf16[64,2048]{1,0:T(8,128)(2,1)S(1)} %collective-permute-done.19.refs_1_), channel_id=1, source_target_pairs={{0,2},{1,3},{4,0},{5,1},{8,4},{9,5},{12,8},{13,9},{14,12},{15,13},... | collective-permute-start | bytes 786440 | tf_op jit(solution)/shard_map/ppermute | solution.py:52
  55.9 11.3 %collective-permute-start.24 = (bf16[64,2048]{1,0:T(8,128)(2,1)S(1)}, bf16[64,2048]{1,0:T(8,128)(2,1)S(1)}, u32[]{:S(2)}, u32[]{:S(2)}) collective-permute-start(bf16[64,2048]{1,0:T(8,128)(2,1)S(1)} %collective-permute-done.22.refs_2_), channel_id=1, source_target_pairs={{0,4},{1,5},{4,8},{5,9},{8,12},{9,13},{12,14},{13,15},{14,10},{15,... | collective-permute-start | bytes 786440 | tf_op jit(solution)/shard_map/ppermute | solution.py:52
  57.7 9.5 %collective-permute-start.25 = (bf16[64,2048]{1,0:T(8,128)(2,1)S(1)}, bf16[64,2048]{1,0:T(8,128)(2,1)S(1)}, u32[]{:S(2)}, u32[]{:S(2)}) collective-permute-start(bf16[64,2048]{1,0:T(8,128)(2,1)S(1)} %collective-permute-done.23.refs_3_), channel_id=1, source_target_pairs={{0,2},{1,3},{4,0},{5,1},{8,4},{9,5},{12,8},{13,9},{14,12},{15,13},... | collective-permute-start | bytes 786440 | tf_op jit(solution)/shard_map/ppermute | solution.py:52
  60.3 10.3 %collective-permute-start.18 = (bf16[64,2048]{1,0:T(8,128)(2,1)S(1)}, bf16[64,2048]{1,0:T(8,128)(2,1)S(1)}, u32[]{:S(2)}, u32[]{:S(2)}) collective-permute-start(bf16[64,2048]{1,0:T(8,128)(2,1)S(1)} %collective-permute-done.17.refs_0_), channel_id=1, source_target_pairs={{0,4},{1,5},{4,8},{5,9},{8,12},{9,13},{12,14},{13,15},{14,10},{15,... | collective-permute-start | bytes 786440 | tf_op jit(solution)/shard_map/ppermute | solution.py:52
  61.4 9.2 %collective-permute-start.21 = (bf16[64,2048]{1,0:T(8,128)(2,1)S(1)}, bf16[64,2048]{1,0:T(8,128)(2,1)S(1)}, u32[]{:S(2)}, u32[]{:S(2)}) collective-permute-start(bf16[64,2048]{1,0:T(8,128)(2,1)S(1)} %collective-permute-done.20.refs_1_), channel_id=1, source_target_pairs={{0,2},{1,3},{4,0},{5,1},{8,4},{9,5},{12,8},{13,9},{14,12},{15,13},... | collective-permute-start | bytes 786440 | tf_op jit(solution)/shard_map/ppermute | solution.py:52
  75.5 9.3 %collective-permute-start.26 = (bf16[64,2048]{1,0:T(8,128)(2,1)S(1)}, bf16[64,2048]{1,0:T(8,128)(2,1)S(1)}, u32[]{:S(2)}, u32[]{:S(2)}) collective-permute-start(bf16[64,2048]{1,0:T(8,128)(2,1)S(1)} %get-tuple-element.199), channel_id=1, source_target_pairs={{0,4},{1,5},{4,8},{5,9},{8,12},{9,13},{12,14},{13,15},{14,10},{15,... | collective-permute-start | bytes 786440 | tf_op jit(solution)/shard_map/ppermute | solution.py:52
  77.3 9.3 %collective-permute-start.29 = (bf16[64,2048]{1,0:T(8,128)(2,1)S(1)}, bf16[64,2048]{1,0:T(8,128)(2,1)S(1)}, u32[]{:S(2)}, u32[]{:S(2)}) collective-permute-start(bf16[64,2048]{1,0:T(8,128)(2,1)S(1)} %get-tuple-element.202), channel_id=1, source_target_pairs={{0,2},{1,3},{4,0},{5,1},{8,4},{9,5},{12,8},{13,9},{14,12},{15,13},... | collective-permute-start | bytes 786440 | tf_op jit(solution)/shard_map/ppermute | solution.py:52
  77.6 14.5 %collective-permute-start.33 = (bf16[64,2048]{1,0:T(8,128)(2,1)S(1)}, bf16[64,2048]{1,0:T(8,128)(2,1)S(1)}, u32[]{:S(2)}, u32[]{:S(2)}) collective-permute-start(bf16[64,2048]{1,0:T(8,128)(2,1)S(1)} %get-tuple-element.207), channel_id=1, source_target_pairs={{0,2},{1,3},{4,0},{5,1},{8,4},{9,5},{12,8},{13,9},{14,12},{15,13},... | collective-permute-start | bytes 786440 | tf_op jit(solution)/shard_map/ppermute | solution.py:52
  79.3 13.3 %collective-permute-start.36 = (bf16[64,2048]{1,0:T(8,128)(2,1)S(1)}, bf16[64,2048]{1,0:T(8,128)(2,1)S(1)}, u32[]{:S(2)}, u32[]{:S(2)}) collective-permute-start(bf16[64,2048]{1,0:T(8,128)(2,1)S(1)} %get-tuple-element.210), channel_id=1, source_target_pairs={{0,4},{1,5},{4,8},{5,9},{8,12},{9,13},{12,14},{13,15},{14,10},{15,... | collective-permute-start | bytes 786440 | tf_op jit(solution)/shard_map/ppermute | solution.py:52
  84.9 11.2 %collective-permute-start.27 = (bf16[64,2048]{1,0:T(8,128)(2,1)S(1)}, bf16[64,2048]{1,0:T(8,128)(2,1)S(1)}, u32[]{:S(2)}, u32[]{:S(2)}) collective-permute-start(bf16[64,2048]{1,0:T(8,128)(2,1)S(1)} %add_convert_fusion.12), channel_id=1, source_target_pairs={{0,4},{1,5},{4,8},{5,9},{8,12},{9,13},{12,14},{13,15},{14,10},{15,... | collective-permute-start | bytes 786440 | tf_op jit(solution)/shard_map/ppermute | solution.py:52
  86.6 11.2 %collective-permute-start.30 = (bf16[64,2048]{1,0:T(8,128)(2,1)S(1)}, bf16[64,2048]{1,0:T(8,128)(2,1)S(1)}, u32[]{:S(2)}, u32[]{:S(2)}) collective-permute-start(bf16[64,2048]{1,0:T(8,128)(2,1)S(1)} %add_convert_fusion.10), channel_id=1, source_target_pairs={{0,2},{1,3},{4,0},{5,1},{8,4},{9,5},{12,8},{13,9},{14,12},{15,13},... | collective-permute-start | bytes 786440 | tf_op jit(solution)/shard_map/ppermute | solution.py:52
  92.2 11.2 %collective-permute-start.34 = (bf16[64,2048]{1,0:T(8,128)(2,1)S(1)}, bf16[64,2048]{1,0:T(8,128)(2,1)S(1)}, u32[]{:S(2)}, u32[]{:S(2)}) collective-permute-start(bf16[64,2048]{1,0:T(8,128)(2,1)S(1)} %add_convert_fusion.6), channel_id=1, source_target_pairs={{0,2},{1,3},{4,0},{5,1},{8,4},{9,5},{12,8},{13,9},{14,12},{15,13},... | collective-permute-start | bytes 786440 | tf_op jit(solution)/shard_map/ppermute | solution.py:52
  92.6 11.2 %collective-permute-start.37 = (bf16[64,2048]{1,0:T(8,128)(2,1)S(1)}, bf16[64,2048]{1,0:T(8,128)(2,1)S(1)}, u32[]{:S(2)}, u32[]{:S(2)}) collective-permute-start(bf16[64,2048]{1,0:T(8,128)(2,1)S(1)} %add_convert_fusion.4), channel_id=1, source_target_pairs={{0,4},{1,5},{4,8},{5,9},{8,12},{9,13},{12,14},{13,15},{14,10},{15,... | collective-permute-start | bytes 786440 | tf_op jit(solution)/shard_map/ppermute | solution.py:52
  96.1 16.0 %collective-permute-start.28 = (bf16[64,2048]{1,0:T(8,128)(2,1)S(1)}, bf16[64,2048]{1,0:T(8,128)(2,1)S(1)}, u32[]{:S(2)}, u32[]{:S(2)}) collective-permute-start(bf16[64,2048]{1,0:T(8,128)(2,1)S(1)} %add_convert_fusion.11), channel_id=1, source_target_pairs={{0,4},{1,5},{4,8},{5,9},{8,12},{9,13},{12,14},{13,15},{14,10},{15,... | collective-permute-start | bytes 786440 | tf_op jit(solution)/shard_map/ppermute | solution.py:52
  97.9 11.1 %collective-permute-start.31 = (bf16[64,2048]{1,0:T(8,128)(2,1)S(1)}, bf16[64,2048]{1,0:T(8,128)(2,1)S(1)}, u32[]{:S(2)}, u32[]{:S(2)}) collective-permute-start(bf16[64,2048]{1,0:T(8,128)(2,1)S(1)} %add_convert_fusion.9), channel_id=1, source_target_pairs={{0,2},{1,3},{4,0},{5,1},{8,4},{9,5},{12,8},{13,9},{14,12},{15,13},... | collective-permute-start | bytes 786440 | tf_op jit(solution)/shard_map/ppermute | solution.py:52
  103.4 13.8 %collective-permute-start.35 = (bf16[64,2048]{1,0:T(8,128)(2,1)S(1)}, bf16[64,2048]{1,0:T(8,128)(2,1)S(1)}, u32[]{:S(2)}, u32[]{:S(2)}) collective-permute-start(bf16[64,2048]{1,0:T(8,128)(2,1)S(1)} %add_convert_fusion.5), channel_id=1, source_target_pairs={{0,2},{1,3},{4,0},{5,1},{8,4},{9,5},{12,8},{13,9},{14,12},{15,13},... | collective-permute-start | bytes 786440 | tf_op jit(solution)/shard_map/ppermute | solution.py:52
  103.9 7.2 %collective-permute-start.38 = (bf16[64,2048]{1,0:T(8,128)(2,1)S(1)}, bf16[64,2048]{1,0:T(8,128)(2,1)S(1)}, u32[]{:S(2)}, u32[]{:S(2)}) collective-permute-start(bf16[64,2048]{1,0:T(8,128)(2,1)S(1)} %add_convert_fusion.3), channel_id=1, source_target_pairs={{0,4},{1,5},{4,8},{5,9},{8,12},{9,13},{12,14},{13,15},{14,10},{15,... | collective-permute-start | bytes 786440 | tf_op jit(solution)/shard_map/ppermute | solution.py:52
  109.0 8.1 %collective-permute-start.32 = (bf16[64,2048]{1,0:T(8,128)(2,1)S(1)}, bf16[64,2048]{1,0:T(8,128)(2,1)S(1)}, u32[]{:S(2)}, u32[]{:S(2)}) collective-permute-start(bf16[64,2048]{1,0:T(8,128)(2,1)S(1)} %add_convert_fusion.8), channel_id=1, source_target_pairs={{0,2},{1,3},{4,0},{5,1},{8,4},{9,5},{12,8},{13,9},{14,12},{15,13},... | collective-permute-start | bytes 786440 | tf_op jit(solution)/shard_map/ppermute | solution.py:52
  111.1 6.4 %collective-permute-start.39 = (bf16[64,2048]{1,0:T(8,128)(2,1)S(1)}, bf16[64,2048]{1,0:T(8,128)(2,1)S(1)}, u32[]{:S(2)}, u32[]{:S(2)}) collective-permute-start(bf16[64,2048]{1,0:T(8,128)(2,1)S(1)} %add_convert_fusion.2), channel_id=1, source_target_pairs={{0,4},{1,5},{4,8},{5,9},{8,12},{9,13},{12,14},{13,15},{14,10},{15,... | collective-permute-start | bytes 786440 | tf_op jit(solution)/shard_map/ppermute | solution.py:52
  (11 other events, 88.6 us)

commit v4 on v3

--- a/solution.py
+++ b/solution.py
@@ -368,7 +368,7 @@
             mates[block] = ring.go_mate(held[block])
         for hops, source in phase:
             held[hops] = ring.go_split(held[source], hops - source)
-        held, mates, extras = lax.optimization_barrier((held, mates, extras))
+    held[1], extras = hold(held[1], extras)
     for hops in range(1, half):
         if hops not in mates:
             mates[hops] = ring.go_mate(held[hops])

time: 119 us -> 119 us (level)
  waiting for transfers between devices: 46.3 us -> 44.4 us
  starting transfers between devices: 37 us -> 38.8 us
    ppermute x4, waiting for transfers between devices: 7.25 us -> 4.69 us  [go_split(): return lax.ppermute(block, 'ctx', pairs)]
    ppermute x28, waiting for transfers between devices: 34.5 us -> 36.1 us  [go(): return lax.ppermute(block, 'ctx', pairs)]
  transfers between devices with their start and end apart: 40 -> 40, of which waited for: 18 -> 21; matrix products, arithmetic and copies ran while one was open for 2% -> 2% of each run, Pallas kernels for 22% -> 22%
where the time goes in v4:
time: 119 us
  waiting for transfers between devices  44.4 us (37%)
  starting transfers between devices  38.8 us (33%)
  Pallas kernels  32 us (27%)
  other arithmetic  2.63 us (2%)
    ppermute x28, waiting for transfers between devices, go(): return lax.ppermute(block, 'ctx', pairs)  36.1 us
    ppermute x28, starting transfers between devices, go(): return lax.ppermute(block, 'ctx', pairs)  28.9 us
    pallas_call x4, Pallas kernels, ffn(): pl.pallas_call(functools.partial(ffn_kernel, count), out_shape=tuple((jax...  19.4 us
    pallas_call x3, Pallas kernels, load(): pl.pallas_call(functools.partial(load_kernel, count), out_shape=tuple((pl...  8.43 us
    ppermute x4, starting transfers between devices, go_split(): return lax.ppermute(block, 'ctx', pairs)  7.7 us
    ppermute x4, waiting for transfers between devices, go_split(): return lax.ppermute(block, 'ctx', pairs)  4.69 us
    ppermute x8, waiting for transfers between devices, go_mate(): return lax.ppermute(block, 'ctx', self.swap)  3.64 us
    pallas_call x1, Pallas kernels, attend(): pl.pallas_call(functools.partial(attention_kernel, len(blocks), heads, he...  3.36 us
  transfers between devices with their start and end apart: 40, of which 21 were waited for; matrix products, arithmetic and copies ran while one was open for 2% of the time, Pallas kernels for 22%

profile of v4, /device:TPU:0, one launch (start us, length us, event | category | flops | bytes accessed | tf_op | source)
XLA Modules:
  0.0 118.8 jit_solution(4392310733057347589)
XLA Ops:
  3.3 2.7 %collective-permute-start.2 = (bf16[512,128]{1,0:T(8,128)(2,1)S(1)}, bf16[512,128]{1,0:T(8,128)(2,1)S(1)}, u32[]{:S(2)}, u32[]{:S(2)}) collective-permute-start(bf16[512,128]{1,0:T(8,128)(2,1)S(1)} %join.1.refs_0_), channel_id=1, source_target_pairs={{0,4},{1,3},{4,8},{5,1},{8,12},{9,5},{12,14},{13,9},{14,10},{15,13... | collective-permute-start | bytes 393224 | tf_op jit(solution)/shard_map/ppermute | solution.py:63
  6.0 3.5 %collective-permute-start.6 = (bf16[512,128]{1,0:T(8,128)(2,1)S(1)}, bf16[512,128]{1,0:T(8,128)(2,1)S(1)}, u32[]{:S(2)}, u32[]{:S(2)}) collective-permute-start(bf16[512,128]{1,0:T(8,128)(2,1)S(1)} %join.1.refs_0_), channel_id=1, source_target_pairs={{0,12},{1,11},{4,14},{5,7},{8,10},{9,3},{12,6},{13,1},{14,2},{15,5... | collective-permute-start | bytes 393224 | tf_op jit(solution)/shard_map/ppermute | solution.py:63
  9.6 1.4 %collective-permute-start.5 = (bf16[512,128]{1,0:T(8,128)(2,1)S(1)}, bf16[512,128]{1,0:T(8,128)(2,1)S(1)}, u32[]{:S(2)}, u32[]{:S(2)}) collective-permute-start(bf16[512,128]{1,0:T(8,128)(2,1)S(1)} %collective-permute-done.2.refs_1_), channel_id=1, source_target_pairs={{0,4},{1,3},{4,8},{5,1},{8,12},{9,5},{12,14},{13,9},{14,10},{15,13... | collective-permute-start | bytes 393224 | tf_op jit(solution)/shard_map/ppermute | solution.py:63
  11.0 4.7 %collective-permute-done.6.refs_3_ = bf16[512,128]{1,0:T(8,128)(2,1)S(1)} collective-permute-done((bf16[512,128]{1,0:T(8,128)(2,1)S(1)}, bf16[512,128]{1,0:T(8,128)(2,1)S(1)}, u32[]{:S(2)}, u32[]{:S(2)}) %collective-permute-start.6) | collective-permute-done | bytes 131104 | tf_op jit(solution)/shard_map/ppermute | solution.py:63
  17.9 2.7 %load.3 = (bf16[128,1024]{1,0:T(8,128)(2,1)S(1)}, s32[16,128]{1,0:T(8,128)S(1)}, s32[16,128]{1,0:T(8,128)S(1)}, bf16[128,2048]{1,0:T(8,128)(2,1)S(1)}, f32[1,204...) custom-call(bf16[128,1024]{1,0:T(8,128)(2,1)} %refs_0_.3, s32[16,128]{1,0:T(8,128)} %bitcast.7, s32[16,128]{1,0:T(8,128)} %bitcast.9, ...), custom_call_target="tpu_custom_call" | custom-call | tf_op jit(solution)/shard_map/load/pallas_call | solution.py:221
  21.8 3.4 %attention.1 = (bf16[64,2048]{1,0:T(8,128)(2,1)S(1)}, bf16[64,2048]{1,0:T(8,128)(2,1)S(1)}, bf16[128,2048]{1,0:T(8,128)(2,1)S(1)}) custom-call(s32[16]{0:T(128)S(1)} %dynamic-slice_bitcast_fusion.owner_ref, s32[16,128]{1,0:T(8,128)S(1)} %bitcast.8, s32[16,128]{1,0:T(8,128)S(1)} %bitcast.10, bf16[128,1024]{1,0:T(8,128)(2,1)S(1)} %get-tuple-element.101.query_ref, ...), custom_call_target="tpu_custom_call" | custom-call | tf_op jit(solution)/shard_map/attention/pallas_call | solution.py:192
  25.1 1.5 %collective-permute-done.11.refs_2_ = bf16[688,2048]{1,0:T(8,128)(2,1)S(1)} collective-permute-done((bf16[688,2048]{1,0:T(8,128)(2,1)S(1)}, bf16[688,2048]{1,0:T(8,128)(2,1)S(1)}, u32[]{:S(2)}, u32[]{:S(2)}) %collective-permute-start.11) | collective-permute-done | bytes 2818080 | tf_op jit(solution)/shard_map/ppermute | solution.py:55
  30.7 2.2 %load.5 = (bf16[688,2048]{1,0:T(8,128)(2,1)S(1)}, bf16[688,2048]{1,0:T(8,128)(2,1)S(1)}, bf16[688,2048]{1,0:T(8,128)(2,1)S(1)}) custom-call(bf16[688,2048]{1,0:T(8,128)(2,1)S(1)} %collective-permute-done.3.refs_0_, bf16[688,2048]{1,0:T(8,128)(2,1)} %collective-permute-done.4.refs_1_, bf16[688,2048]{1,0:T(8,128)(2,1)S(1)} %collective-permute-done.11.refs_2_), custom_call_target="tpu_custom_call" | custom-call | tf_op jit(solution)/shard_map/load/pallas_call | solution.py:221
  32.9 3.5 %load.4 = (bf16[688,2048]{1,0:T(8,128)(2,1)S(1)}, bf16[688,2048]{1,0:T(8,128)(2,1)S(1)}, bf16[688,2048]{1,0:T(8,128)(2,1)S(1)}) custom-call(bf16[688,2048]{1,0:T(8,128)(2,1)} %bitcast.12, bf16[688,2048]{1,0:T(8,128)(2,1)} %bitcast.14, bf16[688,2048]{1,0:T(8,128)(2,1)} %refs_2_), custom_call_target="tpu_custom_call" | custom-call | tf_op jit(solution)/shard_map/load/pallas_call | solution.py:221
  36.9 2.1 %collective-permute-start.16 = (bf16[64,2048]{1,0:T(8,128)(2,1)S(1)}, bf16[64,2048]{1,0:T(8,128)(2,1)S(1)}, u32[]{:S(2)}, u32[]{:S(2)}) collective-permute-start(bf16[64,2048]{1,0:T(8,128)(2,1)S(1)} %collective-permute-done.12.refs_0_), channel_id=1, source_target_pairs={{0,4},{1,5},{4,8},{5,9},{8,12},{9,13},{12,14},{13,15},{14,10},{15,... | collective-permute-start | bytes 786440 | tf_op jit(solution)/shard_map/ppermute | solution.py:52
  39.0 4.8 %feed_forward.4 = (bf16[64,2048]{1,0:T(8,128)(2,1)S(1)}, bf16[64,2048]{1,0:T(8,128)(2,1)S(1)}, bf16[64,2048]{1,0:T(8,128)(2,1)S(1)}, bf16[64,2048]{1,0:T(8,128)(2,1)S(1)}) custom-call(bf16[64,2048]{1,0:T(8,128)(2,1)S(1)} %collective-permute-done.12.refs_0_, bf16[64,2048]{1,0:T(8,128)(2,1)S(1)} %collective-permute-done.13.refs_1_, ...), custom_call_target="tpu_custom_call" | custom-call | flops 1000 | bytes 1000 | tf_op jit(solution)/shard_map/feed_forward/pallas_call | solution.py:285
  43.9 2.1 %collective-permute-start.22 = (bf16[64,2048]{1,0:T(8,128)(2,1)S(1)}, bf16[64,2048]{1,0:T(8,128)(2,1)S(1)}, u32[]{:S(2)}, u32[]{:S(2)}) collective-permute-start(bf16[64,2048]{1,0:T(8,128)(2,1)S(1)} %collective-permute-done.14.refs_2_), channel_id=1, source_target_pairs={{0,4},{1,5},{4,8},{5,9},{8,12},{9,13},{12,14},{13,15},{14,10},{15,... | collective-permute-start | bytes 786440 | tf_op jit(solution)/shard_map/ppermute | solution.py:52
  49.0 4.9 %feed_forward.6 = (bf16[64,2048]{1,0:T(8,128)(2,1)S(1)}, bf16[64,2048]{1,0:T(8,128)(2,1)S(1)}, bf16[64,2048]{1,0:T(8,128)(2,1)S(1)}, bf16[64,2048]{1,0:T(8,128)(2,1)S(1)}) custom-call(bf16[64,2048]{1,0:T(8,128)(2,1)S(1)} %collective-permute-done.16.refs_0_, bf16[64,2048]{1,0:T(8,128)(2,1)S(1)} %collective-permute-done.19.refs_1_, ...), custom_call_target="tpu_custom_call" | custom-call | flops 1000 | bytes 1000 | tf_op jit(solution)/shard_map/feed_forward/pallas_call | solution.py:285
  57.2 1.6 %collective-permute-done.17.refs_0_ = bf16[64,2048]{1,0:T(8,128)(2,1)S(1)} collective-permute-done((bf16[64,2048]{1,0:T(8,128)(2,1)S(1)}, bf16[64,2048]{1,0:T(8,128)(2,1)S(1)}, u32[]{:S(2)}, u32[]{:S(2)}) %collective-permute-start.17) | collective-permute-done | bytes 262176 | tf_op jit(solution)/shard_map/ppermute | solution.py:52
  58.8 1.5 %collective-permute-start.18 = (bf16[64,2048]{1,0:T(8,128)(2,1)S(1)}, bf16[64,2048]{1,0:T(8,128)(2,1)S(1)}, u32[]{:S(2)}, u32[]{:S(2)}) collective-permute-start(bf16[64,2048]{1,0:T(8,128)(2,1)S(1)} %collective-permute-done.17.refs_0_), channel_id=1, source_target_pairs={{0,4},{1,5},{4,8},{5,9},{8,12},{9,13},{12,14},{13,15},{14,10},{15,... | collective-permute-start | bytes 786440 | tf_op jit(solution)/shard_map/ppermute | solution.py:52
  60.8 4.8 %feed_forward.5 = (bf16[64,2048]{1,0:T(8,128)(2,1)S(1)}, bf16[64,2048]{1,0:T(8,128)(2,1)S(1)}, bf16[64,2048]{1,0:T(8,128)(2,1)S(1)}, bf16[64,2048]{1,0:T(8,128)(2,1)S(1)}) custom-call(bf16[64,2048]{1,0:T(8,128)(2,1)S(1)} %collective-permute-done.17.refs_0_, bf16[64,2048]{1,0:T(8,128)(2,1)S(1)} %collective-permute-done.20.refs_1_, ...), custom_call_target="tpu_custom_call" | custom-call | flops 1000 | bytes 1000 | tf_op jit(solution)/shard_map/feed_forward/pallas_call | solution.py:285
  66.4 2.5 %collective-permute-done.18.refs_0_ = bf16[64,2048]{1,0:T(8,128)(2,1)S(1)} collective-permute-done((bf16[64,2048]{1,0:T(8,128)(2,1)S(1)}, bf16[64,2048]{1,0:T(8,128)(2,1)S(1)}, u32[]{:S(2)}, u32[]{:S(2)}) %collective-permute-start.18) | collective-permute-done | bytes 262176 | tf_op jit(solution)/shard_map/ppermute | solution.py:52
  68.9 1.4 %collective-permute-done.21.refs_1_ = bf16[64,2048]{1,0:T(8,128)(2,1)S(1)} collective-permute-done((bf16[64,2048]{1,0:T(8,128)(2,1)S(1)}, bf16[64,2048]{1,0:T(8,128)(2,1)S(1)}, u32[]{:S(2)}, u32[]{:S(2)}) %collective-permute-start.21) | collective-permute-done | bytes 262176 | tf_op jit(solution)/shard_map/ppermute | solution.py:52
  70.2 4.8 %feed_forward.7 = (bf16[64,2048]{1,0:T(8,128)(2,1)S(1)}, bf16[64,2048]{1,0:T(8,128)(2,1)S(1)}, bf16[64,2048]{1,0:T(8,128)(2,1)S(1)}, bf16[64,2048]{1,0:T(8,128)(2,1)S(1)}) custom-call(bf16[64,2048]{1,0:T(8,128)(2,1)S(1)} %collective-permute-done.18.refs_0_, bf16[64,2048]{1,0:T(8,128)(2,1)S(1)} %collective-permute-done.21.refs_1_, ...), custom_call_target="tpu_custom_call" | custom-call | flops 1000 | bytes 1000 | tf_op jit(solution)/shard_map/feed_forward/pallas_call | solution.py:285
  75.1 1.8 %collective-permute-start.26 = (bf16[64,2048]{1,0:T(8,128)(2,1)S(1)}, bf16[64,2048]{1,0:T(8,128)(2,1)S(1)}, u32[]{:S(2)}, u32[]{:S(2)}) collective-permute-start(bf16[64,2048]{1,0:T(8,128)(2,1)S(1)} %get-tuple-element.165), channel_id=1, source_target_pairs={{0,4},{1,5},{4,8},{5,9},{8,12},{9,13},{12,14},{13,15},{14,10},{15,... | collective-permute-start | bytes 786440 | tf_op jit(solution)/shard_map/ppermute | solution.py:52
  77.6 1.6 %collective-permute-start.36 = (bf16[64,2048]{1,0:T(8,128)(2,1)S(1)}, bf16[64,2048]{1,0:T(8,128)(2,1)S(1)}, u32[]{:S(2)}, u32[]{:S(2)}) collective-permute-start(bf16[64,2048]{1,0:T(8,128)(2,1)S(1)} %get-tuple-element.176), channel_id=1, source_target_pairs={{0,4},{1,5},{4,8},{5,9},{8,12},{9,13},{12,14},{13,15},{14,10},{15,... | collective-permute-start | bytes 786440 | tf_op jit(solution)/shard_map/ppermute | solution.py:52
  79.2 5.2 %collective-permute-done.26 = bf16[64,2048]{1,0:T(8,128)(2,1)S(1)} collective-permute-done((bf16[64,2048]{1,0:T(8,128)(2,1)S(1)}, bf16[64,2048]{1,0:T(8,128)(2,1)S(1)}, u32[]{:S(2)}, u32[]{:S(2)}) %collective-permute-start.26) | collective-permute-done | bytes 262176 | tf_op jit(solution)/shard_map/ppermute | solution.py:52
  84.5 1.8 %collective-permute-start.27 = (bf16[64,2048]{1,0:T(8,128)(2,1)S(1)}, bf16[64,2048]{1,0:T(8,128)(2,1)S(1)}, u32[]{:S(2)}, u32[]{:S(2)}) collective-permute-start(bf16[64,2048]{1,0:T(8,128)(2,1)S(1)} %add_convert_fusion.12), channel_id=1, source_target_pairs={{0,4},{1,5},{4,8},{5,9},{8,12},{9,13},{12,14},{13,15},{14,10},{15,... | collective-permute-start | bytes 786440 | tf_op jit(solution)/shard_map/ppermute | solution.py:52
  86.7 5.1 %collective-permute-done.33 = bf16[64,2048]{1,0:T(8,128)(2,1)S(1)} collective-permute-done((bf16[64,2048]{1,0:T(8,128)(2,1)S(1)}, bf16[64,2048]{1,0:T(8,128)(2,1)S(1)}, u32[]{:S(2)}, u32[]{:S(2)}) %collective-permute-start.33) | collective-permute-done | bytes 262176 | tf_op jit(solution)/shard_map/ppermute | solution.py:52
  92.2 1.8 %collective-permute-start.37 = (bf16[64,2048]{1,0:T(8,128)(2,1)S(1)}, bf16[64,2048]{1,0:T(8,128)(2,1)S(1)}, u32[]{:S(2)}, u32[]{:S(2)}) collective-permute-start(bf16[64,2048]{1,0:T(8,128)(2,1)S(1)} %add_convert_fusion.4), channel_id=1, source_target_pairs={{0,4},{1,5},{4,8},{5,9},{8,12},{9,13},{12,14},{13,15},{14,10},{15,... | collective-permute-start | bytes 786440 | tf_op jit(solution)/shard_map/ppermute | solution.py:52
  94.0 1.6 %collective-permute-done.27 = bf16[64,2048]{1,0:T(8,128)(2,1)S(1)} collective-permute-done((bf16[64,2048]{1,0:T(8,128)(2,1)S(1)}, bf16[64,2048]{1,0:T(8,128)(2,1)S(1)}, u32[]{:S(2)}, u32[]{:S(2)}) %collective-permute-start.27) | collective-permute-done | bytes 262176 | tf_op jit(solution)/shard_map/ppermute | solution.py:52
  95.7 1.8 %collective-permute-start.28 = (bf16[64,2048]{1,0:T(8,128)(2,1)S(1)}, bf16[64,2048]{1,0:T(8,128)(2,1)S(1)}, u32[]{:S(2)}, u32[]{:S(2)}) collective-permute-start(bf16[64,2048]{1,0:T(8,128)(2,1)S(1)} %add_convert_fusion.11), channel_id=1, source_target_pairs={{0,4},{1,5},{4,8},{5,9},{8,12},{9,13},{12,14},{13,15},{14,10},{15,... | collective-permute-start | bytes 786440 | tf_op jit(solution)/shard_map/ppermute | solution.py:52
  97.9 5.1 %collective-permute-done.34 = bf16[64,2048]{1,0:T(8,128)(2,1)S(1)} collective-permute-done((bf16[64,2048]{1,0:T(8,128)(2,1)S(1)}, bf16[64,2048]{1,0:T(8,128)(2,1)S(1)}, u32[]{:S(2)}, u32[]{:S(2)}) %collective-permute-start.34) | collective-permute-done | bytes 262176 | tf_op jit(solution)/shard_map/ppermute | solution.py:52
  103.5 1.8 %collective-permute-start.38 = (bf16[64,2048]{1,0:T(8,128)(2,1)S(1)}, bf16[64,2048]{1,0:T(8,128)(2,1)S(1)}, u32[]{:S(2)}, u32[]{:S(2)}) collective-permute-start(bf16[64,2048]{1,0:T(8,128)(2,1)S(1)} %add_convert_fusion.3), channel_id=1, source_target_pairs={{0,4},{1,5},{4,8},{5,9},{8,12},{9,13},{12,14},{13,15},{14,10},{15,... | collective-permute-start | bytes 786440 | tf_op jit(solution)/shard_map/ppermute | solution.py:52
  105.3 3.3 %collective-permute-done.31 = bf16[64,2048]{1,0:T(8,128)(2,1)S(1)} collective-permute-done((bf16[64,2048]{1,0:T(8,128)(2,1)S(1)}, bf16[64,2048]{1,0:T(8,128)(2,1)S(1)}, u32[]{:S(2)}, u32[]{:S(2)}) %collective-permute-start.31) | collective-permute-done | bytes 262176 | tf_op jit(solution)/shard_map/ppermute | solution.py:52
  110.0 2.4 %collective-permute-start.39 = (bf16[64,2048]{1,0:T(8,128)(2,1)S(1)}, bf16[64,2048]{1,0:T(8,128)(2,1)S(1)}, u32[]{:S(2)}, u32[]{:S(2)}) collective-permute-start(bf16[64,2048]{1,0:T(8,128)(2,1)S(1)} %add_convert_fusion.2), channel_id=1, source_target_pairs={{0,4},{1,5},{4,8},{5,9},{8,12},{9,13},{12,14},{13,15},{14,10},{15,... | collective-permute-start | bytes 786440 | tf_op jit(solution)/shard_map/ppermute | solution.py:52
  112.3 5.2 %collective-permute-done.32 = bf16[64,2048]{1,0:T(8,128)(2,1)S(1)} collective-permute-done((bf16[64,2048]{1,0:T(8,128)(2,1)S(1)}, bf16[64,2048]{1,0:T(8,128)(2,1)S(1)}, u32[]{:S(2)}, u32[]{:S(2)}) %collective-permute-start.32) | collective-permute-done | bytes 262176 | tf_op jit(solution)/shard_map/ppermute | solution.py:52
  (78 shorter events, 23.9 us)
Async XLA Ops:
  2.7 18.6 %collective-permute-start.3 = (bf16[688,2048]{1,0:T(8,128)(2,1)}, bf16[688,2048]{1,0:T(8,128)(2,1)S(1)}, u32[]{:S(2)}, u32[]{:S(2)}) collective-permute-start(bf16[688,2048]{1,0:T(8,128)(2,1)} %bitcast.11), channel_id=1, source_target_pairs={{0,1},{1,0},{2,3},{3,2},{4,5},{5,4},{6,7},{7,6},{8,9},{9,8},{10,11... | collective-permute-start | bytes 8454152 | tf_op jit(solution)/shard_map/ppermute | solution.py:55
  2.9 18.4 %collective-permute-start.4 = (bf16[688,2048]{1,0:T(8,128)(2,1)}, bf16[688,2048]{1,0:T(8,128)(2,1)}, u32[]{:S(2)}, u32[]{:S(2)}) collective-permute-start(bf16[688,2048]{1,0:T(8,128)(2,1)} %bitcast.13), channel_id=1, source_target_pairs={{0,1},{1,0},{2,3},{3,2},{4,5},{5,4},{6,7},{7,6},{8,9},{9,8},{10,11... | collective-permute-start | bytes 8454152 | tf_op jit(solution)/shard_map/ppermute | solution.py:55
  3.3 6.3 %collective-permute-start.2 = (bf16[512,128]{1,0:T(8,128)(2,1)S(1)}, bf16[512,128]{1,0:T(8,128)(2,1)S(1)}, u32[]{:S(2)}, u32[]{:S(2)}) collective-permute-start(bf16[512,128]{1,0:T(8,128)(2,1)S(1)} %join.1.refs_0_), channel_id=1, source_target_pairs={{0,4},{1,3},{4,8},{5,1},{8,12},{9,5},{12,14},{13,9},{14,10},{15,13... | collective-permute-start | bytes 393224 | tf_op jit(solution)/shard_map/ppermute | solution.py:63
  6.0 9.6 %collective-permute-start.6 = (bf16[512,128]{1,0:T(8,128)(2,1)S(1)}, bf16[512,128]{1,0:T(8,128)(2,1)S(1)}, u32[]{:S(2)}, u32[]{:S(2)}) collective-permute-start(bf16[512,128]{1,0:T(8,128)(2,1)S(1)} %join.1.refs_0_), channel_id=1, source_target_pairs={{0,12},{1,11},{4,14},{5,7},{8,10},{9,3},{12,6},{13,1},{14,2},{15,5... | collective-permute-start | bytes 393224 | tf_op jit(solution)/shard_map/ppermute | solution.py:63
  26.6 9.8 %collective-permute-start.12 = (bf16[64,2048]{1,0:T(8,128)(2,1)S(1)}, bf16[64,2048]{1,0:T(8,128)(2,1)S(1)}, u32[]{:S(2)}, u32[]{:S(2)}) collective-permute-start(bf16[64,2048]{1,0:T(8,128)(2,1)S(1)} %get-tuple-element.136.refs_2_), channel_id=1, source_target_pairs={{0,4},{1,5},{4,8},{5,9},{8,12},{9,13},{12,14},{13,15},{14,10},{15,... | collective-permute-start | bytes 786440 | tf_op jit(solution)/shard_map/ppermute | solution.py:52
  27.5 9.4 %collective-permute-start.13 = (bf16[64,2048]{1,0:T(8,128)(2,1)S(1)}, bf16[64,2048]{1,0:T(8,128)(2,1)S(1)}, u32[]{:S(2)}, u32[]{:S(2)}) collective-permute-start(bf16[64,2048]{1,0:T(8,128)(2,1)S(1)} %get-tuple-element.137.refs_3_), channel_id=1, source_target_pairs={{0,2},{1,3},{4,0},{5,1},{8,4},{9,5},{12,8},{13,9},{14,12},{15,13},... | collective-permute-start | bytes 786440 | tf_op jit(solution)/shard_map/ppermute | solution.py:52
  28.6 15.2 %collective-permute-start.14 = (bf16[64,2048]{1,0:T(8,128)(2,1)S(1)}, bf16[64,2048]{1,0:T(8,128)(2,1)S(1)}, u32[]{:S(2)}, u32[]{:S(2)}) collective-permute-start(bf16[64,2048]{1,0:T(8,128)(2,1)S(1)} %get-tuple-element.137.refs_3_), channel_id=1, source_target_pairs={{0,4},{1,5},{4,8},{5,9},{8,12},{9,13},{12,14},{13,15},{14,10},{15,... | collective-permute-start | bytes 786440 | tf_op jit(solution)/shard_map/ppermute | solution.py:52
  29.9 14.0 %collective-permute-start.15 = (bf16[64,2048]{1,0:T(8,128)(2,1)S(1)}, bf16[64,2048]{1,0:T(8,128)(2,1)S(1)}, u32[]{:S(2)}, u32[]{:S(2)}) collective-permute-start(bf16[64,2048]{1,0:T(8,128)(2,1)S(1)} %get-tuple-element.136.refs_2_), channel_id=1, source_target_pairs={{0,2},{1,3},{4,0},{5,1},{8,4},{9,5},{12,8},{13,9},{14,12},{15,13},... | collective-permute-start | bytes 786440 | tf_op jit(solution)/shard_map/ppermute | solution.py:52
  36.9 10.0 %collective-permute-start.16 = (bf16[64,2048]{1,0:T(8,128)(2,1)S(1)}, bf16[64,2048]{1,0:T(8,128)(2,1)S(1)}, u32[]{:S(2)}, u32[]{:S(2)}) collective-permute-start(bf16[64,2048]{1,0:T(8,128)(2,1)S(1)} %collective-permute-done.12.refs_0_), channel_id=1, source_target_pairs={{0,4},{1,5},{4,8},{5,9},{8,12},{9,13},{12,14},{13,15},{14,10},{15,... | collective-permute-start | bytes 786440 | tf_op jit(solution)/shard_map/ppermute | solution.py:52
  39.0 9.2 %collective-permute-start.19 = (bf16[64,2048]{1,0:T(8,128)(2,1)S(1)}, bf16[64,2048]{1,0:T(8,128)(2,1)S(1)}, u32[]{:S(2)}, u32[]{:S(2)}) collective-permute-start(bf16[64,2048]{1,0:T(8,128)(2,1)S(1)} %collective-permute-done.13.refs_1_), channel_id=1, source_target_pairs={{0,2},{1,3},{4,0},{5,1},{8,4},{9,5},{12,8},{13,9},{14,12},{15,13},... | collective-permute-start | bytes 786440 | tf_op jit(solution)/shard_map/ppermute | solution.py:52
  43.9 10.0 %collective-permute-start.22 = (bf16[64,2048]{1,0:T(8,128)(2,1)S(1)}, bf16[64,2048]{1,0:T(8,128)(2,1)S(1)}, u32[]{:S(2)}, u32[]{:S(2)}) collective-permute-start(bf16[64,2048]{1,0:T(8,128)(2,1)S(1)} %collective-permute-done.14.refs_2_), channel_id=1, source_target_pairs={{0,4},{1,5},{4,8},{5,9},{8,12},{9,13},{12,14},{13,15},{14,10},{15,... | collective-permute-start | bytes 786440 | tf_op jit(solution)/shard_map/ppermute | solution.py:52
  45.9 9.2 %collective-permute-start.23 = (bf16[64,2048]{1,0:T(8,128)(2,1)S(1)}, bf16[64,2048]{1,0:T(8,128)(2,1)S(1)}, u32[]{:S(2)}, u32[]{:S(2)}) collective-permute-start(bf16[64,2048]{1,0:T(8,128)(2,1)S(1)} %collective-permute-done.15.refs_3_), channel_id=1, source_target_pairs={{0,2},{1,3},{4,0},{5,1},{8,4},{9,5},{12,8},{13,9},{14,12},{15,13},... | collective-permute-start | bytes 786440 | tf_op jit(solution)/shard_map/ppermute | solution.py:52
  47.0 11.8 %collective-permute-start.17 = (bf16[64,2048]{1,0:T(8,128)(2,1)S(1)}, bf16[64,2048]{1,0:T(8,128)(2,1)S(1)}, u32[]{:S(2)}, u32[]{:S(2)}) collective-permute-start(bf16[64,2048]{1,0:T(8,128)(2,1)S(1)} %collective-permute-done.16.refs_0_), channel_id=1, source_target_pairs={{0,4},{1,5},{4,8},{5,9},{8,12},{9,13},{12,14},{13,15},{14,10},{15,... | collective-permute-start | bytes 786440 | tf_op jit(solution)/shard_map/ppermute | solution.py:52
  48.2 12.6 %collective-permute-start.20 = (bf16[64,2048]{1,0:T(8,128)(2,1)S(1)}, bf16[64,2048]{1,0:T(8,128)(2,1)S(1)}, u32[]{:S(2)}, u32[]{:S(2)}) collective-permute-start(bf16[64,2048]{1,0:T(8,128)(2,1)S(1)} %collective-permute-done.19.refs_1_), channel_id=1, source_target_pairs={{0,2},{1,3},{4,0},{5,1},{8,4},{9,5},{12,8},{13,9},{14,12},{15,13},... | collective-permute-start | bytes 786440 | tf_op jit(solution)/shard_map/ppermute | solution.py:52
  55.2 10.5 %collective-permute-start.24 = (bf16[64,2048]{1,0:T(8,128)(2,1)S(1)}, bf16[64,2048]{1,0:T(8,128)(2,1)S(1)}, u32[]{:S(2)}, u32[]{:S(2)}) collective-permute-start(bf16[64,2048]{1,0:T(8,128)(2,1)S(1)} %collective-permute-done.22.refs_2_), channel_id=1, source_target_pairs={{0,4},{1,5},{4,8},{5,9},{8,12},{9,13},{12,14},{13,15},{14,10},{15,... | collective-permute-start | bytes 786440 | tf_op jit(solution)/shard_map/ppermute | solution.py:52
  56.2 10.2 %collective-permute-start.25 = (bf16[64,2048]{1,0:T(8,128)(2,1)S(1)}, bf16[64,2048]{1,0:T(8,128)(2,1)S(1)}, u32[]{:S(2)}, u32[]{:S(2)}) collective-permute-start(bf16[64,2048]{1,0:T(8,128)(2,1)S(1)} %collective-permute-done.23.refs_3_), channel_id=1, source_target_pairs={{0,2},{1,3},{4,0},{5,1},{8,4},{9,5},{12,8},{13,9},{14,12},{15,13},... | collective-permute-start | bytes 786440 | tf_op jit(solution)/shard_map/ppermute | solution.py:52
  58.8 10.1 %collective-permute-start.18 = (bf16[64,2048]{1,0:T(8,128)(2,1)S(1)}, bf16[64,2048]{1,0:T(8,128)(2,1)S(1)}, u32[]{:S(2)}, u32[]{:S(2)}) collective-permute-start(bf16[64,2048]{1,0:T(8,128)(2,1)S(1)} %collective-permute-done.17.refs_0_), channel_id=1, source_target_pairs={{0,4},{1,5},{4,8},{5,9},{8,12},{9,13},{12,14},{13,15},{14,10},{15,... | collective-permute-start | bytes 786440 | tf_op jit(solution)/shard_map/ppermute | solution.py:52
  60.8 9.4 %collective-permute-start.21 = (bf16[64,2048]{1,0:T(8,128)(2,1)S(1)}, bf16[64,2048]{1,0:T(8,128)(2,1)S(1)}, u32[]{:S(2)}, u32[]{:S(2)}) collective-permute-start(bf16[64,2048]{1,0:T(8,128)(2,1)S(1)} %collective-permute-done.20.refs_1_), channel_id=1, source_target_pairs={{0,2},{1,3},{4,0},{5,1},{8,4},{9,5},{12,8},{13,9},{14,12},{15,13},... | collective-permute-start | bytes 786440 | tf_op jit(solution)/shard_map/ppermute | solution.py:52
  75.1 9.3 %collective-permute-start.26 = (bf16[64,2048]{1,0:T(8,128)(2,1)S(1)}, bf16[64,2048]{1,0:T(8,128)(2,1)S(1)}, u32[]{:S(2)}, u32[]{:S(2)}) collective-permute-start(bf16[64,2048]{1,0:T(8,128)(2,1)S(1)} %get-tuple-element.165), channel_id=1, source_target_pairs={{0,4},{1,5},{4,8},{5,9},{8,12},{9,13},{12,14},{13,15},{14,10},{15,... | collective-permute-start | bytes 786440 | tf_op jit(solution)/shard_map/ppermute | solution.py:52
  76.9 9.4 %collective-permute-start.29 = (bf16[64,2048]{1,0:T(8,128)(2,1)S(1)}, bf16[64,2048]{1,0:T(8,128)(2,1)S(1)}, u32[]{:S(2)}, u32[]{:S(2)}) collective-permute-start(bf16[64,2048]{1,0:T(8,128)(2,1)S(1)} %get-tuple-element.168), channel_id=1, source_target_pairs={{0,2},{1,3},{4,0},{5,1},{8,4},{9,5},{12,8},{13,9},{14,12},{15,13},... | collective-permute-start | bytes 786440 | tf_op jit(solution)/shard_map/ppermute | solution.py:52
  77.2 14.6 %collective-permute-start.33 = (bf16[64,2048]{1,0:T(8,128)(2,1)S(1)}, bf16[64,2048]{1,0:T(8,128)(2,1)S(1)}, u32[]{:S(2)}, u32[]{:S(2)}) collective-permute-start(bf16[64,2048]{1,0:T(8,128)(2,1)S(1)} %get-tuple-element.173), channel_id=1, source_target_pairs={{0,2},{1,3},{4,0},{5,1},{8,4},{9,5},{12,8},{13,9},{14,12},{15,13},... | collective-permute-start | bytes 786440 | tf_op jit(solution)/shard_map/ppermute | solution.py:52
  77.6 14.6 %collective-permute-start.36 = (bf16[64,2048]{1,0:T(8,128)(2,1)S(1)}, bf16[64,2048]{1,0:T(8,128)(2,1)S(1)}, u32[]{:S(2)}, u32[]{:S(2)}) collective-permute-start(bf16[64,2048]{1,0:T(8,128)(2,1)S(1)} %get-tuple-element.176), channel_id=1, source_target_pairs={{0,4},{1,5},{4,8},{5,9},{8,12},{9,13},{12,14},{13,15},{14,10},{15,... | collective-permute-start | bytes 786440 | tf_op jit(solution)/shard_map/ppermute | solution.py:52
  84.5 11.2 %collective-permute-start.27 = (bf16[64,2048]{1,0:T(8,128)(2,1)S(1)}, bf16[64,2048]{1,0:T(8,128)(2,1)S(1)}, u32[]{:S(2)}, u32[]{:S(2)}) collective-permute-start(bf16[64,2048]{1,0:T(8,128)(2,1)S(1)} %add_convert_fusion.12), channel_id=1, source_target_pairs={{0,4},{1,5},{4,8},{5,9},{8,12},{9,13},{12,14},{13,15},{14,10},{15,... | collective-permute-start | bytes 786440 | tf_op jit(solution)/shard_map/ppermute | solution.py:52
  86.3 11.2 %collective-permute-start.30 = (bf16[64,2048]{1,0:T(8,128)(2,1)S(1)}, bf16[64,2048]{1,0:T(8,128)(2,1)S(1)}, u32[]{:S(2)}, u32[]{:S(2)}) collective-permute-start(bf16[64,2048]{1,0:T(8,128)(2,1)S(1)} %add_convert_fusion.10), channel_id=1, source_target_pairs={{0,2},{1,3},{4,0},{5,1},{8,4},{9,5},{12,8},{13,9},{14,12},{15,13},... | collective-permute-start | bytes 786440 | tf_op jit(solution)/shard_map/ppermute | solution.py:52
  91.8 11.2 %collective-permute-start.34 = (bf16[64,2048]{1,0:T(8,128)(2,1)S(1)}, bf16[64,2048]{1,0:T(8,128)(2,1)S(1)}, u32[]{:S(2)}, u32[]{:S(2)}) collective-permute-start(bf16[64,2048]{1,0:T(8,128)(2,1)S(1)} %add_convert_fusion.6), channel_id=1, source_target_pairs={{0,2},{1,3},{4,0},{5,1},{8,4},{9,5},{12,8},{13,9},{14,12},{15,13},... | collective-permute-start | bytes 786440 | tf_op jit(solution)/shard_map/ppermute | solution.py:52
  92.2 11.2 %collective-permute-start.37 = (bf16[64,2048]{1,0:T(8,128)(2,1)S(1)}, bf16[64,2048]{1,0:T(8,128)(2,1)S(1)}, u32[]{:S(2)}, u32[]{:S(2)}) collective-permute-start(bf16[64,2048]{1,0:T(8,128)(2,1)S(1)} %add_convert_fusion.4), channel_id=1, source_target_pairs={{0,4},{1,5},{4,8},{5,9},{8,12},{9,13},{12,14},{13,15},{14,10},{15,... | collective-permute-start | bytes 786440 | tf_op jit(solution)/shard_map/ppermute | solution.py:52
  95.7 16.6 %collective-permute-start.28 = (bf16[64,2048]{1,0:T(8,128)(2,1)S(1)}, bf16[64,2048]{1,0:T(8,128)(2,1)S(1)}, u32[]{:S(2)}, u32[]{:S(2)}) collective-permute-start(bf16[64,2048]{1,0:T(8,128)(2,1)S(1)} %add_convert_fusion.11), channel_id=1, source_target_pairs={{0,4},{1,5},{4,8},{5,9},{8,12},{9,13},{12,14},{13,15},{14,10},{15,... | collective-permute-start | bytes 786440 | tf_op jit(solution)/shard_map/ppermute | solution.py:52
  97.6 11.0 %collective-permute-start.31 = (bf16[64,2048]{1,0:T(8,128)(2,1)S(1)}, bf16[64,2048]{1,0:T(8,128)(2,1)S(1)}, u32[]{:S(2)}, u32[]{:S(2)}) collective-permute-start(bf16[64,2048]{1,0:T(8,128)(2,1)S(1)} %add_convert_fusion.9), channel_id=1, source_target_pairs={{0,2},{1,3},{4,0},{5,1},{8,4},{9,5},{12,8},{13,9},{14,12},{15,13},... | collective-permute-start | bytes 786440 | tf_op jit(solution)/shard_map/ppermute | solution.py:52
  103.1 14.6 %collective-permute-start.35 = (bf16[64,2048]{1,0:T(8,128)(2,1)S(1)}, bf16[64,2048]{1,0:T(8,128)(2,1)S(1)}, u32[]{:S(2)}, u32[]{:S(2)}) collective-permute-start(bf16[64,2048]{1,0:T(8,128)(2,1)S(1)} %add_convert_fusion.5), channel_id=1, source_target_pairs={{0,2},{1,3},{4,0},{5,1},{8,4},{9,5},{12,8},{13,9},{14,12},{15,13},... | collective-permute-start | bytes 786440 | tf_op jit(solution)/shard_map/ppermute | solution.py:52
  103.5 6.4 %collective-permute-start.38 = (bf16[64,2048]{1,0:T(8,128)(2,1)S(1)}, bf16[64,2048]{1,0:T(8,128)(2,1)S(1)}, u32[]{:S(2)}, u32[]{:S(2)}) collective-permute-start(bf16[64,2048]{1,0:T(8,128)(2,1)S(1)} %add_convert_fusion.3), channel_id=1, source_target_pairs={{0,4},{1,5},{4,8},{5,9},{8,12},{9,13},{12,14},{13,15},{14,10},{15,... | collective-permute-start | bytes 786440 | tf_op jit(solution)/shard_map/ppermute | solution.py:52
  108.7 8.9 %collective-permute-start.32 = (bf16[64,2048]{1,0:T(8,128)(2,1)S(1)}, bf16[64,2048]{1,0:T(8,128)(2,1)S(1)}, u32[]{:S(2)}, u32[]{:S(2)}) collective-permute-start(bf16[64,2048]{1,0:T(8,128)(2,1)S(1)} %add_convert_fusion.8), channel_id=1, source_target_pairs={{0,2},{1,3},{4,0},{5,1},{8,4},{9,5},{12,8},{13,9},{14,12},{15,13},... | collective-permute-start | bytes 786440 | tf_op jit(solution)/shard_map/ppermute | solution.py:52
  110.0 7.7 %collective-permute-start.39 = (bf16[64,2048]{1,0:T(8,128)(2,1)S(1)}, bf16[64,2048]{1,0:T(8,128)(2,1)S(1)}, u32[]{:S(2)}, u32[]{:S(2)}) collective-permute-start(bf16[64,2048]{1,0:T(8,128)(2,1)S(1)} %add_convert_fusion.2), channel_id=1, source_target_pairs={{0,4},{1,5},{4,8},{5,9},{8,12},{9,13},{12,14},{13,15},{14,10},{15,... | collective-permute-start | bytes 786440 | tf_op jit(solution)/shard_map/ppermute | solution.py:52
  (11 other events, 78.2 us)

commit v5 on v4

--- a/solution.py
+++ b/solution.py
@@ -354,7 +354,7 @@
     return phases
 
 
-def gather_kv(ring, keys, values, weights, extras):
+def gather_kv(ring, keys, values, weights, inputs, extras):
     half = ring.half
     gate, up, down = weights
     both = join(
@@ -367,8 +367,14 @@
         for block in [b for b in held if 0 < b and b not in mates]:
             mates[block] = ring.go_mate(held[block])
         for hops, source in phase:
+            if (hops, source) == (4, 3):
+                held[2], held[3], inputs, extras = lax.optimization_barrier(
+                    (held[2], held[3], inputs, extras)
+                )
             held[hops] = ring.go_split(held[source], hops - source)
-    held[1], extras = hold(held[1], extras)
+        if phase[0][1] == 0:
+            held[1], inputs = hold(held[1], inputs)
+            inputs = load(*(in_hbm(x) for x in inputs))
     for hops in range(1, half):
         if hops not in mates:
             mates[hops] = ring.go_mate(held[hops])
@@ -378,7 +384,7 @@
     down_mate = ring.go_mate(down)
     blocks = tuple(held[hops] for hops in range(half + 1))
     blocks += tuple(mates[hops] for hops in range(1, half))
-    return blocks, (gate_mate, up_mate, down_mate), extras
+    return blocks, (gate_mate, up_mate, down_mate), inputs, extras
 
 
 def block_owners(ring):
@@ -412,11 +418,9 @@
     parts = roles.reshape(-1, tok_rows)
     my_roles = lax.dynamic_slice_in_dim(roles, my_index * tok_rows, tok_rows)
     live = (my_roles != 0).astype(jnp.float32)
-    inputs = load(
-        *(in_hbm(x) for x in (queries, pairs, parts, hidden_in, norm_gain.reshape(1, -1), out_weight))
-    )
-    blocks, mates, extras = gather_kv(ring, keys, values, own, (owners, live, inputs))
-    owners, live, inputs = extras
+    inputs = (queries, pairs, parts, hidden_in, norm_gain.reshape(1, -1), out_weight)
+    blocks, mates, inputs, extras = gather_kv(ring, keys, values, own, inputs, (owners, live))
+    owners, live = extras
     residual, chunks = attend(owners, pairs, parts, inputs, blocks)
     summed = feed_forward(ring, chunks, own, mates)
     ffn_back = jnp.concatenate(summed, axis=0).astype(jnp.bfloat16).astype(jnp.float32)

time: 119 us -> 119 us (level)
    ppermute x4, starting transfers between devices: 7.7 us -> 9.27 us  [go_split(): return lax.ppermute(block, 'ctx', pairs)]
where the time goes in v5:
time: 119 us
  waiting for transfers between devices  44.2 us (37%)
  starting transfers between devices  39.3 us (33%)
  Pallas kernels  31.7 us (27%)
  other arithmetic  2.63 us (2%)
    ppermute x28, waiting for transfers between devices, go(): return lax.ppermute(block, 'ctx', pairs)  36.9 us
    ppermute x28, starting transfers between devices, go(): return lax.ppermute(block, 'ctx', pairs)  28.8 us
    pallas_call x4, Pallas kernels, ffn(): pl.pallas_call(functools.partial(ffn_kernel, count), out_shape=tuple((jax...  19.4 us
    ppermute x4, starting transfers between devices, go_split(): return lax.ppermute(block, 'ctx', pairs)  9.27 us
    pallas_call x3, Pallas kernels, load(): pl.pallas_call(functools.partial(load_kernel, count), out_shape=tuple((pl...  8.32 us
    ppermute x4, waiting for transfers between devices, go_split(): return lax.ppermute(block, 'ctx', pairs)  3.89 us
    ppermute x8, waiting for transfers between devices, go_mate(): return lax.ppermute(block, 'ctx', self.swap)  3.34 us
    pallas_call x1, Pallas kernels, attend(): pl.pallas_call(functools.partial(attention_kernel, len(blocks), heads, he...  3.16 us
  transfers between devices with their start and end apart: 40, of which 21 were waited for; matrix products, arithmetic and copies ran while one was open for 2% of the time, Pallas kernels for 22%

profile of v5, /device:TPU:0, one launch (start us, length us, event | category | flops | bytes accessed | tf_op | source)
XLA Modules:
  0.0 118.9 jit_solution(8909632933026079588)
XLA Ops:
  3.3 2.7 %collective-permute-start.2 = (bf16[512,128]{1,0:T(8,128)(2,1)S(1)}, bf16[512,128]{1,0:T(8,128)(2,1)S(1)}, u32[]{:S(2)}, u32[]{:S(2)}) collective-permute-start(bf16[512,128]{1,0:T(8,128)(2,1)S(1)} %join.1.refs_0_), channel_id=1, source_target_pairs={{0,4},{1,3},{4,8},{5,1},{8,12},{9,5},{12,14},{13,9},{14,10},{15,13... | collective-permute-start | bytes 393224 | tf_op jit(solution)/shard_map/ppermute | solution.py:63
  6.0 3.5 %collective-permute-start.4 = (bf16[512,128]{1,0:T(8,128)(2,1)S(1)}, bf16[512,128]{1,0:T(8,128)(2,1)S(1)}, u32[]{:S(2)}, u32[]{:S(2)}) collective-permute-start(bf16[512,128]{1,0:T(8,128)(2,1)S(1)} %join.1.refs_0_), channel_id=1, source_target_pairs={{0,12},{1,11},{4,14},{5,7},{8,10},{9,3},{12,6},{13,1},{14,2},{15,5... | collective-permute-start | bytes 393224 | tf_op jit(solution)/shard_map/ppermute | solution.py:63
  12.6 2.6 %load.3 = (bf16[128,1024]{1,0:T(8,128)(2,1)S(1)}, s32[16,128]{1,0:T(8,128)S(1)}, s32[16,128]{1,0:T(8,128)S(1)}, bf16[128,2048]{1,0:T(8,128)(2,1)S(1)}, f32[1,204...) custom-call(bf16[128,1024]{1,0:T(8,128)(2,1)} %refs_0_.2, s32[16,128]{1,0:T(8,128)} %bitcast.7, s32[16,128]{1,0:T(8,128)} %bitcast.9, ...), custom_call_target="tpu_custom_call" | custom-call | tf_op jit(solution)/shard_map/load/pallas_call | solution.py:221
  15.7 1.6 %collective-permute-start.7 = (bf16[512,128]{1,0:T(8,128)(2,1)S(1)}, bf16[512,128]{1,0:T(8,128)(2,1)S(1)}, u32[]{:S(2)}, u32[]{:S(2)}) collective-permute-start(bf16[512,128]{1,0:T(8,128)(2,1)S(1)} %collective-permute-done.4.refs_3_), channel_id=1, source_target_pairs={{0,4},{1,3},{4,8},{5,1},{8,12},{9,5},{12,14},{13,9},{14,10},{15,13... | collective-permute-start | bytes 393224 | tf_op jit(solution)/shard_map/ppermute | solution.py:63
  17.3 3.4 %collective-permute-done.7.refs_4_ = bf16[512,128]{1,0:T(8,128)(2,1)S(1)} collective-permute-done((bf16[512,128]{1,0:T(8,128)(2,1)S(1)}, bf16[512,128]{1,0:T(8,128)(2,1)S(1)}, u32[]{:S(2)}, u32[]{:S(2)}) %collective-permute-start.7) | collective-permute-done | bytes 131104 | tf_op jit(solution)/shard_map/ppermute | solution.py:63
  20.8 3.2 %attention.1 = (bf16[64,2048]{1,0:T(8,128)(2,1)S(1)}, bf16[64,2048]{1,0:T(8,128)(2,1)S(1)}, bf16[128,2048]{1,0:T(8,128)(2,1)S(1)}) custom-call(s32[16]{0:T(128)S(1)} %dynamic-slice_bitcast_fusion.owner_ref, s32[16,128]{1,0:T(8,128)S(1)} %bitcast.8, s32[16,128]{1,0:T(8,128)S(1)} %bitcast.10, bf16[128,1024]{1,0:T(8,128)(2,1)S(1)} %get-tuple-element.116.query_ref, ...), custom_call_target="tpu_custom_call" | custom-call | tf_op jit(solution)/shard_map/attention/pallas_call | solution.py:192
  24.0 2.0 %collective-permute-done.11.refs_2_ = bf16[688,2048]{1,0:T(8,128)(2,1)S(1)} collective-permute-done((bf16[688,2048]{1,0:T(8,128)(2,1)S(1)}, bf16[688,2048]{1,0:T(8,128)(2,1)S(1)}, u32[]{:S(2)}, u32[]{:S(2)}) %collective-permute-start.11) | collective-permute-done | bytes 2818080 | tf_op jit(solution)/shard_map/ppermute | solution.py:55
  28.0 1.9 %collective-permute-start.14 = (bf16[64,2048]{1,0:T(8,128)(2,1)S(1)}, bf16[64,2048]{1,0:T(8,128)(2,1)S(1)}, u32[]{:S(2)}, u32[]{:S(2)}) collective-permute-start(bf16[64,2048]{1,0:T(8,128)(2,1)S(1)} %get-tuple-element.153.refs_3_), channel_id=1, source_target_pairs={{0,4},{1,5},{4,8},{5,9},{8,12},{9,13},{12,14},{13,15},{14,10},{15,... | collective-permute-start | bytes 786440 | tf_op jit(solution)/shard_map/ppermute | solution.py:52
  30.0 2.2 %load.5 = (bf16[688,2048]{1,0:T(8,128)(2,1)S(1)}, bf16[688,2048]{1,0:T(8,128)(2,1)S(1)}, bf16[688,2048]{1,0:T(8,128)(2,1)S(1)}) custom-call(bf16[688,2048]{1,0:T(8,128)(2,1)S(1)} %collective-permute-done.5.refs_0_, bf16[688,2048]{1,0:T(8,128)(2,1)} %collective-permute-done.6.refs_1_, bf16[688,2048]{1,0:T(8,128)(2,1)S(1)} %collective-permute-done.11.refs_2_), custom_call_target="tpu_custom_call" | custom-call | tf_op jit(solution)/shard_map/load/pallas_call | solution.py:221
  32.3 3.5 %load.4 = (bf16[688,2048]{1,0:T(8,128)(2,1)S(1)}, bf16[688,2048]{1,0:T(8,128)(2,1)S(1)}, bf16[688,2048]{1,0:T(8,128)(2,1)S(1)}) custom-call(bf16[688,2048]{1,0:T(8,128)(2,1)} %bitcast.12, bf16[688,2048]{1,0:T(8,128)(2,1)} %bitcast.14, bf16[688,2048]{1,0:T(8,128)(2,1)} %refs_2_), custom_call_target="tpu_custom_call" | custom-call | tf_op jit(solution)/shard_map/load/pallas_call | solution.py:221
  37.0 2.1 %collective-permute-start.16 = (bf16[64,2048]{1,0:T(8,128)(2,1)S(1)}, bf16[64,2048]{1,0:T(8,128)(2,1)S(1)}, u32[]{:S(2)}, u32[]{:S(2)}) collective-permute-start(bf16[64,2048]{1,0:T(8,128)(2,1)S(1)} %collective-permute-done.12.refs_0_), channel_id=1, source_target_pairs={{0,4},{1,5},{4,8},{5,9},{8,12},{9,13},{12,14},{13,15},{14,10},{15,... | collective-permute-start | bytes 786440 | tf_op jit(solution)/shard_map/ppermute | solution.py:52
  39.1 4.8 %feed_forward.4 = (bf16[64,2048]{1,0:T(8,128)(2,1)S(1)}, bf16[64,2048]{1,0:T(8,128)(2,1)S(1)}, bf16[64,2048]{1,0:T(8,128)(2,1)S(1)}, bf16[64,2048]{1,0:T(8,128)(2,1)S(1)}) custom-call(bf16[64,2048]{1,0:T(8,128)(2,1)S(1)} %collective-permute-done.12.refs_0_, bf16[64,2048]{1,0:T(8,128)(2,1)S(1)} %collective-permute-done.13.refs_1_, ...), custom_call_target="tpu_custom_call" | custom-call | flops 1000 | bytes 1000 | tf_op jit(solution)/shard_map/feed_forward/pallas_call | solution.py:285
  44.0 2.1 %collective-permute-start.22 = (bf16[64,2048]{1,0:T(8,128)(2,1)S(1)}, bf16[64,2048]{1,0:T(8,128)(2,1)S(1)}, u32[]{:S(2)}, u32[]{:S(2)}) collective-permute-start(bf16[64,2048]{1,0:T(8,128)(2,1)S(1)} %collective-permute-done.14.refs_2_), channel_id=1, source_target_pairs={{0,4},{1,5},{4,8},{5,9},{8,12},{9,13},{12,14},{13,15},{14,10},{15,... | collective-permute-start | bytes 786440 | tf_op jit(solution)/shard_map/ppermute | solution.py:52
  46.1 2.0 %collective-permute-start.17 = (bf16[64,2048]{1,0:T(8,128)(2,1)S(1)}, bf16[64,2048]{1,0:T(8,128)(2,1)S(1)}, u32[]{:S(2)}, u32[]{:S(2)}) collective-permute-start(bf16[64,2048]{1,0:T(8,128)(2,1)S(1)} %collective-permute-done.16.refs_0_), channel_id=1, source_target_pairs={{0,4},{1,5},{4,8},{5,9},{8,12},{9,13},{12,14},{13,15},{14,10},{15,... | collective-permute-start | bytes 786440 | tf_op jit(solution)/shard_map/ppermute | solution.py:52
  48.3 4.9 %feed_forward.6 = (bf16[64,2048]{1,0:T(8,128)(2,1)S(1)}, bf16[64,2048]{1,0:T(8,128)(2,1)S(1)}, bf16[64,2048]{1,0:T(8,128)(2,1)S(1)}, bf16[64,2048]{1,0:T(8,128)(2,1)S(1)}) custom-call(bf16[64,2048]{1,0:T(8,128)(2,1)S(1)} %collective-permute-done.16.refs_0_, bf16[64,2048]{1,0:T(8,128)(2,1)S(1)} %collective-permute-done.19.refs_1_, ...), custom_call_target="tpu_custom_call" | custom-call | flops 1000 | bytes 1000 | tf_op jit(solution)/shard_map/feed_forward/pallas_call | solution.py:285
  53.3 2.0 %collective-permute-done.23.refs_3_ = bf16[64,2048]{1,0:T(8,128)(2,1)S(1)} collective-permute-done((bf16[64,2048]{1,0:T(8,128)(2,1)S(1)}, bf16[64,2048]{1,0:T(8,128)(2,1)S(1)}, u32[]{:S(2)}, u32[]{:S(2)}) %collective-permute-start.23) | collective-permute-done | bytes 262176 | tf_op jit(solution)/shard_map/ppermute | solution.py:52
  60.9 4.8 %feed_forward.5 = (bf16[64,2048]{1,0:T(8,128)(2,1)S(1)}, bf16[64,2048]{1,0:T(8,128)(2,1)S(1)}, bf16[64,2048]{1,0:T(8,128)(2,1)S(1)}, bf16[64,2048]{1,0:T(8,128)(2,1)S(1)}) custom-call(bf16[64,2048]{1,0:T(8,128)(2,1)S(1)} %collective-permute-done.17.refs_0_, bf16[64,2048]{1,0:T(8,128)(2,1)S(1)} %collective-permute-done.20.refs_1_, ...), custom_call_target="tpu_custom_call" | custom-call | flops 1000 | bytes 1000 | tf_op jit(solution)/shard_map/feed_forward/pallas_call | solution.py:285
  66.5 1.6 %collective-permute-done.18.refs_0_ = bf16[64,2048]{1,0:T(8,128)(2,1)S(1)} collective-permute-done((bf16[64,2048]{1,0:T(8,128)(2,1)S(1)}, bf16[64,2048]{1,0:T(8,128)(2,1)S(1)}, u32[]{:S(2)}, u32[]{:S(2)}) %collective-permute-start.18) | collective-permute-done | bytes 262176 | tf_op jit(solution)/shard_map/ppermute | solution.py:52
  68.1 2.2 %collective-permute-done.21.refs_1_ = bf16[64,2048]{1,0:T(8,128)(2,1)S(1)} collective-permute-done((bf16[64,2048]{1,0:T(8,128)(2,1)S(1)}, bf16[64,2048]{1,0:T(8,128)(2,1)S(1)}, u32[]{:S(2)}, u32[]{:S(2)}) %collective-permute-start.21) | collective-permute-done | bytes 262176 | tf_op jit(solution)/shard_map/ppermute | solution.py:52
  70.3 4.9 %feed_forward.7 = (bf16[64,2048]{1,0:T(8,128)(2,1)S(1)}, bf16[64,2048]{1,0:T(8,128)(2,1)S(1)}, bf16[64,2048]{1,0:T(8,128)(2,1)S(1)}, bf16[64,2048]{1,0:T(8,128)(2,1)S(1)}) custom-call(bf16[64,2048]{1,0:T(8,128)(2,1)S(1)} %collective-permute-done.18.refs_0_, bf16[64,2048]{1,0:T(8,128)(2,1)S(1)} %collective-permute-done.21.refs_1_, ...), custom_call_target="tpu_custom_call" | custom-call | flops 1000 | bytes 1000 | tf_op jit(solution)/shard_map/feed_forward/pallas_call | solution.py:285
  75.2 1.8 %collective-permute-start.26 = (bf16[64,2048]{1,0:T(8,128)(2,1)S(1)}, bf16[64,2048]{1,0:T(8,128)(2,1)S(1)}, u32[]{:S(2)}, u32[]{:S(2)}) collective-permute-start(bf16[64,2048]{1,0:T(8,128)(2,1)S(1)} %get-tuple-element.181), channel_id=1, source_target_pairs={{0,4},{1,5},{4,8},{5,9},{8,12},{9,13},{12,14},{13,15},{14,10},{15,... | collective-permute-start | bytes 786440 | tf_op jit(solution)/shard_map/ppermute | solution.py:52
  77.3 2.0 %collective-permute-start.36 = (bf16[64,2048]{1,0:T(8,128)(2,1)S(1)}, bf16[64,2048]{1,0:T(8,128)(2,1)S(1)}, u32[]{:S(2)}, u32[]{:S(2)}) collective-permute-start(bf16[64,2048]{1,0:T(8,128)(2,1)S(1)} %get-tuple-element.192), channel_id=1, source_target_pairs={{0,4},{1,5},{4,8},{5,9},{8,12},{9,13},{12,14},{13,15},{14,10},{15,... | collective-permute-start | bytes 786440 | tf_op jit(solution)/shard_map/ppermute | solution.py:52
  79.3 5.2 %collective-permute-done.26 = bf16[64,2048]{1,0:T(8,128)(2,1)S(1)} collective-permute-done((bf16[64,2048]{1,0:T(8,128)(2,1)S(1)}, bf16[64,2048]{1,0:T(8,128)(2,1)S(1)}, u32[]{:S(2)}, u32[]{:S(2)}) %collective-permute-start.26) | collective-permute-done | bytes 262176 | tf_op jit(solution)/shard_map/ppermute | solution.py:52
  84.6 1.8 %collective-permute-start.27 = (bf16[64,2048]{1,0:T(8,128)(2,1)S(1)}, bf16[64,2048]{1,0:T(8,128)(2,1)S(1)}, u32[]{:S(2)}, u32[]{:S(2)}) collective-permute-start(bf16[64,2048]{1,0:T(8,128)(2,1)S(1)} %add_convert_fusion.12), channel_id=1, source_target_pairs={{0,4},{1,5},{4,8},{5,9},{8,12},{9,13},{12,14},{13,15},{14,10},{15,... | collective-permute-start | bytes 786440 | tf_op jit(solution)/shard_map/ppermute | solution.py:52
  86.8 5.1 %collective-permute-done.33 = bf16[64,2048]{1,0:T(8,128)(2,1)S(1)} collective-permute-done((bf16[64,2048]{1,0:T(8,128)(2,1)S(1)}, bf16[64,2048]{1,0:T(8,128)(2,1)S(1)}, u32[]{:S(2)}, u32[]{:S(2)}) %collective-permute-start.33) | collective-permute-done | bytes 262176 | tf_op jit(solution)/shard_map/ppermute | solution.py:52
  92.3 1.8 %collective-permute-start.37 = (bf16[64,2048]{1,0:T(8,128)(2,1)S(1)}, bf16[64,2048]{1,0:T(8,128)(2,1)S(1)}, u32[]{:S(2)}, u32[]{:S(2)}) collective-permute-start(bf16[64,2048]{1,0:T(8,128)(2,1)S(1)} %add_convert_fusion.4), channel_id=1, source_target_pairs={{0,4},{1,5},{4,8},{5,9},{8,12},{9,13},{12,14},{13,15},{14,10},{15,... | collective-permute-start | bytes 786440 | tf_op jit(solution)/shard_map/ppermute | solution.py:52
  95.7 1.9 %collective-permute-start.28 = (bf16[64,2048]{1,0:T(8,128)(2,1)S(1)}, bf16[64,2048]{1,0:T(8,128)(2,1)S(1)}, u32[]{:S(2)}, u32[]{:S(2)}) collective-permute-start(bf16[64,2048]{1,0:T(8,128)(2,1)S(1)} %add_convert_fusion.11), channel_id=1, source_target_pairs={{0,4},{1,5},{4,8},{5,9},{8,12},{9,13},{12,14},{13,15},{14,10},{15,... | collective-permute-start | bytes 786440 | tf_op jit(solution)/shard_map/ppermute | solution.py:52
  97.9 5.2 %collective-permute-done.34 = bf16[64,2048]{1,0:T(8,128)(2,1)S(1)} collective-permute-done((bf16[64,2048]{1,0:T(8,128)(2,1)S(1)}, bf16[64,2048]{1,0:T(8,128)(2,1)S(1)}, u32[]{:S(2)}, u32[]{:S(2)}) %collective-permute-start.34) | collective-permute-done | bytes 262176 | tf_op jit(solution)/shard_map/ppermute | solution.py:52
  103.6 1.8 %collective-permute-start.38 = (bf16[64,2048]{1,0:T(8,128)(2,1)S(1)}, bf16[64,2048]{1,0:T(8,128)(2,1)S(1)}, u32[]{:S(2)}, u32[]{:S(2)}) collective-permute-start(bf16[64,2048]{1,0:T(8,128)(2,1)S(1)} %add_convert_fusion.3), channel_id=1, source_target_pairs={{0,4},{1,5},{4,8},{5,9},{8,12},{9,13},{12,14},{13,15},{14,10},{15,... | collective-permute-start | bytes 786440 | tf_op jit(solution)/shard_map/ppermute | solution.py:52
  105.4 3.3 %collective-permute-done.31 = bf16[64,2048]{1,0:T(8,128)(2,1)S(1)} collective-permute-done((bf16[64,2048]{1,0:T(8,128)(2,1)S(1)}, bf16[64,2048]{1,0:T(8,128)(2,1)S(1)}, u32[]{:S(2)}, u32[]{:S(2)}) %collective-permute-start.31) | collective-permute-done | bytes 262176 | tf_op jit(solution)/shard_map/ppermute | solution.py:52
  110.1 2.4 %collective-permute-start.39 = (bf16[64,2048]{1,0:T(8,128)(2,1)S(1)}, bf16[64,2048]{1,0:T(8,128)(2,1)S(1)}, u32[]{:S(2)}, u32[]{:S(2)}) collective-permute-start(bf16[64,2048]{1,0:T(8,128)(2,1)S(1)} %add_convert_fusion.2), channel_id=1, source_target_pairs={{0,4},{1,5},{4,8},{5,9},{8,12},{9,13},{12,14},{13,15},{14,10},{15,... | collective-permute-start | bytes 786440 | tf_op jit(solution)/shard_map/ppermute | solution.py:52
  112.5 5.2 %collective-permute-done.32 = bf16[64,2048]{1,0:T(8,128)(2,1)S(1)} collective-permute-done((bf16[64,2048]{1,0:T(8,128)(2,1)S(1)}, bf16[64,2048]{1,0:T(8,128)(2,1)S(1)}, u32[]{:S(2)}, u32[]{:S(2)}) %collective-permute-start.32) | collective-permute-done | bytes 262176 | tf_op jit(solution)/shard_map/ppermute | solution.py:52
  (78 shorter events, 23.3 us)
Async XLA Ops:
  2.7 18.0 %collective-permute-start.5 = (bf16[688,2048]{1,0:T(8,128)(2,1)}, bf16[688,2048]{1,0:T(8,128)(2,1)S(1)}, u32[]{:S(2)}, u32[]{:S(2)}) collective-permute-start(bf16[688,2048]{1,0:T(8,128)(2,1)} %bitcast.11), channel_id=1, source_target_pairs={{0,1},{1,0},{2,3},{3,2},{4,5},{5,4},{6,7},{7,6},{8,9},{9,8},{10,11... | collective-permute-start | bytes 8454152 | tf_op jit(solution)/shard_map/ppermute | solution.py:55
  2.9 17.8 %collective-permute-start.6 = (bf16[688,2048]{1,0:T(8,128)(2,1)}, bf16[688,2048]{1,0:T(8,128)(2,1)}, u32[]{:S(2)}, u32[]{:S(2)}) collective-permute-start(bf16[688,2048]{1,0:T(8,128)(2,1)} %bitcast.13), channel_id=1, source_target_pairs={{0,1},{1,0},{2,3},{3,2},{4,5},{5,4},{6,7},{7,6},{8,9},{9,8},{10,11... | collective-permute-start | bytes 8454152 | tf_op jit(solution)/shard_map/ppermute | solution.py:55
  6.0 9.6 %collective-permute-start.4 = (bf16[512,128]{1,0:T(8,128)(2,1)S(1)}, bf16[512,128]{1,0:T(8,128)(2,1)S(1)}, u32[]{:S(2)}, u32[]{:S(2)}) collective-permute-start(bf16[512,128]{1,0:T(8,128)(2,1)S(1)} %join.1.refs_0_), channel_id=1, source_target_pairs={{0,12},{1,11},{4,14},{5,7},{8,10},{9,3},{12,6},{13,1},{14,2},{15,5... | collective-permute-start | bytes 393224 | tf_op jit(solution)/shard_map/ppermute | solution.py:63
  11.0 6.3 %collective-permute-start.8 = (bf16[512,128]{1,0:T(8,128)(2,1)S(1)}, bf16[512,128]{1,0:T(8,128)(2,1)S(1)}, u32[]{:S(2)}, u32[]{:S(2)}) collective-permute-start(bf16[512,128]{1,0:T(8,128)(2,1)S(1)} %collective-permute-done.2.refs_1_), channel_id=1, source_target_pairs={{0,1},{1,0},{2,3},{3,2},{4,5},{5,4},{6,7},{7,6},{8,9},{9,8},{10,11... | collective-permute-start | bytes 393224 | tf_op jit(solution)/shard_map/ppermute | solution.py:55
  26.0 9.8 %collective-permute-start.12 = (bf16[64,2048]{1,0:T(8,128)(2,1)S(1)}, bf16[64,2048]{1,0:T(8,128)(2,1)S(1)}, u32[]{:S(2)}, u32[]{:S(2)}) collective-permute-start(bf16[64,2048]{1,0:T(8,128)(2,1)S(1)} %get-tuple-element.152.refs_2_), channel_id=1, source_target_pairs={{0,4},{1,5},{4,8},{5,9},{8,12},{9,13},{12,14},{13,15},{14,10},{15,... | collective-permute-start | bytes 786440 | tf_op jit(solution)/shard_map/ppermute | solution.py:52
  27.6 9.5 %collective-permute-start.13 = (bf16[64,2048]{1,0:T(8,128)(2,1)S(1)}, bf16[64,2048]{1,0:T(8,128)(2,1)S(1)}, u32[]{:S(2)}, u32[]{:S(2)}) collective-permute-start(bf16[64,2048]{1,0:T(8,128)(2,1)S(1)} %get-tuple-element.153.refs_3_), channel_id=1, source_target_pairs={{0,2},{1,3},{4,0},{5,1},{8,4},{9,5},{12,8},{13,9},{14,12},{15,13},... | collective-permute-start | bytes 786440 | tf_op jit(solution)/shard_map/ppermute | solution.py:52
  28.0 15.9 %collective-permute-start.14 = (bf16[64,2048]{1,0:T(8,128)(2,1)S(1)}, bf16[64,2048]{1,0:T(8,128)(2,1)S(1)}, u32[]{:S(2)}, u32[]{:S(2)}) collective-permute-start(bf16[64,2048]{1,0:T(8,128)(2,1)S(1)} %get-tuple-element.153.refs_3_), channel_id=1, source_target_pairs={{0,4},{1,5},{4,8},{5,9},{8,12},{9,13},{12,14},{13,15},{14,10},{15,... | collective-permute-start | bytes 786440 | tf_op jit(solution)/shard_map/ppermute | solution.py:52
  30.0 14.0 %collective-permute-start.15 = (bf16[64,2048]{1,0:T(8,128)(2,1)S(1)}, bf16[64,2048]{1,0:T(8,128)(2,1)S(1)}, u32[]{:S(2)}, u32[]{:S(2)}) collective-permute-start(bf16[64,2048]{1,0:T(8,128)(2,1)S(1)} %get-tuple-element.152.refs_2_), channel_id=1, source_target_pairs={{0,2},{1,3},{4,0},{5,1},{8,4},{9,5},{12,8},{13,9},{14,12},{15,13},... | collective-permute-start | bytes 786440 | tf_op jit(solution)/shard_map/ppermute | solution.py:52
  37.0 9.0 %collective-permute-start.16 = (bf16[64,2048]{1,0:T(8,128)(2,1)S(1)}, bf16[64,2048]{1,0:T(8,128)(2,1)S(1)}, u32[]{:S(2)}, u32[]{:S(2)}) collective-permute-start(bf16[64,2048]{1,0:T(8,128)(2,1)S(1)} %collective-permute-done.12.refs_0_), channel_id=1, source_target_pairs={{0,4},{1,5},{4,8},{5,9},{8,12},{9,13},{12,14},{13,15},{14,10},{15,... | collective-permute-start | bytes 786440 | tf_op jit(solution)/shard_map/ppermute | solution.py:52
  39.1 9.2 %collective-permute-start.19 = (bf16[64,2048]{1,0:T(8,128)(2,1)S(1)}, bf16[64,2048]{1,0:T(8,128)(2,1)S(1)}, u32[]{:S(2)}, u32[]{:S(2)}) collective-permute-start(bf16[64,2048]{1,0:T(8,128)(2,1)S(1)} %collective-permute-done.13.refs_1_), channel_id=1, source_target_pairs={{0,2},{1,3},{4,0},{5,1},{8,4},{9,5},{12,8},{13,9},{14,12},{15,13},... | collective-permute-start | bytes 786440 | tf_op jit(solution)/shard_map/ppermute | solution.py:52
  44.0 9.3 %collective-permute-start.22 = (bf16[64,2048]{1,0:T(8,128)(2,1)S(1)}, bf16[64,2048]{1,0:T(8,128)(2,1)S(1)}, u32[]{:S(2)}, u32[]{:S(2)}) collective-permute-start(bf16[64,2048]{1,0:T(8,128)(2,1)S(1)} %collective-permute-done.14.refs_2_), channel_id=1, source_target_pairs={{0,4},{1,5},{4,8},{5,9},{8,12},{9,13},{12,14},{13,15},{14,10},{15,... | collective-permute-start | bytes 786440 | tf_op jit(solution)/shard_map/ppermute | solution.py:52
  46.0 9.2 %collective-permute-start.23 = (bf16[64,2048]{1,0:T(8,128)(2,1)S(1)}, bf16[64,2048]{1,0:T(8,128)(2,1)S(1)}, u32[]{:S(2)}, u32[]{:S(2)}) collective-permute-start(bf16[64,2048]{1,0:T(8,128)(2,1)S(1)} %collective-permute-done.15.refs_3_), channel_id=1, source_target_pairs={{0,2},{1,3},{4,0},{5,1},{8,4},{9,5},{12,8},{13,9},{14,12},{15,13},... | collective-permute-start | bytes 786440 | tf_op jit(solution)/shard_map/ppermute | solution.py:52
  46.1 12.6 %collective-permute-start.17 = (bf16[64,2048]{1,0:T(8,128)(2,1)S(1)}, bf16[64,2048]{1,0:T(8,128)(2,1)S(1)}, u32[]{:S(2)}, u32[]{:S(2)}) collective-permute-start(bf16[64,2048]{1,0:T(8,128)(2,1)S(1)} %collective-permute-done.16.refs_0_), channel_id=1, source_target_pairs={{0,4},{1,5},{4,8},{5,9},{8,12},{9,13},{12,14},{13,15},{14,10},{15,... | collective-permute-start | bytes 786440 | tf_op jit(solution)/shard_map/ppermute | solution.py:52
  48.3 12.6 %collective-permute-start.20 = (bf16[64,2048]{1,0:T(8,128)(2,1)S(1)}, bf16[64,2048]{1,0:T(8,128)(2,1)S(1)}, u32[]{:S(2)}, u32[]{:S(2)}) collective-permute-start(bf16[64,2048]{1,0:T(8,128)(2,1)S(1)} %collective-permute-done.19.refs_1_), channel_id=1, source_target_pairs={{0,2},{1,3},{4,0},{5,1},{8,4},{9,5},{12,8},{13,9},{14,12},{15,13},... | collective-permute-start | bytes 786440 | tf_op jit(solution)/shard_map/ppermute | solution.py:52
  55.3 10.5 %collective-permute-start.24 = (bf16[64,2048]{1,0:T(8,128)(2,1)S(1)}, bf16[64,2048]{1,0:T(8,128)(2,1)S(1)}, u32[]{:S(2)}, u32[]{:S(2)}) collective-permute-start(bf16[64,2048]{1,0:T(8,128)(2,1)S(1)} %collective-permute-done.22.refs_2_), channel_id=1, source_target_pairs={{0,4},{1,5},{4,8},{5,9},{8,12},{9,13},{12,14},{13,15},{14,10},{15,... | collective-permute-start | bytes 786440 | tf_op jit(solution)/shard_map/ppermute | solution.py:52
  56.3 10.2 %collective-permute-start.25 = (bf16[64,2048]{1,0:T(8,128)(2,1)S(1)}, bf16[64,2048]{1,0:T(8,128)(2,1)S(1)}, u32[]{:S(2)}, u32[]{:S(2)}) collective-permute-start(bf16[64,2048]{1,0:T(8,128)(2,1)S(1)} %collective-permute-done.23.refs_3_), channel_id=1, source_target_pairs={{0,2},{1,3},{4,0},{5,1},{8,4},{9,5},{12,8},{13,9},{14,12},{15,13},... | collective-permute-start | bytes 786440 | tf_op jit(solution)/shard_map/ppermute | solution.py:52
  58.6 9.5 %collective-permute-start.18 = (bf16[64,2048]{1,0:T(8,128)(2,1)S(1)}, bf16[64,2048]{1,0:T(8,128)(2,1)S(1)}, u32[]{:S(2)}, u32[]{:S(2)}) collective-permute-start(bf16[64,2048]{1,0:T(8,128)(2,1)S(1)} %collective-permute-done.17.refs_0_), channel_id=1, source_target_pairs={{0,4},{1,5},{4,8},{5,9},{8,12},{9,13},{12,14},{13,15},{14,10},{15,... | collective-permute-start | bytes 786440 | tf_op jit(solution)/shard_map/ppermute | solution.py:52
  60.9 9.4 %collective-permute-start.21 = (bf16[64,2048]{1,0:T(8,128)(2,1)S(1)}, bf16[64,2048]{1,0:T(8,128)(2,1)S(1)}, u32[]{:S(2)}, u32[]{:S(2)}) collective-permute-start(bf16[64,2048]{1,0:T(8,128)(2,1)S(1)} %collective-permute-done.20.refs_1_), channel_id=1, source_target_pairs={{0,2},{1,3},{4,0},{5,1},{8,4},{9,5},{12,8},{13,9},{14,12},{15,13},... | collective-permute-start | bytes 786440 | tf_op jit(solution)/shard_map/ppermute | solution.py:52
  75.2 9.3 %collective-permute-start.26 = (bf16[64,2048]{1,0:T(8,128)(2,1)S(1)}, bf16[64,2048]{1,0:T(8,128)(2,1)S(1)}, u32[]{:S(2)}, u32[]{:S(2)}) collective-permute-start(bf16[64,2048]{1,0:T(8,128)(2,1)S(1)} %get-tuple-element.181), channel_id=1, source_target_pairs={{0,4},{1,5},{4,8},{5,9},{8,12},{9,13},{12,14},{13,15},{14,10},{15,... | collective-permute-start | bytes 786440 | tf_op jit(solution)/shard_map/ppermute | solution.py:52
  77.0 9.4 %collective-permute-start.29 = (bf16[64,2048]{1,0:T(8,128)(2,1)S(1)}, bf16[64,2048]{1,0:T(8,128)(2,1)S(1)}, u32[]{:S(2)}, u32[]{:S(2)}) collective-permute-start(bf16[64,2048]{1,0:T(8,128)(2,1)S(1)} %get-tuple-element.184), channel_id=1, source_target_pairs={{0,2},{1,3},{4,0},{5,1},{8,4},{9,5},{12,8},{13,9},{14,12},{15,13},... | collective-permute-start | bytes 786440 | tf_op jit(solution)/shard_map/ppermute | solution.py:52
  77.3 14.6 %collective-permute-start.33 = (bf16[64,2048]{1,0:T(8,128)(2,1)S(1)}, bf16[64,2048]{1,0:T(8,128)(2,1)S(1)}, u32[]{:S(2)}, u32[]{:S(2)}) collective-permute-start(bf16[64,2048]{1,0:T(8,128)(2,1)S(1)} %get-tuple-element.189), channel_id=1, source_target_pairs={{0,2},{1,3},{4,0},{5,1},{8,4},{9,5},{12,8},{13,9},{14,12},{15,13},... | collective-permute-start | bytes 786440 | tf_op jit(solution)/shard_map/ppermute | solution.py:52
  77.3 15.0 %collective-permute-start.36 = (bf16[64,2048]{1,0:T(8,128)(2,1)S(1)}, bf16[64,2048]{1,0:T(8,128)(2,1)S(1)}, u32[]{:S(2)}, u32[]{:S(2)}) collective-permute-start(bf16[64,2048]{1,0:T(8,128)(2,1)S(1)} %get-tuple-element.192), channel_id=1, source_target_pairs={{0,4},{1,5},{4,8},{5,9},{8,12},{9,13},{12,14},{13,15},{14,10},{15,... | collective-permute-start | bytes 786440 | tf_op jit(solution)/shard_map/ppermute | solution.py:52
  84.6 11.1 %collective-permute-start.27 = (bf16[64,2048]{1,0:T(8,128)(2,1)S(1)}, bf16[64,2048]{1,0:T(8,128)(2,1)S(1)}, u32[]{:S(2)}, u32[]{:S(2)}) collective-permute-start(bf16[64,2048]{1,0:T(8,128)(2,1)S(1)} %add_convert_fusion.12), channel_id=1, source_target_pairs={{0,4},{1,5},{4,8},{5,9},{8,12},{9,13},{12,14},{13,15},{14,10},{15,... | collective-permute-start | bytes 786440 | tf_op jit(solution)/shard_map/ppermute | solution.py:52
  86.4 11.2 %collective-permute-start.30 = (bf16[64,2048]{1,0:T(8,128)(2,1)S(1)}, bf16[64,2048]{1,0:T(8,128)(2,1)S(1)}, u32[]{:S(2)}, u32[]{:S(2)}) collective-permute-start(bf16[64,2048]{1,0:T(8,128)(2,1)S(1)} %add_convert_fusion.10), channel_id=1, source_target_pairs={{0,2},{1,3},{4,0},{5,1},{8,4},{9,5},{12,8},{13,9},{14,12},{15,13},... | collective-permute-start | bytes 786440 | tf_op jit(solution)/shard_map/ppermute | solution.py:52
  91.9 11.2 %collective-permute-start.34 = (bf16[64,2048]{1,0:T(8,128)(2,1)S(1)}, bf16[64,2048]{1,0:T(8,128)(2,1)S(1)}, u32[]{:S(2)}, u32[]{:S(2)}) collective-permute-start(bf16[64,2048]{1,0:T(8,128)(2,1)S(1)} %add_convert_fusion.6), channel_id=1, source_target_pairs={{0,2},{1,3},{4,0},{5,1},{8,4},{9,5},{12,8},{13,9},{14,12},{15,13},... | collective-permute-start | bytes 786440 | tf_op jit(solution)/shard_map/ppermute | solution.py:52
  92.3 11.2 %collective-permute-start.37 = (bf16[64,2048]{1,0:T(8,128)(2,1)S(1)}, bf16[64,2048]{1,0:T(8,128)(2,1)S(1)}, u32[]{:S(2)}, u32[]{:S(2)}) collective-permute-start(bf16[64,2048]{1,0:T(8,128)(2,1)S(1)} %add_convert_fusion.4), channel_id=1, source_target_pairs={{0,4},{1,5},{4,8},{5,9},{8,12},{9,13},{12,14},{13,15},{14,10},{15,... | collective-permute-start | bytes 786440 | tf_op jit(solution)/shard_map/ppermute | solution.py:52
  95.7 16.7 %collective-permute-start.28 = (bf16[64,2048]{1,0:T(8,128)(2,1)S(1)}, bf16[64,2048]{1,0:T(8,128)(2,1)S(1)}, u32[]{:S(2)}, u32[]{:S(2)}) collective-permute-start(bf16[64,2048]{1,0:T(8,128)(2,1)S(1)} %add_convert_fusion.11), channel_id=1, source_target_pairs={{0,4},{1,5},{4,8},{5,9},{8,12},{9,13},{12,14},{13,15},{14,10},{15,... | collective-permute-start | bytes 786440 | tf_op jit(solution)/shard_map/ppermute | solution.py:52
  97.7 11.0 %collective-permute-start.31 = (bf16[64,2048]{1,0:T(8,128)(2,1)S(1)}, bf16[64,2048]{1,0:T(8,128)(2,1)S(1)}, u32[]{:S(2)}, u32[]{:S(2)}) collective-permute-start(bf16[64,2048]{1,0:T(8,128)(2,1)S(1)} %add_convert_fusion.9), channel_id=1, source_target_pairs={{0,2},{1,3},{4,0},{5,1},{8,4},{9,5},{12,8},{13,9},{14,12},{15,13},... | collective-permute-start | bytes 786440 | tf_op jit(solution)/shard_map/ppermute | solution.py:52
  103.1 14.6 %collective-permute-start.35 = (bf16[64,2048]{1,0:T(8,128)(2,1)S(1)}, bf16[64,2048]{1,0:T(8,128)(2,1)S(1)}, u32[]{:S(2)}, u32[]{:S(2)}) collective-permute-start(bf16[64,2048]{1,0:T(8,128)(2,1)S(1)} %add_convert_fusion.5), channel_id=1, source_target_pairs={{0,2},{1,3},{4,0},{5,1},{8,4},{9,5},{12,8},{13,9},{14,12},{15,13},... | collective-permute-start | bytes 786440 | tf_op jit(solution)/shard_map/ppermute | solution.py:52
  103.6 6.4 %collective-permute-start.38 = (bf16[64,2048]{1,0:T(8,128)(2,1)S(1)}, bf16[64,2048]{1,0:T(8,128)(2,1)S(1)}, u32[]{:S(2)}, u32[]{:S(2)}) collective-permute-start(bf16[64,2048]{1,0:T(8,128)(2,1)S(1)} %add_convert_fusion.3), channel_id=1, source_target_pairs={{0,4},{1,5},{4,8},{5,9},{8,12},{9,13},{12,14},{13,15},{14,10},{15,... | collective-permute-start | bytes 786440 | tf_op jit(solution)/shard_map/ppermute | solution.py:52
  108.8 8.9 %collective-permute-start.32 = (bf16[64,2048]{1,0:T(8,128)(2,1)S(1)}, bf16[64,2048]{1,0:T(8,128)(2,1)S(1)}, u32[]{:S(2)}, u32[]{:S(2)}) collective-permute-start(bf16[64,2048]{1,0:T(8,128)(2,1)S(1)} %add_convert_fusion.8), channel_id=1, source_target_pairs={{0,2},{1,3},{4,0},{5,1},{8,4},{9,5},{12,8},{13,9},{14,12},{15,13},... | collective-permute-start | bytes 786440 | tf_op jit(solution)/shard_map/ppermute | solution.py:52
  110.1 7.7 %collective-permute-start.39 = (bf16[64,2048]{1,0:T(8,128)(2,1)S(1)}, bf16[64,2048]{1,0:T(8,128)(2,1)S(1)}, u32[]{:S(2)}, u32[]{:S(2)}) collective-permute-start(bf16[64,2048]{1,0:T(8,128)(2,1)S(1)} %add_convert_fusion.2), channel_id=1, source_target_pairs={{0,4},{1,5},{4,8},{5,9},{8,12},{9,13},{12,14},{13,15},{14,10},{15,... | collective-permute-start | bytes 786440 | tf_op jit(solution)/shard_map/ppermute | solution.py:52
  (11 other events, 81.3 us)
